TPU v7x, 32 devices: a whole 2x2x4 slice. The times are simulated.
32 devices in a mesh: dp: 8 (over y, x, core), ctx: 4 (over z).
Axes of the slice: x: 2, y: 2, z: 4, core: 2. Of those that a mesh axis runs over, the one named last changes fastest.
Arguments:
- query: bfloat16 [8, 512, 2560], P('dp', 'ctx'), may hold values from -213 to 213
- key_in: bfloat16 [8, 512, 2560], P('dp', 'ctx'), may hold values from -2 to 2
- value: bfloat16 [8, 512, 2560], P('dp', 'ctx'), may hold values from -6 to 6
- gate_table: float32 [1000, 5120], P(None, 'ctx'), may hold values from 1 to 4
- timestep: int32 [8], P('dp'), may hold values from 0 to 999
- out_weight: bfloat16 [2560, 5120], P('dp', 'ctx'), may hold values from -0.125 to 0.125
- grad_out: bfloat16 [8, 512, 5120], P('dp', None, 'ctx'), may hold values from -0.59765625 to 0.59765625
Outputs:
- branch_out: bfloat16 [8, 512, 5120], P('dp', None, 'ctx')
- grad_query: bfloat16 [8, 512, 2560], P('dp', 'ctx')
- grad_key: bfloat16 [8, 512, 2560], P('dp', 'ctx')
- grad_value: bfloat16 [8, 512, 2560], P('dp', 'ctx')
- grad_weight: float32 [2560, 5120], P('dp', 'ctx')
All inputs are finite; a program needn't handle non-finite values.
Results may differ from a plain program's by a relative error of at most 0.035.
Values may be sent and summed in bfloat16 or wider, within the bound.
No kernel may reach another device: no remote copies, remote signals or barrier semaphores. Data moves between devices by JAX's collectives and lax.ppermute only.
A program may use at most 128 MiB of HBM per device.

v0:
```python
import jax
import jax.numpy as jnp
from jax import lax
from jax.sharding import PartitionSpec as P

HEAD_DIM = 128


def on_device(query, key_in, value, gate_table, timestep, out_weight, grad_out):
    slab_rows = query.shape[1]
    attn_width = query.shape[2]
    head_count = attn_width // HEAD_DIM
    score_scale = HEAD_DIM ** (-0.5)
    query_heads = query[0].reshape(slab_rows, head_count, HEAD_DIM)
    keys_whole, values_whole = (
        lax.all_gather(key_in, "ctx", axis=1, tiled=True),
        lax.all_gather(value, "ctx", axis=1, tiled=True),
    )
    keys_all = keys_whole[0]
    values_all = values_whole[0]
    scores = (
        jnp.einsum(
            "qhd,khd->hqk",
            query_heads,
            keys_all.reshape(keys_all.shape[0], head_count, HEAD_DIM),
            preferred_element_type=jnp.float32,
        )
        * score_scale
    )
    length = keys_all.shape[0]
    key_heads = keys_all.reshape(length, head_count, HEAD_DIM)
    value_heads = values_all.reshape(length, head_count, HEAD_DIM)
    row_max = jnp.max(scores, axis=2, keepdims=True)
    exp_scores = jnp.exp(scores - row_max)
    probability = exp_scores / jnp.sum(exp_scores, axis=2, keepdims=True)
    prob_half = probability.astype(jnp.bfloat16)
    attention = jnp.einsum(
        "hqk,khd->qhd", prob_half, value_heads, preferred_element_type=jnp.float32
    )
    attention = attention.reshape(slab_rows, attn_width).astype(jnp.bfloat16)
    marker = (
        timestep[:, None] == jnp.arange(gate_table.shape[0], dtype=jnp.int32)[None, :]
    ).astype(jnp.float32)
    gate_row = jnp.dot(marker, gate_table, precision=lax.Precision.HIGHEST)
    attn_rows = lax.all_gather(attention, "ctx", axis=0, tiled=True)
    columns = attn_rows
    projected = jnp.dot(
        columns,
        lax.all_gather(out_weight, "dp", axis=0, tiled=True),
        preferred_element_type=jnp.float32,
    )
    branch_out = (projected * gate_row).astype(jnp.bfloat16)[None]
    d_proj = (grad_out[0].astype(jnp.float32) * gate_row).astype(jnp.bfloat16)
    partial_rows = jnp.einsum(
        "td,rd->tr",
        d_proj,
        lax.all_gather(out_weight, "dp", axis=0, tiled=True),
        preferred_element_type=jnp.float32,
    )
    d_attn = lax.psum_scatter(
        partial_rows.astype(jnp.bfloat16), "ctx", scatter_dimension=0, tiled=True
    ).astype(jnp.float32)
    d_attn = d_attn.astype(jnp.bfloat16)
    columns = attn_rows
    grad_weight = lax.psum_scatter(
        jnp.einsum("tr,td->rd", columns, d_proj, preferred_element_type=jnp.float32).astype(
            jnp.bfloat16
        ),
        "dp",
        scatter_dimension=0,
        tiled=True,
    ).astype(jnp.float32)
    d_heads = d_attn.reshape(slab_rows, head_count, HEAD_DIM)
    out_heads = attention.reshape(slab_rows, head_count, HEAD_DIM)
    row_delta = jnp.einsum("qhd,qhd->hq", d_heads, out_heads, preferred_element_type=jnp.float32)
    d_scores = jnp.einsum("qhd,khd->hqk", d_heads, value_heads, preferred_element_type=jnp.float32)
    d_half = (probability * (d_scores - row_delta[:, :, None]) * score_scale).astype(jnp.bfloat16)
    grad_query = jnp.einsum("hqk,khd->qhd", d_half, key_heads, preferred_element_type=jnp.float32)
    grad_query = grad_query.reshape(slab_rows, attn_width).astype(jnp.bfloat16)
    key_part = jnp.einsum(
        "hqk,qhd->khd", d_half, query_heads, preferred_element_type=jnp.float32
    ).reshape(slab_rows * lax.axis_size("ctx"), attn_width)
    value_part = jnp.einsum(
        "hqk,qhd->khd", prob_half, d_heads, preferred_element_type=jnp.float32
    ).reshape(slab_rows * lax.axis_size("ctx"), attn_width)
    key_sums = lax.psum_scatter(
        jnp.concatenate([key_part, value_part], axis=1).astype(jnp.bfloat16),
        "ctx",
        scatter_dimension=0,
        tiled=True,
    ).astype(jnp.float32)
    grad_key = key_sums[:, :attn_width].astype(jnp.bfloat16)
    grad_value = key_sums[:, attn_width:].astype(jnp.bfloat16)
    return (branch_out, grad_query[None], grad_key[None], grad_value[None], grad_weight)


def solution(mesh):
    in_specs = (
        P("dp", "ctx", None),
        P("dp", "ctx", None),
        P("dp", "ctx", None),
        P(None, "ctx"),
        P("dp"),
        P("dp", "ctx"),
        P("dp", None, "ctx"),
    )
    out_specs = (
        P("dp", None, "ctx"),
        P("dp", "ctx", None),
        P("dp", "ctx", None),
        P("dp", "ctx", None),
        P("dp", "ctx"),
    )
    return jax.shard_map(
        on_device, mesh=mesh, in_specs=in_specs, out_specs=out_specs, check_vma=False
    )
```

profile of v0, /device:TPU:0, one launch (start us, length us, event | category | flops | bytes accessed | tf_op | source)
XLA Modules:
  0.0 454.8 jit_solution(4660328474102483353)
XLA Ops:
  11.7 4.2 convolution_reduce_fusion
  15.9 43.3 %all-gather.11.cloned.1.call-done = bf16[2560,1280]{1,0:T(8,128)(2,1)} async-done(((bf16[320,1280]{1,0:T(8,128)(2,1)}), bf16[2560,1280]{1,0:T(8,128)(2,1)}) %all-gather.11.cloned.1.call-update) | async-done | bytes 6553616 | tf_op jit(solution)/shard_map/all_gather | solution.py:49
  59.3 7.8 %convolution_convert_fusion.1 = bf16[512,2560]{1,0:T(8,128)(2,1)} fusion(bf16[2560,1280]{1,0:T(8,128)(2,1)} %all-gather.11.cloned.1.call-done, bf16[1,512,1280]{2,1,0:T(8,128)(2,1)S(1)} %copy-done.3, f32[1280]{0:T(1024)S(1)} %convolution_reduce_fusion), kind=kOutput, calls=%fused_computation.7 | convolution fusion | flops 3358720000 | bytes 10490880 | tf_op jit(solution)/shard_map/td,rd->tr/dot_general | solution.py:54
  68.5 47.2 %all-gather.7.cloned.1.call-done = bf16[1,512,2560]{2,1,0:T(8,128)(2,1)} async-done(((bf16[1,128,2560]{2,1,0:T(8,128)(2,1)}), bf16[1,512,2560]{2,1,0:T(8,128)(2,1)}) %all-gather.7.cloned.1.call-update) | async-done | bytes 2621456 | tf_op jit(solution)/shard_map/all_gather | solution.py:17
  115.7 4.4 copy.26
  120.1 51.4 %all-gather.5.cloned.1.call-done = bf16[1,512,2560]{1,2,0:T(8,128)(2,1)} async-done(((bf16[1,128,2560]{1,2,0:T(8,128)(2,1)}), bf16[1,512,2560]{1,2,0:T(8,128)(2,1)}) %all-gather.5.cloned.1.call-update) | async-done | bytes 2621456 | tf_op jit(solution)/shard_map/all_gather | solution.py:16
  171.5 5.9 %fusion.15 = (f32[20,128]{1,0:T(8,128)S(1)}, f32[20,128,512]{2,1,0:T(8,128)}) fusion(bf16[128,20,128]{0,2,1:T(8,128)(2,1)S(1)} %bitcast.61, bf16[512,20,128]{0,2,1:T(8,128)(2,1)} %bitcast.55), kind=kOutput, calls=%fused_computation.28 | convolution fusion | flops 339476992 | bytes 8529920 | tf_op jit(solution)/shard_map/sub | solution.py:34
  177.4 3.2 fusion.8
  180.6 43.4 %reduce-scatter.4.cloned.1.call-done = bf16[128,2560]{1,0:T(8,128)(2,1)} async-done(((bf16[512,2560]{1,0:T(8,128)(2,1)}), bf16[128,2560]{1,0:T(8,128)(2,1)}) %reduce-scatter.4.cloned.1.call-update) | async-done | bytes 655376 | tf_op jit(solution)/shard_map/reduce_scatter | solution.py:60
  226.1 3.6 fusion.9
  229.7 3.4 convolution_convert_fusion.3
  233.1 3.0 copy.31
  236.1 5.1 %multiply_convert_fusion = bf16[20,128,512]{2,1,0:T(8,128)(2,1)S(1)} fusion(f32[20,128]{1,0:T(8,128)S(1)} %get-tuple-element.19, bf16[128,20,128]{0,2,1:T(8,128)(2,1)} %bitcast.65, bf16[512,20,128]{0,2,1:T(8,128)(2,1)} %bitcast.58, f32[20,128,512]{2,1,0:T(8,128)} %get-tuple-element.18, f32[20,128]{1,0:T(8,128)S(1)} %get-tuple-element.17), kind=kOutput, calls=%fused_computation.3 | convolution fusion | flops 342097920 | bytes 11161600 | tf_op jit(solution)/shard_map/qhd,khd->hqk/dot_general | solution.py:76
  241.3 2.4 convolution_convert_fusion.2
  243.7 4.5 copy.30
  248.1 4.8 %pad_maximum_fusion = bf16[512,5120]{1,0:T(8,128)(2,1)} fusion(bf16[512,2560]{1,0:T(8,128)(2,1)S(1)} %copy.31, bf16[512,2560]{1,0:T(8,128)(2,1)} %copy.30), kind=kLoop, calls=%fused_computation.2 | loop fusion | flops 10485760 | bytes 10485760 | tf_op jit(solution)/shard_map/concatenate | solution.py:87
  253.2 31.2 %all-gather.9.cloned.1.call-done = bf16[512,2560]{0,1:T(8,128)(2,1)} async-done(((bf16[128,2560]{0,1:T(8,128)(2,1)}), bf16[512,2560]{0,1:T(8,128)(2,1)}) %all-gather.9.cloned.1.call-update) | async-done | bytes 2621456 | tf_op jit(solution)/shard_map/all_gather | solution.py:45
  284.4 8.0 %convolution_convert_fusion = bf16[2560,1280]{1,0:T(8,128)(2,1)} fusion(bf16[512,2560]{0,1:T(8,128)(2,1)} %all-gather.9.cloned.1.call-done, bf16[1,512,1280]{2,1,0:T(8,128)(2,1)S(1)} %copy-done.4, f32[1280]{0:T(1024)S(1)} %convolution_reduce_fusion), kind=kOutput, calls=%fused_computation.1 | convolution fusion | flops 3360686080 | bytes 10490880 | tf_op jit(solution)/shard_map/tr,td->rd/dot_general | solution.py:66
  294.1 2.6 convolution_convert_fusion.4
  297.8 8.3 %fusion.5 = bf16[1,512,1280]{2,1,0:T(8,128)(2,1)} fusion(bf16[512,2560]{0,1:T(8,128)(2,1)} %all-gather.9.cloned.1.call-done, bf16[2560,1280]{1,0:T(8,128)(2,1)} %all-gather.11.cloned.1.call-done, f32[1280]{0:T(1024)S(1)} %convolution_reduce_fusion), kind=kOutput, calls=%fused_computation.10 | convolution fusion | flops 3356753920 | bytes 10490880 | tf_op jit(solution)/shard_map/dot_general | solution.py:47
  306.1 72.4 %reduce-scatter.6.cloned.1.call-done = bf16[128,5120]{1,0:T(8,128)(2,1)} async-done(((bf16[512,5120]{1,0:T(8,128)(2,1)}), bf16[128,5120]{1,0:T(8,128)(2,1)}) %reduce-scatter.6.cloned.1.call-update) | async-done | bytes 1310736 | tf_op jit(solution)/shard_map/reduce_scatter | solution.py:86
  378.5 2.4 slice_bitcast_fusion
  380.9 64.6 %reduce-scatter.8.cloned.1.call-done = bf16[320,1280]{1,0:T(8,128)(2,1)} async-done(((bf16[2560,1280]{1,0:T(8,128)(2,1)}), bf16[320,1280]{1,0:T(8,128)(2,1)}) %reduce-scatter.8.cloned.1.call-update) | async-done | bytes 819216 | tf_op jit(solution)/shard_map/reduce_scatter | solution.py:65
  445.5 2.4 convert_element_type.75
  (30 shorter events, 10.5 us)
Async XLA Ops:
  7.2 52.1 %all-gather.11.cloned.1.call-start = ((), (), s32[]{:S(2)}) async-start(), calls=%async_computation.6 | async-start | bytes 7372800 | tf_op jit(solution)/shard_map/all_gather | solution.py:49
  7.9 107.8 %all-gather.7.cloned.1.call-start = ((), (), s32[]{:S(2)}) async-start(), calls=%async_computation.4 | async-start | bytes 3276800 | tf_op jit(solution)/shard_map/all_gather | solution.py:17
  8.6 162.8 %all-gather.5.cloned.1.call-start = ((), (), s32[]{:S(2)}) async-start(), calls=%async_computation.3 | async-start | bytes 3276800 | tf_op jit(solution)/shard_map/all_gather | solution.py:16
  10.9 48.4 %copy-start.3 = (bf16[1,512,1280]{2,1,0:T(8,128)(2,1)S(1)}, bf16[1,512,1280]{2,1,0:T(8,128)(2,1)}, u32[]{:S(2)}) copy-start(bf16[1,512,1280]{2,1,0:T(8,128)(2,1)} %param.13) | copy-start | bytes 3932164
  10.9 213.0 %reduce-scatter.4.cloned.1.call-start = ((), (), s32[]{:S(2)}) async-start(), calls=%async_computation.7 | async-start | bytes 3276800 | tf_op jit(solution)/shard_map/reduce_scatter | solution.py:60
  67.0 1.1 copy-start.2
  67.0 217.3 %all-gather.9.cloned.1.call-start = ((), (), s32[]{:S(2)}) async-start(), calls=%async_computation.5 | async-start | bytes 3276800 | tf_op jit(solution)/shard_map/all_gather | solution.py:45
  229.7 148.8 %reduce-scatter.6.cloned.1.call-start = ((), (), s32[]{:S(2)}) async-start(), calls=%async_computation.8 | async-start | bytes 6553600 | tf_op jit(solution)/shard_map/reduce_scatter | solution.py:86
  241.3 2.4 copy-start.1
  252.9 31.5 %copy-start.4 = (bf16[1,512,1280]{2,1,0:T(8,128)(2,1)S(1)}, bf16[1,512,1280]{2,1,0:T(8,128)(2,1)}, u32[]{:S(2)}) copy-start(bf16[1,512,1280]{2,1,0:T(8,128)(2,1)} %param.13) | copy-start | bytes 3932164
  253.0 192.6 %reduce-scatter.8.cloned.1.call-start = ((), (), s32[]{:S(2)}) async-start(), calls=%async_computation.9 | async-start | bytes 7372800 | tf_op jit(solution)/shard_map/reduce_scatter | solution.py:65
  292.3 1.7 copy-start
Sparse Core Ops, SparseCore 0:
  9.9 49.3 all-gather.10
  60.8 54.7 all-gather.6
  117.8 53.6 all-gather.4
  173.6 50.2 reduce-scatter.3
  229.8 54.5 all-gather.8
  286.5 91.9 reduce-scatter.5
  382.0 63.5 reduce-scatter.7
where the time goes:
time: 456 us; the launch traced here: 455 us
  waiting for transfers between devices  355 us (78%)
  matrix products  51.2 us (11%)
  local copies, waits for them, and re-layouts  22.8 us (5%)
  between operations  14.9 us (3%)
  other arithmetic  10.4 us (2%)
    reduce_scatter x1, waiting for transfers between devices, on_device(): lax.psum_scatter(jnp.concatenate([key_part, value_part], axis=1).astype(j...  72.4 us
    reduce_scatter x1, waiting for transfers between devices, on_device(): lax.psum_scatter(jnp.einsum('tr,td->rd', columns, d_proj, preferred_eleme...  64.6 us
    all_gather x1, waiting for transfers between devices, on_device(): lax.all_gather(key_in, 'ctx', axis=1, tiled=True)  51.4 us
    all_gather x1, waiting for transfers between devices, on_device(): lax.all_gather(value, 'ctx', axis=1, tiled=True)  47.2 us
    reduce_scatter x1, waiting for transfers between devices, on_device(): lax.psum_scatter(partial_rows.astype(jnp.bfloat16), 'ctx', scatter_dimens...  43.4 us
    all_gather x1, waiting for transfers between devices, on_device(): lax.all_gather(out_weight, 'dp', axis=0, tiled=True)  43.3 us
    all_gather x1, waiting for transfers between devices, on_device(): attn_rows = lax.all_gather(attention, 'ctx', axis=0, tiled=True)  31.2 us
  transfers between devices with their start and end apart: 7, of which 7 were waited for; matrix products, arithmetic and copies ran while one was open for 16% of the time, Pallas kernels for 0%

commit v1 on v0

--- a/solution.py
+++ b/solution.py
@@ -1,12 +1,368 @@
 import jax
 import jax.numpy as jnp
 from jax import lax
+from jax.experimental import pallas as pl
+from jax.experimental.pallas import tpu as pltpu
 from jax.sharding import PartitionSpec as P
 
 HEAD_DIM = 128
-
-
-def on_device(query, key_in, value, gate_table, timestep, out_weight, grad_out):
+F32 = jnp.float32
+BF16 = jnp.bfloat16
+VMEM_LIMIT = 48 * 1024 * 1024
+
+
+def dot(a, b, dims):
+    return lax.dot_general(a, b, (dims, ((), ())), preferred_element_type=F32)
+
+
+def params():
+    return pltpu.CompilerParams(
+        dimension_semantics=("arbitrary",), vmem_limit_bytes=VMEM_LIMIT
+    )
+
+
+def cost(flops, nbytes, exps=0):
+    return pl.CostEstimate(flops=flops, bytes_accessed=nbytes, transcendentals=exps)
+
+
+def add_rounded(a, b):
+    return (a.astype(F32) + b.astype(F32)).astype(BF16)
+
+
+def probabilities(q, k):
+    scores = dot(q, k, ((1,), (1,))) * (HEAD_DIM ** (-0.5))
+    shifted = jnp.exp(scores - jnp.max(scores, axis=1, keepdims=True))
+    return shifted * (1.0 / jnp.sum(shifted, axis=1, keepdims=True))
+
+
+def attention_call(me, pieces):
+    n = len(pieces)
+    _, rows, width = pieces[0].shape
+    heads = width // HEAD_DIM
+
+    def body(me_ref, *refs):
+        piece_refs, out_ref = refs[:n], refs[n]
+        q, k, v = (jnp.concatenate([r[t] for r in piece_refs], axis=0) for t in range(3))
+        out = dot(probabilities(q, k).astype(BF16), v, ((1,), (0,))).astype(BF16)
+        for s in range(n):
+            slab = lax.rem(me_ref[0] + n - s, n)
+            out_ref[pl.ds(pl.multiple_of(slab * rows, rows), rows), :] = out[
+                s * rows : (s + 1) * rows
+            ]
+
+    length = n * rows
+    return pl.pallas_call(
+        body,
+        grid_spec=pltpu.PrefetchScalarGridSpec(
+            num_scalar_prefetch=1,
+            grid=(heads,),
+            in_specs=[pl.BlockSpec((3, rows, HEAD_DIM), lambda h, me: (0, 0, h))] * n,
+            out_specs=pl.BlockSpec((length, HEAD_DIM), lambda h, me: (0, h)),
+        ),
+        out_shape=jax.ShapeDtypeStruct((length, width), BF16),
+        compiler_params=params(),
+        cost_estimate=cost(
+            4 * length * length * width, 8 * length * width, heads * length * length
+        ),
+        name="attention_heads",
+    )(me, *pieces)
+
+
+def attention_grad_call(me, pieces, attention, d_terms):
+    n = len(pieces)
+    _, rows, width = pieces[0].shape
+    heads = width // HEAD_DIM
+    length = n * rows
+    n_terms = len(d_terms)
+    scale = HEAD_DIM ** (-0.5)
+
+    def body(me_ref, *refs):
+        piece_refs, attn_ref = refs[:n], refs[n]
+        term_refs, out_refs = refs[n + 1 : n + 1 + n_terms], refs[n + 1 + n_terms :]
+        q, k, v = (jnp.concatenate([r[t] for r in piece_refs], axis=0) for t in range(3))
+        places = [
+            pl.ds(pl.multiple_of(lax.rem(me_ref[0] + n - s, n) * rows, rows), rows)
+            for s in range(n)
+        ]
+        attn = jnp.concatenate([attn_ref[p, :] for p in places], axis=0).astype(F32)
+        d_attn = jnp.concatenate(
+            [sum(t[p, :].astype(F32) for t in term_refs) for p in places], axis=0
+        ).astype(BF16)
+        prob = probabilities(q, k)
+        delta = jnp.sum(d_attn.astype(F32) * attn, axis=1, keepdims=True)
+        d_prob = dot(d_attn, v, ((1,), (1,)))
+        d_half = (prob * (d_prob - delta) * scale).astype(BF16)
+        grads = (
+            dot(d_half, k, ((1,), (0,))),
+            dot(d_half, q, ((0,), (0,))),
+            dot(prob.astype(BF16), d_attn, ((0,), (0,))),
+        )
+        for t in range(3):
+            g = grads[t].astype(BF16)
+            for s in range(n):
+                out_refs[s][t] = g[s * rows : (s + 1) * rows]
+
+    piece = pl.BlockSpec((3, rows, HEAD_DIM), lambda h, me: (0, 0, h))
+    whole = pl.BlockSpec((length, HEAD_DIM), lambda h, me: (0, h))
+    return pl.pallas_call(
+        body,
+        grid_spec=pltpu.PrefetchScalarGridSpec(
+            num_scalar_prefetch=1,
+            grid=(heads,),
+            in_specs=[piece] * n + [whole] * (1 + n_terms),
+            out_specs=[piece] * n,
+        ),
+        out_shape=[jax.ShapeDtypeStruct((3, rows, width), BF16)] * n,
+        compiler_params=params(),
+        cost_estimate=cost(
+            10 * length * length * width, 24 * length * width, heads * length * length
+        ),
+        name="attention_heads_grad",
+    )(me, *pieces, attention, *d_terms)
+
+
+def d_attn_parts_call(me, d_proj, weight, n):
+    length, cols = d_proj.shape
+    width = weight.shape[0] // n
+
+    def body(me_ref, d_ref, w_ref, *out_refs):
+        part = dot(d_ref[...], w_ref[...], ((1,), (1,))).astype(BF16)
+        for s in range(n):
+
+            @pl.when(pl.program_id(0) == s)
+            def _():
+                out_refs[s][...] = part
+
+    return pl.pallas_call(
+        body,
+        grid_spec=pltpu.PrefetchScalarGridSpec(
+            num_scalar_prefetch=1,
+            grid=(n,),
+            in_specs=[
+                pl.BlockSpec((length, cols), lambda s, me: (0, 0)),
+                pl.BlockSpec((width, cols), lambda s, me: (lax.rem(me[0] + s, n), 0)),
+            ],
+            out_specs=[pl.BlockSpec((length, width), lambda s, me: (0, 0))] * n,
+        ),
+        out_shape=[jax.ShapeDtypeStruct((length, width), BF16)] * n,
+        compiler_params=params(),
+        cost_estimate=cost(
+            2 * length * cols * width * n, 2 * (length * cols + n * width * (cols + length))
+        ),
+        name="d_attn_parts",
+    )(me, d_proj, weight)
+
+
+def gathered_specs(n, length, width):
+    return [pl.BlockSpec((length, width), lambda s, *_: (0, 0))] * (2 * n - 1)
+
+
+def gathered_piece(refs, me, n, s):
+    own, from_left, from_right = refs[0], refs[1:n], refs[n:]
+    if s == 0:
+        return own[...]
+    return jnp.where(me + s < n, from_right[s - 1][...], from_left[n - s - 1][...])
+
+
+def projection_call(me, gathered, weight, gate_row, n):
+    length, width = gathered[0].shape
+    cols = weight.shape[1]
+
+    def body(me_ref, *refs):
+        w_ref, gate_ref, out_ref, total = refs[2 * n - 1 :]
+        for s in range(n):
+
+            @pl.when(pl.program_id(0) == s)
+            def _():
+                piece = gathered_piece(refs[: 2 * n - 1], me_ref[0], n, s)
+                term = dot(piece, w_ref[...], ((1,), (0,)))
+                if s == 0:
+                    total[...] = term
+                elif s < n - 1:
+                    total[...] += term
+                else:
+                    out_ref[...] = ((total[...] + term) * gate_ref[...]).astype(BF16)
+
+    return pl.pallas_call(
+        body,
+        grid_spec=pltpu.PrefetchScalarGridSpec(
+            num_scalar_prefetch=1,
+            grid=(n,),
+            in_specs=gathered_specs(n, length, width)
+            + [
+                pl.BlockSpec((width, cols), lambda s, me: (lax.rem(me[0] + s, n), 0)),
+                pl.BlockSpec((1, cols), lambda s, me: (0, 0)),
+            ],
+            out_specs=pl.BlockSpec((length, cols), lambda s, me: (0, 0)),
+            scratch_shapes=[pltpu.VMEM((length, cols), F32)],
+        ),
+        out_shape=jax.ShapeDtypeStruct((length, cols), BF16),
+        compiler_params=params(),
+        cost_estimate=cost(
+            2 * length * cols * width * n, 2 * (length * cols + n * width * (cols + 2 * length))
+        ),
+        name="projection",
+    )(me, *gathered, weight, gate_row)
+
+
+def weight_grad_call(place, gathered, d_proj, n, dp):
+    length, width = gathered[0].shape
+    cols = d_proj.shape[1]
+    rows = n * width // dp
+    per_piece = width // (2 * rows)
+
+    def body(place_ref, *refs):
+        d_ref, keep_ref, send_ref = refs[2 * n - 1 :]
+        for s in range(n):
+
+            @pl.when(pl.program_id(0) == s)
+            def _():
+                piece = gathered_piece(refs[: 2 * n - 1], place_ref[0], n, s)
+                term = dot(piece, d_ref[...], ((0,), (0,))).astype(BF16)
+                term = term.reshape(per_piece, 2, rows, cols)
+                first = place_ref[1] == 0
+                keep_ref[...] = jnp.where(first, term[:, 0], term[:, 1])
+                send_ref[...] = jnp.where(first, term[:, 1], term[:, 0])
+
+    block = pl.BlockSpec(
+        (per_piece, rows, cols), lambda s, place: (lax.rem(place[0] + s, n), 0, 0)
+    )
+    return pl.pallas_call(
+        body,
+        grid_spec=pltpu.PrefetchScalarGridSpec(
+            num_scalar_prefetch=1,
+            grid=(n,),
+            in_specs=gathered_specs(n, length, width)
+            + [pl.BlockSpec((length, cols), lambda s, place: (0, 0))],
+            out_specs=[block, block],
+        ),
+        out_shape=[jax.ShapeDtypeStruct((dp // 2, rows, cols), BF16)] * 2,
+        compiler_params=params(),
+        cost_estimate=cost(
+            2 * length * cols * width * n, 2 * (length * cols + n * width * (cols + 2 * length))
+        ),
+        name="weight_grad",
+    )(place, *gathered, d_proj)
+
+
+def assemble_call(me, pieces):
+    n = len(pieces)
+    _, rows, width = pieces[0].shape
+
+    def body(me_ref, *refs):
+        for t in range(3):
+            for s in range(n):
+                source = lax.rem(me_ref[0] + s, n)
+                refs[n + t][:, pl.ds(pl.multiple_of(source * width, 128), width)] = refs[s][t]
+
+    return pl.pallas_call(
+        body,
+        grid_spec=pltpu.PrefetchScalarGridSpec(
+            num_scalar_prefetch=1,
+            grid=(1,),
+            in_specs=[pl.BlockSpec((3, rows, width), lambda i, me: (0, 0, 0))] * n,
+            out_specs=[pl.BlockSpec((rows, n * width), lambda i, me: (0, 0))] * 3,
+        ),
+        out_shape=[jax.ShapeDtypeStruct((rows, n * width), BF16)] * 3,
+        compiler_params=params(),
+        cost_estimate=cost(0, 12 * n * rows * width),
+        name="assemble_heads",
+    )(me, *pieces)
+
+
+def shift(x, axis, by):
+    n = lax.axis_size(axis)
+    return lax.ppermute(x, axis, [(i, (i + by) % n) for i in range(n)])
+
+
+def line_gather(own, axis):
+    n = lax.axis_size(axis)
+    left, right = [], []
+    to_right = to_left = own
+    for i in range(1, n):
+        to_right = lax.ppermute(to_right, axis, [(d, d + 1) for d in range(i - 1, n - 1)])
+        to_left = lax.ppermute(to_left, axis, [(d, d - 1) for d in range(1, n - i + 1)])
+        left.append(to_right)
+        right.append(to_left)
+    return left, right
+
+
+def line_scatter(parts, axis):
+    n = lax.axis_size(axis)
+    to_right, to_left = parts[n - 1], parts[1]
+    for i in range(1, n):
+        if i > 1:
+            to_right = add_rounded(parts[n - i], to_right)
+            to_left = add_rounded(parts[i], to_left)
+        to_right = lax.ppermute(to_right, axis, [(d, d + 1) for d in range(i)])
+        to_left = lax.ppermute(to_left, axis, [(d, d - 1) for d in range(n - i, n)])
+    return [parts[0], to_right, to_left]
+
+
+def halving_scatter(keep, send, axis):
+    n = lax.axis_size(axis)
+    index = lax.axis_index(axis)
+
+    def swap(x, bit):
+        return lax.ppermute(x, axis, [(i, i ^ (1 << bit)) for i in range(n)])
+
+    bits = list(range(1, n.bit_length() - 1))
+    total = add_rounded(keep, swap(send, 0))
+    rows, cols = keep.shape[1:]
+    total = total.reshape((2,) * len(bits) + (2, rows // 2, cols))
+    halves = [lax.index_in_dim(total, i, len(bits), False) for i in range(2)]
+    orders = [bits, bits[::-1]]
+    left = [list(bits[::-1]), list(bits[::-1])]
+    for step in range(len(bits)):
+        for h in range(2):
+            bit = orders[h][step]
+            dim = left[h].index(bit)
+            left[h].remove(bit)
+            mine = (index >> bit) & 1
+            got = swap(lax.dynamic_index_in_dim(halves[h], 1 - mine, dim, False), bit)
+            kept = lax.dynamic_index_in_dim(halves[h], mine, dim, False)
+            halves[h] = kept.astype(F32) + got.astype(F32)
+            if step < len(bits) - 1:
+                halves[h] = halves[h].astype(BF16)
+    return jnp.concatenate(halves, axis=0)
+
+
+def by_heads(query, key_in, value, gate_table, timestep, out_weight, grad_out):
+    n, dp = lax.axis_size("ctx"), lax.axis_size("dp")
+    me = lax.axis_index("ctx").astype(jnp.int32)
+    me_ref = me[None]
+    width = query.shape[2] // n
+    weight = lax.all_gather(out_weight, "dp", axis=0, tiled=True)
+
+    def columns_for(device):
+        return jnp.concatenate(
+            [lax.dynamic_slice_in_dim(x, device * width, width, 2) for x in (query, key_in, value)],
+            axis=0,
+        )
+
+    pieces = [columns_for(me)]
+    pieces += [shift(columns_for((me + s) % n), "ctx", s) for s in range(1, n)]
+
+    gate_row = lax.dynamic_slice_in_dim(gate_table, timestep[0], 1, 0)
+    d_proj = (grad_out[0].astype(F32) * gate_row).astype(BF16)
+
+    attention = attention_call(me_ref, pieces)
+    parts = d_attn_parts_call(me_ref, d_proj, weight, n)
+    left, right = line_gather(attention, "ctx")
+    d_terms = line_scatter(parts, "ctx")
+    gathered = [attention] + left + right
+    place = jnp.stack([me, (lax.axis_index("dp") % 2).astype(jnp.int32)])
+    keep, send = weight_grad_call(place, gathered, d_proj, n, dp)
+    grad_weight = halving_scatter(keep, send, "dp")
+    branch_out = projection_call(me_ref, gathered, weight, gate_row, n)[None]
+
+    grads = attention_grad_call(me_ref, pieces, attention, d_terms)
+    grads = [grads[0]] + [shift(grads[s], "ctx", -s) for s in range(1, n)]
+    grad_query, grad_key, grad_value = assemble_call(me_ref, grads)
+    return (branch_out, grad_query[None], grad_key[None], grad_value[None], grad_weight)
+
+
+def by_tokens(query, key_in, value, gate_table, timestep, out_weight, grad_out):
     slab_rows = query.shape[1]
     attn_width = query.shape[2]
     head_count = attn_width // HEAD_DIM
@@ -94,6 +450,16 @@
     return (branch_out, grad_query[None], grad_key[None], grad_value[None], grad_weight)
 
 
+def on_device(query, key_in, value, gate_table, timestep, out_weight, grad_out):
+    n, dp = lax.axis_size("ctx"), lax.axis_size("dp")
+    heads = query.shape[2] // HEAD_DIM
+    rows = out_weight.shape[0]
+    fits = heads % n == 0 and dp & (dp - 1) == 0 and dp >= 4
+    fits = fits and (heads // n) * HEAD_DIM % (2 * rows) == 0 and rows % 32 == 0 and n > 1
+    plan = by_heads if fits else by_tokens
+    return plan(query, key_in, value, gate_table, timestep, out_weight, grad_out)
+
+
 def solution(mesh):
     in_specs = (
         P("dp", "ctx", None),

time: 456 us -> 266 us (0.58)
  waiting for transfers between devices: 355 us -> 145 us
  matrix products: 51.2 us -> 0 us
  starting transfers between devices: 0.46 us -> 47.3 us
  Pallas kernels: 0 us -> 37.8 us
  local copies, waits for them, and re-layouts: 22.8 us -> 10 us
    reduce_scatter x3 -> x0, waiting for transfers between devices: 180 us -> none  [the longest x1 72.4 us: on_device(): lax.psum_scatter(jnp.concatenate([key_part, value_part], axis=1).astype(j...]
    all_gather x4 -> x1, waiting for transfers between devices: 173 us -> 0.01 us  [by_heads(): weight = lax.all_gather(out_weight, 'dp', axis=0, tiled=True)]
    ppermute x0 -> x23, waiting for transfers between devices: none -> 144 us  [the longest x6 59.9 us: shift(): return lax.ppermute(x, axis, [(i, (i + by) % n) for i in range(n)])]
    ppermute x0 -> x23, starting transfers between devices: none -> 47.2 us  [the longest x3 15.1 us: line_gather(): lax.ppermute(to_right, axis, [(d, d + 1) for d in range(i - 1, n - 1)])]
    dot_general x9 -> x0, matrix products: 45.3 us -> none  [the longest x1 8.34 us: on_device(): jnp.dot(columns, lax.all_gather(out_weight, 'dp', axis=0, tiled=True), pr...]
    pallas_call x0 -> x6, Pallas kernels: none -> 37.8 us  [the longest x1 8.46 us: attention_grad_call(): pl.pallas_call(body, grid_spec=pltpu.PrefetchScalarGridSpec(num_scalar_pr...]
    reshape x2 -> x0, local copies, waits for them, and re-layouts: 7.46 us -> none  [the longest x1 4.47 us: on_device(): key_part = jnp.einsum('hqk,qhd->khd', d_half, query_heads, preferred_elem...]
    sub x1 -> x0, matrix products: 5.9 us -> none  [on_device(): exp_scores = jnp.exp(scores - row_max)]
  transfers between devices with their start and end apart: 7 -> 24, of which waited for: 7 -> 13; matrix products, arithmetic and copies ran while one was open for 16% -> 6% of each run, Pallas kernels for 0% -> 11%
where the time goes in v1:
time: 266 us; the launch traced here: 265 us
  waiting for transfers between devices  145 us (55%)
  starting transfers between devices  47.3 us (18%)
  Pallas kernels  37.8 us (14%)
  between operations  15.1 us (6%)
  other arithmetic  10.3 us (4%)
  local copies, waits for them, and re-layouts  10 us (4%)
    ppermute x6, waiting for transfers between devices, shift(): return lax.ppermute(x, axis, [(i, (i + by) % n) for i in range(n)])  59.9 us
    ppermute x3, waiting for transfers between devices, line_gather(): lax.ppermute(to_left, axis, [(d, d - 1) for d in range(1, n - i + 1)])  29.7 us
    ppermute x3, waiting for transfers between devices, line_scatter(): to_right = lax.ppermute(to_right, axis, [(d, d + 1) for d in range(i)])  24.4 us
    ppermute x3, starting transfers between devices, line_gather(): lax.ppermute(to_right, axis, [(d, d + 1) for d in range(i - 1, n - 1)])  15.1 us
    ppermute x3, waiting for transfers between devices, line_gather(): lax.ppermute(to_right, axis, [(d, d + 1) for d in range(i - 1, n - 1)])  12.9 us
    ppermute x5, waiting for transfers between devices, swap(): return lax.ppermute(x, axis, [(i, i ^ 1 << bit) for i in range(n)])  12.5 us
    ppermute x3, starting transfers between devices, line_scatter(): to_right = lax.ppermute(to_right, axis, [(d, d + 1) for d in range(i)])  10.6 us
    ppermute x6, starting transfers between devices, shift(): return lax.ppermute(x, axis, [(i, (i + by) % n) for i in range(n)])  9.46 us
  transfers between devices with their start and end apart: 24, of which 13 were waited for; matrix products, arithmetic and copies ran while one was open for 6% of the time, Pallas kernels for 11%

profile of v1, /device:TPU:0, one launch (start us, length us, event | category | flops | bytes accessed | tf_op | source)
XLA Modules:
  0.0 265.1 jit_solution(16860835590766068123)
XLA Ops:
  9.4 3.1 %collective-permute-start = (bf16[3,128,640]{2,1,0:T(8,128)(2,1)S(1)}, bf16[3,128,640]{2,1,0:T(8,128)(2,1)S(1)}, u32[]{:S(2)}, u32[]{:S(2)}) collective-permute-start(bf16[3,128,640]{2,1,0:T(8,128)(2,1)S(1)} %pad_maximum_fusion.2), channel_id=1, source_target_pairs={{0,1},{1,2},{2,3},{3,0},{4,5},{5,6},{6,7},{7,4},{8,9},{9,10},{10,1... | collective-permute-start | bytes 1474568 | tf_op jit(solution)/shard_map/ppermute | solution.py:275
  12.6 2.7 %collective-permute-start.1 = (bf16[3,128,640]{2,1,0:T(8,128)(2,1)S(1)}, bf16[3,128,640]{2,1,0:T(8,128)(2,1)S(1)}, u32[]{:S(2)}, u32[]{:S(2)}) collective-permute-start(bf16[3,128,640]{2,1,0:T(8,128)(2,1)S(1)} %pad_maximum_fusion.3), channel_id=1, source_target_pairs={{0,2},{1,3},{2,0},{3,1},{4,6},{5,7},{6,4},{7,5},{8,10},{9,11},{10,... | collective-permute-start | bytes 1474568 | tf_op jit(solution)/shard_map/ppermute | solution.py:275
  16.8 9.9 %collective-permute-done.refs_1_ = bf16[3,128,640]{2,1,0:T(8,128)(2,1)S(1)} collective-permute-done((bf16[3,128,640]{2,1,0:T(8,128)(2,1)S(1)}, bf16[3,128,640]{2,1,0:T(8,128)(2,1)S(1)}, u32[]{:S(2)}, u32[]{:S(2)}) %collective-permute-start) | collective-permute-done | bytes 491552 | tf_op jit(solution)/shard_map/ppermute | solution.py:275
  26.7 20.2 %collective-permute-done.1.refs_2_ = bf16[3,128,640]{2,1,0:T(8,128)(2,1)S(1)} collective-permute-done((bf16[3,128,640]{2,1,0:T(8,128)(2,1)S(1)}, bf16[3,128,640]{2,1,0:T(8,128)(2,1)S(1)}, u32[]{:S(2)}, u32[]{:S(2)}) %collective-permute-start.1) | collective-permute-done | bytes 491552 | tf_op jit(solution)/shard_map/ppermute | solution.py:275
  47.0 5.4 %attention_heads.1.refs_0_.refs_4_ = bf16[512,640]{1,0:T(8,128)(2,1)S(1)} custom-call(s32[1]{0:T(128)} %bitcast.me_ref, bf16[3,128,640]{2,1,0:T(8,128)(2,1)S(1)} %pad_maximum_fusion.1.refs_0_, bf16[3,128,640]{2,1,0:T(8,128)(2,1)S(1)} %collective-permute-done.refs_1_, bf16[3,128,640]{2,1,0:T(8,128)(2,1)S(1)} %collective-permute-done.1.refs_2_, ...), custom_call_target="tpu_custom_call" | custom-call | flops 671088640 | bytes 2621440 | tf_op jit(solution)/shard_map/attention_heads/pallas_call | solution.py:54
  52.4 12.9 %collective-permute-start.3 = (bf16[512,640]{1,0:T(8,128)(2,1)S(1)}, bf16[512,640]{1,0:T(8,128)(2,1)S(1)}, u32[]{:S(2)}, u32[]{:S(2)}) collective-permute-start(bf16[512,640]{1,0:T(8,128)(2,1)S(1)} %attention_heads.1.refs_0_.refs_4_), channel_id=1, source_target_pairs={{0,1},{1,2},{2,3},{4,5},{5,6},{6,7},{8,9},{9,10},{10,11},{12,13},{... | collective-permute-start | bytes 1966088 | tf_op jit(solution)/shard_map/ppermute | solution.py:283
  66.6 12.9 %collective-permute-done.3.refs_1_ = bf16[512,640]{1,0:T(8,128)(2,1)S(1)} collective-permute-done((bf16[512,640]{1,0:T(8,128)(2,1)S(1)}, bf16[512,640]{1,0:T(8,128)(2,1)S(1)}, u32[]{:S(2)}, u32[]{:S(2)}) %collective-permute-start.3) | collective-permute-done | bytes 655392 | tf_op jit(solution)/shard_map/ppermute | solution.py:283
  81.0 2.7 %collective-permute-done.6.refs_4_ = bf16[512,640]{1,0:T(8,128)(2,1)S(1)} collective-permute-done((bf16[512,640]{1,0:T(8,128)(2,1)S(1)}, bf16[512,640]{1,0:T(8,128)(2,1)S(1)}, u32[]{:S(2)}, u32[]{:S(2)}) %collective-permute-start.6) | collective-permute-done | bytes 655392 | tf_op jit(solution)/shard_map/ppermute | solution.py:284
  88.1 13.2 %collective-permute-done.7.refs_5_ = bf16[512,640]{1,0:T(8,128)(2,1)} collective-permute-done((bf16[512,640]{1,0:T(8,128)(2,1)S(1)}, bf16[512,640]{1,0:T(8,128)(2,1)}, u32[]{:S(2)}, u32[]{:S(2)}) %collective-permute-start.7) | collective-permute-done | bytes 655392 | tf_op jit(solution)/shard_map/ppermute | solution.py:284
  104.2 13.9 %collective-permute-done.8.refs_6_ = bf16[512,640]{1,0:T(8,128)(2,1)S(1)} collective-permute-done((bf16[512,640]{1,0:T(8,128)(2,1)}, bf16[512,640]{1,0:T(8,128)(2,1)S(1)}, u32[]{:S(2)}, u32[]{:S(2)}) %collective-permute-start.8) | collective-permute-done | bytes 655392 | tf_op jit(solution)/shard_map/ppermute | solution.py:284
  118.1 7.6 %weight_grad.1 = (bf16[4,320,1280]{2,1,0:T(8,128)(2,1)}, bf16[4,320,1280]{2,1,0:T(8,128)(2,1)}) custom-call(s32[2]{0:T(128)S(1)} %pad_add_fusion.place_ref, bf16[512,640]{1,0:T(8,128)(2,1)S(1)} %attention_heads.1.refs_0_.refs_4_, bf16[512,640]{1,0:T(8,128)(2,1)S(1)} %collective-permute-done.3.refs_1_, bf16[512,640]{1,0:T(8,128)(2,1)} %collective-permute-done.4.refs_2_, ...), custom_call_target="tpu_custom_call" | custom-call | flops 3355443200 | bytes 13107200 | tf_op jit(solution)/shard_map/weight_grad/pallas_call | solution.py:230
  125.8 6.2 %collective-permute-done.18 = bf16[4,320,1280]{2,1,0:T(8,128)(2,1)} collective-permute-done((bf16[4,320,1280]{2,1,0:T(8,128)(2,1)}, bf16[4,320,1280]{2,1,0:T(8,128)(2,1)}, u32[]{:S(2)}, u32[]{:S(2)}) %collective-permute-start.18) | collective-permute-done | bytes 3276832 | tf_op jit(solution)/shard_map/ppermute | solution.py:307
  132.0 3.7 %add_convert_fusion = bf16[4,320,1280]{2,1,0:T(8,128)(2,1)S(1)} fusion(bf16[4,320,1280]{2,1,0:T(8,128)(2,1)} %collective-permute-done.18, bf16[4,320,1280]{2,1,0:T(8,128)(2,1)} %get-tuple-element.29), kind=kLoop, calls=%fused_computation | loop fusion | flops 6553600 | bytes 9830400 | tf_op jit(solution)/shard_map/convert_element_type | solution.py:29
  144.3 6.9 %d_attn_parts.1 = (bf16[512,640]{1,0:T(8,128)(2,1)S(1)}, bf16[512,640]{1,0:T(8,128)(2,1)S(1)}, bf16[512,640]{1,0:T(8,128)(2,1)S(1)}, bf16[512,640]{1,0:T(8,128)(2,1)S(1)}) custom-call(s32[1]{0:T(128)} %bitcast.me_ref, bf16[512,1280]{1,0:T(8,128)(2,1)S(1)} %fusion.d_ref.refs_7_, bf16[2560,1280]{1,0:T(8,128)(2,1)} %all-gather.2.cloned.1.call-done.refs_7_.w_ref), custom_call_target="tpu_custom_call" | custom-call | flops 3355443200 | bytes 10485760 | tf_op jit(solution)/shard_map/d_attn_parts/pallas_call | solution.py:136
  153.6 6.3 %collective-permute-done.21 = bf16[2,160,1280]{2,1,0:T(8,128)(2,1)} collective-permute-done((bf16[2,160,1280]{2,1,0:T(8,128)(2,1)}, bf16[2,160,1280]{2,1,0:T(8,128)(2,1)}, u32[]{:S(2)}, u32[]{:S(2)}) %collective-permute-start.21) | collective-permute-done | bytes 819232 | tf_op jit(solution)/shard_map/ppermute | solution.py:307
  162.8 4.5 %collective-permute-done.9 = bf16[512,640]{1,0:T(8,128)(2,1)S(1)} collective-permute-done((bf16[512,640]{1,0:T(8,128)(2,1)S(1)}, bf16[512,640]{1,0:T(8,128)(2,1)S(1)}, u32[]{:S(2)}, u32[]{:S(2)}) %collective-permute-start.9) | collective-permute-done | bytes 655392 | tf_op jit(solution)/shard_map/ppermute | solution.py:297
  167.6 4.6 %collective-permute-start.10 = (bf16[512,640]{1,0:T(8,128)(2,1)S(1)}, bf16[512,640]{1,0:T(8,128)(2,1)S(1)}, u32[]{:S(2)}, u32[]{:S(2)}) collective-permute-start(bf16[512,640]{1,0:T(8,128)(2,1)S(1)} %get-tuple-element.36), channel_id=1, source_target_pairs={{0,1},{1,2},{4,5},{5,6},{8,9},{9,10},{12,13},{13,14},{16,17},{17,1... | collective-permute-start | bytes 1966088 | tf_op jit(solution)/shard_map/ppermute | solution.py:297
  174.8 10.1 %collective-permute-done.10 = bf16[512,640]{1,0:T(8,128)(2,1)S(1)} collective-permute-done((bf16[512,640]{1,0:T(8,128)(2,1)S(1)}, bf16[512,640]{1,0:T(8,128)(2,1)S(1)}, u32[]{:S(2)}, u32[]{:S(2)}) %collective-permute-start.10) | collective-permute-done | bytes 655392 | tf_op jit(solution)/shard_map/ppermute | solution.py:297
  185.1 4.4 %collective-permute-start.11 = (bf16[512,640]{1,0:T(8,128)(2,1)S(1)}, bf16[512,640]{1,0:T(8,128)(2,1)S(1)}, u32[]{:S(2)}, u32[]{:S(2)}) collective-permute-start(bf16[512,640]{1,0:T(8,128)(2,1)S(1)} %add_convert_fusion.2), channel_id=1, source_target_pairs={{0,1},{1,2},{2,3},{4,5},{5,6},{6,7},{8,9},{9,10},{10,11},{12,13},{... | collective-permute-start | bytes 1966088 | tf_op jit(solution)/shard_map/ppermute | solution.py:297
  191.6 9.8 %collective-permute-done.11.refs_6_ = bf16[512,640]{1,0:T(8,128)(2,1)S(1)} collective-permute-done((bf16[512,640]{1,0:T(8,128)(2,1)S(1)}, bf16[512,640]{1,0:T(8,128)(2,1)S(1)}, u32[]{:S(2)}, u32[]{:S(2)}) %collective-permute-start.11) | collective-permute-done | bytes 655392 | tf_op jit(solution)/shard_map/ppermute | solution.py:297
  201.4 4.5 %collective-permute-done.14.refs_7_ = bf16[512,640]{1,0:T(8,128)(2,1)S(1)} collective-permute-done((bf16[512,640]{1,0:T(8,128)(2,1)S(1)}, bf16[512,640]{1,0:T(8,128)(2,1)S(1)}, u32[]{:S(2)}, u32[]{:S(2)}) %collective-permute-start.14) | collective-permute-done | bytes 655392 | tf_op jit(solution)/shard_map/ppermute | solution.py:298
  206.8 8.5 %attention_heads_grad.1 = (bf16[3,128,640]{2,1,0:T(8,128)(2,1)S(1)}, bf16[3,128,640]{2,1,0:T(8,128)(2,1)S(1)}, bf16[3,128,640]{2,1,0:T(8,128)(2,1)S(1)}, bf16[3,128,640]{2,1,0:T(8,128)(2,1)S(1)}) custom-call(s32[1]{0:T(128)} %bitcast.me_ref, bf16[3,128,640]{2,1,0:T(8,128)(2,1)S(1)} %pad_maximum_fusion.1.refs_0_, bf16[3,128,640]{2,1,0:T(8,128)(2,1)S(1)} %copy-done.8, ...), custom_call_target="tpu_custom_call" | custom-call | flops 1677721600 | bytes 7864320 | tf_op jit(solution)/shard_map/attention_heads_grad/pallas_call | solution.py:107
  219.2 8.0 %projection.1 = bf16[512,1280]{1,0:T(8,128)(2,1)} custom-call(s32[1]{0:T(128)} %bitcast.me_ref, bf16[512,640]{1,0:T(8,128)(2,1)S(1)} %attention_heads.1.refs_0_.refs_4_, bf16[512,640]{1,0:T(8,128)(2,1)S(1)} %collective-permute-done.3.refs_1_, bf16[512,640]{1,0:T(8,128)(2,1)} %collective-permute-done.4.refs_2_, bf16[512,640]{1,0:T(8,128)(2,1)S(1)} %copy-done.4, ...), custom_call_target="tpu_custom_call" | custom-call | flops 3355443200 | bytes 13107200 | tf_op jit(solution)/shard_map/projection/pallas_call | solution.py:186
  227.2 29.7 %collective-permute-done.16.refs_2_ = bf16[3,128,640]{2,1,0:T(8,128)(2,1)S(1)} collective-permute-done((bf16[3,128,640]{2,1,0:T(8,128)(2,1)S(1)}, bf16[3,128,640]{2,1,0:T(8,128)(2,1)S(1)}, u32[]{:S(2)}, u32[]{:S(2)}) %collective-permute-start.16) | collective-permute-done | bytes 491552 | tf_op jit(solution)/shard_map/ppermute | solution.py:275
  (92 shorter events, 38.4 us)
Async XLA Ops:
  7.2 137.2 %all-gather.2.cloned.1.call-start = ((), (), s32[]{:S(2)}) async-start(), calls=%async_computation | async-start | bytes 7372800 | tf_op jit(solution)/shard_map/all_gather | solution.py:335
  9.4 17.3 %collective-permute-start = (bf16[3,128,640]{2,1,0:T(8,128)(2,1)S(1)}, bf16[3,128,640]{2,1,0:T(8,128)(2,1)S(1)}, u32[]{:S(2)}, u32[]{:S(2)}) collective-permute-start(bf16[3,128,640]{2,1,0:T(8,128)(2,1)S(1)} %pad_maximum_fusion.2), channel_id=1, source_target_pairs={{0,1},{1,2},{2,3},{3,0},{4,5},{5,6},{6,7},{7,4},{8,9},{9,10},{10,1... | collective-permute-start | bytes 1474568 | tf_op jit(solution)/shard_map/ppermute | solution.py:275
  12.6 34.4 %collective-permute-start.1 = (bf16[3,128,640]{2,1,0:T(8,128)(2,1)S(1)}, bf16[3,128,640]{2,1,0:T(8,128)(2,1)S(1)}, u32[]{:S(2)}, u32[]{:S(2)}) collective-permute-start(bf16[3,128,640]{2,1,0:T(8,128)(2,1)S(1)} %pad_maximum_fusion.3), channel_id=1, source_target_pairs={{0,2},{1,3},{2,0},{3,1},{4,6},{5,7},{6,4},{7,5},{8,10},{9,11},{10,... | collective-permute-start | bytes 1474568 | tf_op jit(solution)/shard_map/ppermute | solution.py:275
  15.3 31.7 %collective-permute-start.2 = (bf16[3,128,640]{2,1,0:T(8,128)(2,1)S(1)}, bf16[3,128,640]{2,1,0:T(8,128)(2,1)S(1)}, u32[]{:S(2)}, u32[]{:S(2)}) collective-permute-start(bf16[3,128,640]{2,1,0:T(8,128)(2,1)S(1)} %pad_maximum_fusion.4), channel_id=1, source_target_pairs={{0,3},{1,0},{2,1},{3,2},{4,7},{5,4},{6,5},{7,6},{8,11},{9,8},{10,9... | collective-permute-start | bytes 1474568 | tf_op jit(solution)/shard_map/ppermute | solution.py:275
  52.4 27.2 %collective-permute-start.3 = (bf16[512,640]{1,0:T(8,128)(2,1)S(1)}, bf16[512,640]{1,0:T(8,128)(2,1)S(1)}, u32[]{:S(2)}, u32[]{:S(2)}) collective-permute-start(bf16[512,640]{1,0:T(8,128)(2,1)S(1)} %attention_heads.1.refs_0_.refs_4_), channel_id=1, source_target_pairs={{0,1},{1,2},{2,3},{4,5},{5,6},{6,7},{8,9},{9,10},{10,11},{12,13},{... | collective-permute-start | bytes 1966088 | tf_op jit(solution)/shard_map/ppermute | solution.py:283
  65.3 18.4 %collective-permute-start.6 = (bf16[512,640]{1,0:T(8,128)(2,1)S(1)}, bf16[512,640]{1,0:T(8,128)(2,1)S(1)}, u32[]{:S(2)}, u32[]{:S(2)}) collective-permute-start(bf16[512,640]{1,0:T(8,128)(2,1)S(1)} %attention_heads.1.refs_0_.refs_4_), channel_id=1, source_target_pairs={{1,0},{2,1},{3,2},{5,4},{6,5},{7,6},{9,8},{10,9},{11,10},{13,12},{... | collective-permute-start | bytes 1966088 | tf_op jit(solution)/shard_map/ppermute | solution.py:284
  79.5 7.8 %collective-permute-start.4 = (bf16[512,640]{1,0:T(8,128)(2,1)S(1)}, bf16[512,640]{1,0:T(8,128)(2,1)}, u32[]{:S(2)}, u32[]{:S(2)}) collective-permute-start(bf16[512,640]{1,0:T(8,128)(2,1)S(1)} %collective-permute-done.3.refs_1_), channel_id=1, source_target_pairs={{1,2},{2,3},{5,6},{6,7},{9,10},{10,11},{13,14},{14,15},{17,18},{18... | collective-permute-start | bytes 1966088 | tf_op jit(solution)/shard_map/ppermute | solution.py:283
  83.7 17.6 %collective-permute-start.7 = (bf16[512,640]{1,0:T(8,128)(2,1)S(1)}, bf16[512,640]{1,0:T(8,128)(2,1)}, u32[]{:S(2)}, u32[]{:S(2)}) collective-permute-start(bf16[512,640]{1,0:T(8,128)(2,1)S(1)} %collective-permute-done.6.refs_4_), channel_id=1, source_target_pairs={{1,0},{2,1},{5,4},{6,5},{9,8},{10,9},{13,12},{14,13},{17,16},{18,1... | collective-permute-start | bytes 1966088 | tf_op jit(solution)/shard_map/ppermute | solution.py:284
  87.4 16.8 %collective-permute-start.5 = (bf16[512,640]{1,0:T(8,128)(2,1)}, bf16[512,640]{1,0:T(8,128)(2,1)S(1)}, u32[]{:S(2)}, u32[]{:S(2)}) collective-permute-start(bf16[512,640]{1,0:T(8,128)(2,1)} %collective-permute-done.4.refs_2_), channel_id=1, source_target_pairs={{2,3},{6,7},{10,11},{14,15},{18,19},{22,23},{26,27},{30,31}} | collective-permute-start | bytes 1966088 | tf_op jit(solution)/shard_map/ppermute | solution.py:283
  101.3 16.8 %collective-permute-start.8 = (bf16[512,640]{1,0:T(8,128)(2,1)}, bf16[512,640]{1,0:T(8,128)(2,1)S(1)}, u32[]{:S(2)}, u32[]{:S(2)}) collective-permute-start(bf16[512,640]{1,0:T(8,128)(2,1)} %collective-permute-done.7.refs_5_), channel_id=1, source_target_pairs={{1,0},{5,4},{9,8},{13,12},{17,16},{21,20},{25,24},{29,28}} | collective-permute-start | bytes 1966088 | tf_op jit(solution)/shard_map/ppermute | solution.py:284
  125.7 6.2 %collective-permute-start.18 = (bf16[4,320,1280]{2,1,0:T(8,128)(2,1)}, bf16[4,320,1280]{2,1,0:T(8,128)(2,1)}, u32[]{:S(2)}, u32[]{:S(2)}) collective-permute-start(bf16[4,320,1280]{2,1,0:T(8,128)(2,1)} %get-tuple-element.30), channel_id=1, source_target_pairs={{0,4},{4,0},{8,12},{12,8},{16,20},{20,16},{24,28},{28,24},{1,5},{5... | collective-permute-start | bytes 9830408 | tf_op jit(solution)/shard_map/ppermute | solution.py:307
  139.3 20.6 %collective-permute-start.21 = (bf16[2,160,1280]{2,1,0:T(8,128)(2,1)}, bf16[2,160,1280]{2,1,0:T(8,128)(2,1)}, u32[]{:S(2)}, u32[]{:S(2)}) collective-permute-start(bf16[2,160,1280]{2,1,0:T(8,128)(2,1)} %dynamic-slice_bitcast_fusion), channel_id=1, source_target_pairs={{0,16},{4,20},{8,24},{12,28},{16,0},{20,4},{24,8},{28,12},{1,17},{... | collective-permute-start | bytes 2457608 | tf_op jit(solution)/shard_map/ppermute | solution.py:307
  142.9 30.0 %collective-permute-start.19 = (bf16[2,160,1280]{2,1,0:T(8,128)(2,1)}, bf16[2,160,1280]{2,1,0:T(8,128)(2,1)}, u32[]{:S(2)}, u32[]{:S(2)}) collective-permute-start(bf16[2,160,1280]{2,1,0:T(8,128)(2,1)} %dynamic-slice_bitcast_fusion.1), channel_id=1, source_target_pairs={{0,8},{4,12},{8,0},{12,4},{16,24},{20,28},{24,16},{28,20},{1,9},{5... | collective-permute-start | bytes 2457608 | tf_op jit(solution)/shard_map/ppermute | solution.py:307
  151.3 11.5 %collective-permute-start.12 = (bf16[512,640]{1,0:T(8,128)(2,1)S(1)}, bf16[512,640]{1,0:T(8,128)(2,1)S(1)}, u32[]{:S(2)}, u32[]{:S(2)}) collective-permute-start(bf16[512,640]{1,0:T(8,128)(2,1)S(1)} %get-tuple-element.19), channel_id=1, source_target_pairs={{3,2},{7,6},{11,10},{15,14},{19,18},{23,22},{27,26},{31,30}} | collective-permute-start | bytes 1966088 | tf_op jit(solution)/shard_map/ppermute | solution.py:298
  152.0 15.3 %collective-permute-start.9 = (bf16[512,640]{1,0:T(8,128)(2,1)S(1)}, bf16[512,640]{1,0:T(8,128)(2,1)S(1)}, u32[]{:S(2)}, u32[]{:S(2)}) collective-permute-start(bf16[512,640]{1,0:T(8,128)(2,1)S(1)} %get-tuple-element.21), channel_id=1, source_target_pairs={{0,1},{4,5},{8,9},{12,13},{16,17},{20,21},{24,25},{28,29}} | collective-permute-start | bytes 1966088 | tf_op jit(solution)/shard_map/ppermute | solution.py:297
  161.2 30.1 %collective-permute-start.22 = (bf16[160,1280]{1,0:T(8,128)(2,1)S(1)}, bf16[160,1280]{1,0:T(8,128)(2,1)S(1)}, u32[]{:S(2)}, u32[]{:S(2)}) collective-permute-start(bf16[160,1280]{1,0:T(8,128)(2,1)S(1)} %dynamic-slice_bitcast_fusion.2), channel_id=1, source_target_pairs={{0,8},{4,12},{8,0},{12,4},{16,24},{20,28},{24,16},{28,20},{1,9},{5... | collective-permute-start | bytes 1228808 | tf_op jit(solution)/shard_map/ppermute | solution.py:307
  167.6 17.4 %collective-permute-start.10 = (bf16[512,640]{1,0:T(8,128)(2,1)S(1)}, bf16[512,640]{1,0:T(8,128)(2,1)S(1)}, u32[]{:S(2)}, u32[]{:S(2)}) collective-permute-start(bf16[512,640]{1,0:T(8,128)(2,1)S(1)} %get-tuple-element.36), channel_id=1, source_target_pairs={{0,1},{1,2},{4,5},{5,6},{8,9},{9,10},{12,13},{13,14},{16,17},{17,1... | collective-permute-start | bytes 1966088 | tf_op jit(solution)/shard_map/ppermute | solution.py:297
  172.2 17.4 %collective-permute-start.13 = (bf16[512,640]{1,0:T(8,128)(2,1)S(1)}, bf16[512,640]{1,0:T(8,128)(2,1)S(1)}, u32[]{:S(2)}, u32[]{:S(2)}) collective-permute-start(bf16[512,640]{1,0:T(8,128)(2,1)S(1)} %get-tuple-element.35), channel_id=1, source_target_pairs={{2,1},{3,2},{6,5},{7,6},{10,9},{11,10},{14,13},{15,14},{18,17},{19... | collective-permute-start | bytes 1966088 | tf_op jit(solution)/shard_map/ppermute | solution.py:298
  174.3 17.2 %collective-permute-start.20 = (bf16[160,1280]{1,0:T(8,128)(2,1)S(1)}, bf16[160,1280]{1,0:T(8,128)(2,1)S(1)}, u32[]{:S(2)}, u32[]{:S(2)}) collective-permute-start(bf16[160,1280]{1,0:T(8,128)(2,1)S(1)} %dynamic-slice_bitcast_fusion.3), channel_id=1, source_target_pairs={{0,16},{4,20},{8,24},{12,28},{16,0},{20,4},{24,8},{28,12},{1,17},{... | collective-permute-start | bytes 1228808 | tf_op jit(solution)/shard_map/ppermute | solution.py:307
  185.1 16.3 %collective-permute-start.11 = (bf16[512,640]{1,0:T(8,128)(2,1)S(1)}, bf16[512,640]{1,0:T(8,128)(2,1)S(1)}, u32[]{:S(2)}, u32[]{:S(2)}) collective-permute-start(bf16[512,640]{1,0:T(8,128)(2,1)S(1)} %add_convert_fusion.2), channel_id=1, source_target_pairs={{0,1},{1,2},{2,3},{4,5},{5,6},{6,7},{8,9},{9,10},{10,11},{12,13},{... | collective-permute-start | bytes 1966088 | tf_op jit(solution)/shard_map/ppermute | solution.py:297
  189.8 16.2 %collective-permute-start.14 = (bf16[512,640]{1,0:T(8,128)(2,1)S(1)}, bf16[512,640]{1,0:T(8,128)(2,1)S(1)}, u32[]{:S(2)}, u32[]{:S(2)}) collective-permute-start(bf16[512,640]{1,0:T(8,128)(2,1)S(1)} %add_convert_fusion.1), channel_id=1, source_target_pairs={{1,0},{2,1},{3,2},{5,4},{6,5},{7,6},{9,8},{10,9},{11,10},{13,12},{... | collective-permute-start | bytes 1966088 | tf_op jit(solution)/shard_map/ppermute | solution.py:298
  215.2 11.9 %collective-permute-start.15 = (bf16[3,128,640]{2,1,0:T(8,128)(2,1)S(1)}, bf16[3,128,640]{2,1,0:T(8,128)(2,1)S(1)}, u32[]{:S(2)}, u32[]{:S(2)}) collective-permute-start(bf16[3,128,640]{2,1,0:T(8,128)(2,1)S(1)} %get-tuple-element.23), channel_id=1, source_target_pairs={{0,3},{1,0},{2,1},{3,2},{4,7},{5,4},{6,5},{7,6},{8,11},{9,8},{10,9... | collective-permute-start | bytes 1474568 | tf_op jit(solution)/shard_map/ppermute | solution.py:275
  215.3 41.5 %collective-permute-start.16 = (bf16[3,128,640]{2,1,0:T(8,128)(2,1)S(1)}, bf16[3,128,640]{2,1,0:T(8,128)(2,1)S(1)}, u32[]{:S(2)}, u32[]{:S(2)}) collective-permute-start(bf16[3,128,640]{2,1,0:T(8,128)(2,1)S(1)} %get-tuple-element.24), channel_id=1, source_target_pairs={{0,2},{1,3},{2,0},{3,1},{4,6},{5,7},{6,4},{7,5},{8,10},{9,11},{10,... | collective-permute-start | bytes 1474568 | tf_op jit(solution)/shard_map/ppermute | solution.py:275
  217.3 39.6 %collective-permute-start.17 = (bf16[3,128,640]{2,1,0:T(8,128)(2,1)S(1)}, bf16[3,128,640]{2,1,0:T(8,128)(2,1)S(1)}, u32[]{:S(2)}, u32[]{:S(2)}) collective-permute-start(bf16[3,128,640]{2,1,0:T(8,128)(2,1)S(1)} %get-tuple-element.25), channel_id=1, source_target_pairs={{0,1},{1,2},{2,3},{3,0},{4,5},{5,6},{6,7},{7,4},{8,9},{9,10},{10,1... | collective-permute-start | bytes 1474568 | tf_op jit(solution)/shard_map/ppermute | solution.py:275
  (19 other events, 275.4 us)
Sparse Core Ops, SparseCore 0:
  9.9 49.3 all-gather.1

commit v2 on v0

--- a/solution.py
+++ b/solution.py
@@ -1,12 +1,566 @@
+import math
+
 import jax
 import jax.numpy as jnp
 from jax import lax
+from jax.experimental import pallas as pl
+from jax.experimental.pallas import tpu as pltpu
 from jax.sharding import PartitionSpec as P
 
 HEAD_DIM = 128
-
-
-def on_device(query, key_in, value, gate_table, timestep, out_weight, grad_out):
+F32 = jnp.float32
+BF16 = jnp.bfloat16
+MIB = 1024 * 1024
+PARTS = 2
+
+
+def dot(a, b, dims):
+    return lax.dot_general(a, b, (dims, ((), ())), preferred_element_type=F32)
+
+
+def params(mib=32):
+    return pltpu.CompilerParams(
+        dimension_semantics=("arbitrary",), vmem_limit_bytes=mib * MIB
+    )
+
+
+def cost(flops, nbytes, exps=0):
+    return pl.CostEstimate(flops=flops, bytes_accessed=nbytes, transcendentals=exps)
+
+
+def any_specs(count):
+    return [pl.BlockSpec(memory_space=pl.ANY)] * count
+
+
+def add_rounded(a, b):
+    return (a.astype(F32) + b.astype(F32)).astype(BF16)
+
+
+def exponentials(q, k):
+    scores = dot(k, q, ((1,), (1,)))
+    top = jnp.max(scores, axis=0, keepdims=True)
+    shifted = jnp.exp2((scores - top) * (HEAD_DIM ** (-0.5) * math.log2(math.e)))
+    return shifted, 1.0 / jnp.sum(shifted, axis=0, keepdims=True)
+
+
+def slab_rows(me, n, rows):
+    return [pl.ds(pl.multiple_of(lax.rem(me + n - s, n) * rows, rows), rows) for s in range(n)]
+
+
+def head_lanes(width):
+    return [slice(i, i + HEAD_DIM) for i in range(0, width, HEAD_DIM)]
+
+
+def pack_call(place, query, key_in, value, n, widths):
+    rows, width = query.shape[1], sum(widths)
+
+    def body(place_ref, *refs):
+        for s in range(n):
+
+            @pl.when(pl.program_id(0) == s)
+            def _():
+                start = 0
+                for g in range(len(widths)):
+                    for t in range(3):
+                        refs[3 + g * n + s][t] = refs[t][0, :, start : start + widths[g]]
+                    start += widths[g]
+
+    block = pl.BlockSpec((1, rows, width), lambda s, p: (0, 0, lax.rem(p[0] + s, n)))
+    outs = pl.pallas_call(
+        body,
+        grid_spec=pltpu.PrefetchScalarGridSpec(
+            num_scalar_prefetch=1,
+            grid=(n,),
+            in_specs=[block] * 3,
+            out_specs=[
+                pl.BlockSpec((3, rows, w), lambda s, p: (0, 0, 0)) for w in widths for _ in range(n)
+            ],
+        ),
+        out_shape=[jax.ShapeDtypeStruct((3, rows, w), BF16) for w in widths for _ in range(n)],
+        compiler_params=params(),
+        cost_estimate=cost(0, 12 * n * rows * width),
+        name="pack_heads",
+    )(place, query, key_in, value)
+    return [list(outs[g * n : (g + 1) * n]) for g in range(len(widths))]
+
+
+def attention_call(place, pieces):
+    n = len(pieces)
+    _, rows, width = pieces[0].shape
+    length = n * rows
+    block = length // PARTS
+
+    def body(place_ref, *refs):
+        piece_refs, out_refs, out_ref = refs[:n], refs[n:-1], refs[-1]
+        places = slab_rows(place_ref[0], n, rows)
+        for lanes in head_lanes(width):
+            q, k, v = (
+                jnp.concatenate([r[t, :, lanes] for r in piece_refs], axis=0) for t in range(3)
+            )
+            shifted, inverse = exponentials(q, k)
+            out = dot(v, shifted.astype(BF16), ((0,), (0,))) * inverse
+            out = out.T.astype(BF16)
+            for s in range(n):
+                out_ref[places[s], lanes] = out[s * rows : (s + 1) * rows]
+        for i in range(PARTS):
+            out_refs[i][...] = out_ref[i * block : (i + 1) * block]
+
+    return pl.pallas_call(
+        body,
+        grid_spec=pltpu.PrefetchScalarGridSpec(
+            num_scalar_prefetch=1,
+            grid=(1,),
+            in_specs=[pl.BlockSpec((3, rows, width), lambda i, p: (0, 0, 0))] * n,
+            out_specs=[pl.BlockSpec((block, width), lambda i, p: (0, 0))] * PARTS,
+            scratch_shapes=[pltpu.VMEM((length, width), BF16)],
+        ),
+        out_shape=[jax.ShapeDtypeStruct((block, width), BF16)] * PARTS,
+        compiler_params=params(32),
+        cost_estimate=cost(
+            4 * length * length * width, 8 * length * width, length * length * width // HEAD_DIM
+        ),
+        name="attention_heads",
+    )(place, *pieces)
+
+
+def attention_grad_call(place, pieces, attention, d_terms):
+    n = len(pieces)
+    _, rows, width = pieces[0].shape
+    length = n * rows
+    block = length // PARTS
+    n_terms = len(d_terms)
+    scale = HEAD_DIM ** (-0.5)
+
+    def body(place_ref, *refs):
+        piece_refs, attn_refs = refs[:n], refs[n : n + PARTS]
+        term_refs = refs[n + PARTS : n + PARTS * (1 + n_terms)]
+        out_refs, (attn_held, d_held) = refs[n + PARTS * (1 + n_terms) : -2], refs[-2:]
+        places = slab_rows(place_ref[0], n, rows)
+        for i in range(PARTS):
+            here = slice(i * block, (i + 1) * block)
+            attn_held[here] = attn_refs[i][...]
+            terms = [term_refs[t * PARTS + i][...].astype(F32) for t in range(n_terms)]
+            d_held[here] = sum(terms).astype(BF16)
+        for lanes in head_lanes(width):
+            q, k, v = (
+                jnp.concatenate([r[t, :, lanes] for r in piece_refs], axis=0) for t in range(3)
+            )
+            attn = jnp.concatenate([attn_held[p, lanes] for p in places], axis=0).astype(F32)
+            d_attn = jnp.concatenate([d_held[p, lanes] for p in places], axis=0)
+            shifted, inverse = exponentials(q, k)
+            prob = shifted * inverse
+            delta = jnp.sum(d_attn.astype(F32) * attn, axis=1, keepdims=True).T
+            d_prob = dot(v, d_attn, ((1,), (1,)))
+            d_half = (prob * (d_prob - delta) * scale).astype(BF16)
+            grads = (
+                dot(k, d_half, ((0,), (0,))).T,
+                dot(d_half, q, ((1,), (0,))),
+                dot(prob.astype(BF16), d_attn, ((1,), (0,))),
+            )
+            for t in range(3):
+                g = grads[t].astype(BF16)
+                for s in range(n):
+                    out_refs[s][t, :, lanes] = g[s * rows : (s + 1) * rows]
+
+    piece = pl.BlockSpec((3, rows, width), lambda i, p: (0, 0, 0))
+    part = pl.BlockSpec((block, width), lambda i, p: (0, 0))
+    return pl.pallas_call(
+        body,
+        grid_spec=pltpu.PrefetchScalarGridSpec(
+            num_scalar_prefetch=1,
+            grid=(1,),
+            in_specs=[piece] * n + [part] * (PARTS * (1 + n_terms)),
+            out_specs=[piece] * n,
+            scratch_shapes=[pltpu.VMEM((length, width), BF16)] * 2,
+        ),
+        out_shape=[jax.ShapeDtypeStruct((3, rows, width), BF16)] * n,
+        compiler_params=params(32),
+        cost_estimate=cost(
+            10 * length * length * width, 24 * length * width, length * length * width // HEAD_DIM
+        ),
+        name="attention_heads_grad",
+    )(place, *pieces, *attention, *sum(d_terms, []))
+
+
+def ahead(place_ref, s, n):
+    me, core = place_ref[0], place_ref[1]
+    return lax.rem(jnp.where(core == 0, me + s, me + n - s), n)
+
+
+def position(place_ref, n):
+    return jnp.where(place_ref[1] == 0, place_ref[0], n - 1 - place_ref[0])
+
+
+def fetch_weight(shard_refs, held, sems, place_ref):
+    core, index = place_ref[1], place_ref[2]
+    own, one, two, own_o, one_o, two_o = shard_refs
+    first, second = jnp.where(core == 0, 2, 4), jnp.where(core == 0, 4, 2)
+    places = [
+        (own, 0),
+        (own_o, 1),
+        (one, first),
+        (one_o, second + 1),
+        (two.at[0], second),
+        (two_o.at[0], first + 1),
+        (two.at[1], 6),
+        (two_o.at[1], 7),
+    ]
+    for ref, step in places:
+        owner = index ^ step
+        pltpu.make_async_copy(ref, held.at[owner], sems.at[owner]).start()
+
+
+def wait_weight(shard_refs, held, sems, first, count):
+    for i in range(count):
+        pltpu.make_async_copy(shard_refs[0], held.at[first + i], sems.at[first + i]).wait()
+
+
+def fetch_heads(own, left, right, held, sems, pos, n):
+    size = own[0].shape[0]
+    for g in range(len(own)):
+        rows = pl.ds(g * size, size)
+        pltpu.make_async_copy(own[g], held.at[0, rows], sems.at[0, g]).start()
+        for s in range(1, n):
+
+            def copy(source, s=s, g=g, rows=rows):
+                pltpu.make_async_copy(source, held.at[s, rows], sems.at[s, g]).start()
+
+            @pl.when(pos + s < n)
+            def _():
+                copy(right[g][s - 1])
+
+            @pl.when(pos + s >= n)
+            def _():
+                copy(left[g][n - s - 1])
+
+
+def wait_heads(own, held, sems, s):
+    size = own[0].shape[0]
+    for g in range(len(own)):
+        pltpu.make_async_copy(own[g], held.at[s, pl.ds(g * size, size)], sems.at[s, g]).wait()
+
+
+def split_heads_refs(refs, groups, n):
+    own = refs[:groups]
+    rest = refs[groups : groups + 2 * groups * (n - 1)]
+    lists = [rest[i * (n - 1) : (i + 1) * (n - 1)] for i in range(2 * groups)]
+    return own, lists[:groups], lists[groups:]
+
+
+def gated(d_ref, gate_ref):
+    return (d_ref[...].astype(F32) * gate_ref[...]).astype(BF16)
+
+
+def d_attn_parts_call(place, grad_out, gate_row, shards, n):
+    length, cols = grad_out.shape
+    rows, n_shards = shards[0].shape[0], len(shards)
+    width = 2 * rows
+    dp, per, block = 2 * n, 2, length // PARTS
+
+    def body(place_ref, d_ref, gate_ref, *refs):
+        shard_refs, out_refs, (held, sems) = refs[:n_shards], refs[n_shards:-2], refs[-2:]
+        fetch_weight(shard_refs, held, sems, place_ref)
+        d_proj = gated(d_ref, gate_ref)
+        for s in (n - 1, *range(1, n - 1), 0):
+            first = ahead(place_ref, s, n) * per
+            wait_weight(shard_refs, held, sems, first, per)
+            part = dot(d_proj, held[pl.ds(first, per)].reshape(width, cols), ((1,), (1,)))
+            for g in range(PARTS):
+                out_refs[g * n + s][...] = part[g * block : (g + 1) * block].astype(BF16)
+
+    outs = pl.pallas_call(
+        body,
+        grid_spec=pltpu.PrefetchScalarGridSpec(
+            num_scalar_prefetch=1,
+            grid=(1,),
+            in_specs=[
+                pl.BlockSpec((length, cols), lambda i, p: (0, 0)),
+                pl.BlockSpec((1, cols), lambda i, p: (0, 0)),
+            ]
+            + any_specs(n_shards),
+            out_specs=[pl.BlockSpec((block, width), lambda i, p: (0, 0))] * (PARTS * n),
+            scratch_shapes=[pltpu.VMEM((dp, rows, cols), BF16), pltpu.SemaphoreType.DMA((dp,))],
+        ),
+        out_shape=[jax.ShapeDtypeStruct((block, width), BF16)] * (PARTS * n),
+        compiler_params=params(),
+        cost_estimate=cost(
+            2 * length * cols * width * n, 2 * (length * cols + n * width * (cols + length))
+        ),
+        name="d_attn_parts",
+    )(place, grad_out, gate_row, *shards)
+    return [outs[g * n : (g + 1) * n] for g in range(PARTS)]
+
+
+def heads_scratch(n, length, width):
+    return [pltpu.VMEM((n, length, width), BF16), pltpu.SemaphoreType.DMA((n, PARTS))]
+
+
+def projection_call(place, own, behind, front, shards, gate_row, n):
+    groups = len(own)
+    length, width = groups * own[0].shape[0], own[0].shape[1]
+    n_shards, (rows, cols) = len(shards), shards[0].shape
+    dp, per, count = n * width // rows, width // rows, groups * (2 * n - 1)
+
+    def body(place_ref, gate_ref, *refs):
+        heads = split_heads_refs(refs[:count], groups, n)
+        shard_refs = refs[count : count + n_shards]
+        out_ref, w_held, w_sems, held, sems = refs[count + n_shards :]
+        fetch_heads(*heads, held, sems, position(place_ref, n), n)
+        fetch_weight(shard_refs, w_held, w_sems, place_ref)
+        total = None
+        for s in range(n):
+            first = ahead(place_ref, s, n) * per
+            wait_heads(heads[0], held, sems, s)
+            wait_weight(shard_refs, w_held, w_sems, first, per)
+            block = w_held[pl.ds(first, per)].reshape(width, cols)
+            term = dot(held[s], block, ((1,), (0,)))
+            total = term if s == 0 else total + term
+        out_ref[...] = (total * gate_ref[...]).astype(BF16)
+
+    return pl.pallas_call(
+        body,
+        grid_spec=pltpu.PrefetchScalarGridSpec(
+            num_scalar_prefetch=1,
+            grid=(1,),
+            in_specs=[pl.BlockSpec((1, cols), lambda i, p: (0, 0))] + any_specs(count + n_shards),
+            out_specs=pl.BlockSpec((length, cols), lambda i, p: (0, 0)),
+            scratch_shapes=[
+                pltpu.VMEM((dp, rows, cols), BF16),
+                pltpu.SemaphoreType.DMA((dp,)),
+                pltpu.VMEM((n, length, width), BF16),
+                pltpu.SemaphoreType.DMA((n, groups)),
+            ],
+        ),
+        out_shape=jax.ShapeDtypeStruct((length, cols), BF16),
+        compiler_params=params(),
+        cost_estimate=cost(
+            2 * length * cols * width * n, 2 * (length * cols + n * width * (cols + length))
+        ),
+        name="projection",
+    )(place, gate_row, *own, *sum(behind, []), *sum(front, []), *shards)
+
+
+def weight_grad_call(place, steps, items, grad_out, gate_row, n, begun=None):
+    block, width = items[0][0][0].shape
+    length, cols = PARTS * block, grad_out.shape[1]
+    rows, many = width // 2, len(steps)
+
+    def body(place_ref, d_ref, gate_ref, *refs):
+        keep_ref, send_ref, d_proj, held, sems = refs[-5:]
+        i = pl.program_id(0)
+        pos = position(place_ref, n)
+
+        @pl.when(i == 0)
+        def _():
+            for j, s in enumerate(steps):
+                for g in range(PARTS):
+                    behind, front = refs[2 * (j * PARTS + g) : 2 * (j * PARTS + g) + 2]
+                    there = held.at[j, pl.ds(g * block, block)]
+
+                    @pl.when(pos + s < n)
+                    def _():
+                        pltpu.make_async_copy(front, there, sems.at[j, g]).start()
+
+                    @pl.when(pos + s >= n)
+                    def _():
+                        pltpu.make_async_copy(behind, there, sems.at[j, g]).start()
+
+            d_proj[...] = gated(d_ref, gate_ref)
+
+        for g in range(PARTS):
+            there = held.at[i, pl.ds(g * block, block)]
+            pltpu.make_async_copy(refs[0], there, sems.at[i, g]).wait()
+        term = dot(held[i], d_proj[...], ((0,), (0,))).astype(BF16)
+        first = place_ref[1] == 0
+        keep_ref[0] = jnp.where(first, term[:rows], term[rows:])
+        send_ref[0] = jnp.where(first, term[rows:], term[:rows])
+
+    def out_spec(other):
+        def slot(i, place):
+            s = sum(jnp.where(i == j, step, 0) for j, step in enumerate(steps))
+            chip = ahead(place, s, n) ^ (place[2] // 2)
+            x, y = chip % 2, chip // 2
+            return jnp.where((place[1] ^ other) == 0, 2 * x + y, 2 * y + x), 0, 0
+
+        return pl.BlockSpec((1, rows, cols), slot)
+
+    flat = [x for item in items for pair in item for x in pair]
+    begun = list(begun or ())
+    return pl.pallas_call(
+        body,
+        grid_spec=pltpu.PrefetchScalarGridSpec(
+            num_scalar_prefetch=1,
+            grid=(many,),
+            in_specs=[
+                pl.BlockSpec((length, cols), lambda s, p: (0, 0)),
+                pl.BlockSpec((1, cols), lambda s, p: (0, 0)),
+            ]
+            + any_specs(len(flat) + len(begun)),
+            out_specs=[out_spec(0), out_spec(1)],
+            scratch_shapes=[
+                pltpu.VMEM((length, cols), BF16),
+                pltpu.VMEM((many, length, width), BF16),
+                pltpu.SemaphoreType.DMA((many, PARTS)),
+            ],
+        ),
+        out_shape=[jax.ShapeDtypeStruct((n, rows, cols), BF16)] * 2,
+        input_output_aliases={3 + len(flat) + i: i for i in range(len(begun))},
+        compiler_params=params(),
+        cost_estimate=cost(
+            2 * length * cols * width * many,
+            2 * (length * cols + many * width * (cols + 2 * length)),
+        ),
+        name="weight_grad",
+    )(place, grad_out, gate_row, *flat, *begun)
+
+
+def assemble_call(place, pieces):
+    n = len(pieces)
+    _, rows, width = pieces[0].shape
+
+    def body(place_ref, *refs):
+        for t in range(3):
+            for s in range(n):
+                start = lax.rem(place_ref[0] + s, n) * width
+                lanes = pl.ds(pl.multiple_of(start, HEAD_DIM), width)
+                refs[n + t][:, lanes] = refs[s][t]
+
+    return pl.pallas_call(
+        body,
+        grid_spec=pltpu.PrefetchScalarGridSpec(
+            num_scalar_prefetch=1,
+            grid=(1,),
+            in_specs=[pl.BlockSpec((3, rows, width), lambda i, p: (0, 0, 0))] * n,
+            out_specs=[pl.BlockSpec((rows, n * width), lambda i, p: (0, 0))] * 3,
+        ),
+        out_shape=[jax.ShapeDtypeStruct((rows, n * width), BF16)] * 3,
+        compiler_params=params(32),
+        cost_estimate=cost(0, 12 * n * rows * width),
+        name="assemble_heads",
+    )(place, *pieces)
+
+
+def shift(x, axis, by):
+    n = lax.axis_size(axis)
+    return lax.ppermute(x, axis, [(i, (i + by) % n) for i in range(n)])
+
+
+def swap(x, axis, mask):
+    n = lax.axis_size(axis)
+    return lax.ppermute(x, axis, [(i, i ^ mask) for i in range(n)])
+
+
+def chip_swap(x, axis, step):
+    n = lax.axis_size(axis)
+    return lax.ppermute(x, axis, [(i, i ^ (2 if (i + step) % 2 == 0 else 4)) for i in range(n)])
+
+
+def line_move(x, dp_axis, axis, up):
+    n, dp = lax.axis_size(axis), lax.axis_size(dp_axis)
+    pairs = []
+    for g in range(dp):
+        for d in range(n - 1):
+            low, high = g * n + d, g * n + d + 1
+            pairs.append((low, high) if (g % 2 == 0) == up else (high, low))
+    return lax.ppermute(x, (dp_axis, axis), pairs)
+
+
+def line_payload(place, got, parts, t, n):
+    shape = got[0].shape
+
+    def body(place_ref, forward, back, part_f, part_b, out_f, out_b):
+        pos = position(place_ref, n)
+        for passes, x, part, out in (
+            (pos >= t, forward, part_f, out_f),
+            (n - 1 - pos >= t, back, part_b, out_b),
+        ):
+
+            @pl.when(passes)
+            def _():
+                out[...] = x[...]
+
+            @pl.when(jnp.logical_not(passes))
+            def _():
+                out[...] = add_rounded(part[...], x[...])
+
+    block = pl.BlockSpec(shape, lambda i, p: (0, 0))
+    return pl.pallas_call(
+        body,
+        grid_spec=pltpu.PrefetchScalarGridSpec(
+            num_scalar_prefetch=1, grid=(1,), in_specs=[block] * 4, out_specs=[block] * 2
+        ),
+        out_shape=[jax.ShapeDtypeStruct(shape, BF16)] * 2,
+        compiler_params=params(8),
+        cost_estimate=cost(0, 12 * got[0].size),
+        name="line_payload",
+    )(place, *got, parts[n - t], parts[t])
+
+
+def after(x, done):
+    return lax.optimization_barrier((x, done))[0]
+
+
+def by_heads(query, key_in, value, gate_table, timestep, out_weight, grad_out):
+    n, dp = lax.axis_size("ctx"), lax.axis_size("dp")
+    me = lax.axis_index("ctx").astype(jnp.int32)
+    index = lax.axis_index("dp").astype(jnp.int32)
+    place = jnp.stack([me, index % 2, index])
+    width = query.shape[2] // n
+    heads = width // HEAD_DIM
+    widths = [heads * HEAD_DIM]
+
+    packed = pack_call(place, query, key_in, value, n, widths)
+    pieces = [p[:1] + [shift(p[s], "ctx", s) for s in range(1, n)] for p in packed][0]
+    gate_row = lax.dynamic_slice_in_dim(gate_table, timestep[0], 1, 0)
+
+    one = after(chip_swap(after(out_weight, packed), "dp", 0), pieces[1])
+    two = chip_swap(jnp.stack([out_weight, one]), "dp", 1)
+    shards = after([out_weight, one, two], pieces)
+    shards = shards + [swap(x, "dp", 1) for x in shards]
+    parts = d_attn_parts_call(place, grad_out[0], gate_row, shards, n)
+    attention = attention_call(place, pieces)
+
+    def both_ways(forward, back):
+        return line_move(forward, "dp", "ctx", True), line_move(back, "dp", "ctx", False)
+
+    def items(s):
+        if s == 0:
+            return [(a, a) for a in attention]
+        return [(got[g][n - s - 1][0], got[g][s - 1][1]) for g in range(PARTS)]
+
+    got = [[both_ways(a, a)] for a in attention]
+    begun = None
+    for t in range(1, n):
+        sent = [line_payload(place, got[g][-1], parts[g], t, n) for g in range(PARTS)]
+        for g in range(PARTS):
+            got[g].append(both_ways(*sent[g]))
+        if t > 1:
+            steps = [s for s in range(n) if max(s, n - s) <= t and max(s, n - s) > t - 1]
+            steps = [0] * (t == 2) + steps
+            begun = weight_grad_call(
+                place, steps, [items(s) for s in steps], grad_out[0], gate_row, n, begun
+            )
+    keep, send = begun
+    received = swap(send, "dp", 1)
+    behind = [[got[g][i][0] for i in range(n - 1)] for g in range(PARTS)]
+    front = [[got[g][i][1] for i in range(n - 1)] for g in range(PARTS)]
+    d_terms = [[parts[g][0] for g in range(PARTS)]]
+    d_terms += [[got[g][-1][i] for g in range(PARTS)] for i in range(2)]
+
+    far = add_rounded(keep[2:], received[2:])
+    grads = attention_grad_call(place, pieces, attention, after(d_terms, far))
+    grads = [grads[0]] + [shift(grads[s], "ctx", -s) for s in range(1, n)]
+    far = after(chip_swap(far, "dp", 0), grads[n // 2])
+    near = keep[:2].astype(F32) + received[:2].astype(F32) + far.astype(F32)
+    grad_weight = near[0] + chip_swap(near[1].astype(BF16), "dp", 1).astype(F32)
+
+    gate_row = after(gate_row, near)
+    branch_out = projection_call(place, attention, behind, front, shards, gate_row, n)[None]
+    grad_query, grad_key, grad_value = assemble_call(place, after(grads, grad_weight))
+    return (branch_out, grad_query[None], grad_key[None], grad_value[None], grad_weight)
+
+
+def by_tokens(query, key_in, value, gate_table, timestep, out_weight, grad_out):
     slab_rows = query.shape[1]
     attn_width = query.shape[2]
     head_count = attn_width // HEAD_DIM
@@ -94,6 +648,15 @@
     return (branch_out, grad_query[None], grad_key[None], grad_value[None], grad_weight)
 
 
+def on_device(query, key_in, value, gate_table, timestep, out_weight, grad_out):
+    n, dp = lax.axis_size("ctx"), lax.axis_size("dp")
+    heads = query.shape[2] // HEAD_DIM
+    fits = heads % n == 0 and dp == 8 and dp == 2 * n
+    fits = fits and out_weight.shape[0] * dp == query.shape[2]
+    plan = by_heads if fits else by_tokens
+    return plan(query, key_in, value, gate_table, timestep, out_weight, grad_out)
+
+
 def solution(mesh):
     in_specs = (
         P("dp", "ctx", None),

time: 456 us -> 214 us (0.47)
  waiting for transfers between devices: 355 us -> 91 us
  starting transfers between devices: 0.46 us -> 62.4 us
  matrix products: 51.2 us -> 0 us
  Pallas kernels: 0 us -> 42.1 us
  between operations: 14.9 us -> 1.73 us
  local copies, waits for them, and re-layouts: 22.8 us -> 12 us
  other arithmetic: 10.4 us -> 3.61 us
    reduce_scatter x3 -> x0, waiting for transfers between devices: 180 us -> none  [the longest x1 72.4 us: on_device(): lax.psum_scatter(jnp.concatenate([key_part, value_part], axis=1).astype(j...]
    all_gather x4 -> x0, waiting for transfers between devices: 173 us -> none  [the longest x1 51.4 us: on_device(): lax.all_gather(key_in, 'ctx', axis=1, tiled=True)]
    ppermute x0 -> x30, waiting for transfers between devices: none -> 91 us  [the longest x6 68.8 us: shift(): return lax.ppermute(x, axis, [(i, (i + by) % n) for i in range(n)])]
    ppermute x0 -> x30, starting transfers between devices: none -> 62.4 us  [the longest x16 50.5 us: line_move(): return lax.ppermute(x, (dp_axis, axis), pairs)]
    dot_general x9 -> x0, matrix products: 45.3 us -> none  [the longest x1 8.34 us: on_device(): jnp.dot(columns, lax.all_gather(out_weight, 'dp', axis=0, tiled=True), pr...]
    pallas_call x0 -> x14, Pallas kernels: none -> 42.1 us  [the longest x1 9.7 us: projection_call(): pl.pallas_call(body, grid_spec=pltpu.PrefetchScalarGridSpec(num_scalar_pr...]
    reshape x2 -> x0, local copies, waits for them, and re-layouts: 7.46 us -> none  [the longest x1 4.47 us: on_device(): key_part = jnp.einsum('hqk,qhd->khd', d_half, query_heads, preferred_elem...]
    sub x1 -> x0, matrix products: 5.9 us -> none  [on_device(): exp_scores = jnp.exp(scores - row_max)]
  transfers between devices with their start and end apart: 7 -> 30, of which waited for: 7 -> 13; matrix products, arithmetic and copies ran while one was open for 16% -> 1% of each run, Pallas kernels for 0% -> 17%
where the time goes in v2:
time: 214 us; the launch traced here: 213 us
  waiting for transfers between devices  91 us (43%)
  starting transfers between devices  62.4 us (29%)
  Pallas kernels  42.1 us (20%)
  local copies, waits for them, and re-layouts  12 us (6%)
  other arithmetic  3.61 us (2%)
    ppermute x6, waiting for transfers between devices, shift(): return lax.ppermute(x, axis, [(i, (i + by) % n) for i in range(n)])  68.8 us
    ppermute x16, starting transfers between devices, line_move(): return lax.ppermute(x, (dp_axis, axis), pairs)  50.5 us
    ppermute x16, waiting for transfers between devices, line_move(): return lax.ppermute(x, (dp_axis, axis), pairs)  16.4 us
    unnamed x36, local copies, waits for them, and re-layouts  11.1 us
    pallas_call x1, Pallas kernels, projection_call(): pl.pallas_call(body, grid_spec=pltpu.PrefetchScalarGridSpec(num_scalar_pr...  9.7 us
    pallas_call x1, Pallas kernels, d_attn_parts_call(): pl.pallas_call(body, grid_spec=pltpu.PrefetchScalarGridSpec(num_scalar_pr...  8.82 us
    ppermute x6, starting transfers between devices, shift(): return lax.ppermute(x, axis, [(i, (i + by) % n) for i in range(n)])  7.15 us
    pallas_call x2, Pallas kernels, weight_grad_call(): pl.pallas_call(body, grid_spec=pltpu.PrefetchScalarGridSpec(num_scalar_pr...  6.96 us
  transfers between devices with their start and end apart: 30, of which 13 were waited for; matrix products, arithmetic and copies ran while one was open for 1% of the time, Pallas kernels for 17%

profile of v2, /device:TPU:0, one launch (start us, length us, event | category | flops | bytes accessed | tf_op | source)
XLA Modules:
  0.0 212.9 jit_solution(18216304685288475725)
XLA Ops:
  5.2 3.0 %collective-permute-start.5 = (bf16[320,1280]{1,0:T(8,128)(2,1)}, bf16[320,1280]{1,0:T(8,128)(2,1)S(1)}, u32[]{:S(2)}, u32[]{:S(2)}) collective-permute-start(bf16[320,1280]{1,0:T(8,128)(2,1)} %refs_14_), channel_id=1, source_target_pairs={{0,8},{4,20},{8,0},{12,28},{16,24},{20,4},{24,16},{28,12},{1,9},{5... | collective-permute-start | bytes 2457608 | tf_op jit(solution)/shard_map/ppermute | solution.py:455
  9.8 13.0 %collective-permute-done.refs_1_ = bf16[3,128,640]{2,1,0:T(8,128)(2,1)S(1)} collective-permute-done((bf16[3,128,640]{2,1,0:T(8,128)(2,1)S(1)}, bf16[3,128,640]{2,1,0:T(8,128)(2,1)S(1)}, u32[]{:S(2)}, u32[]{:S(2)}) %collective-permute-start) | collective-permute-done | bytes 491552 | tf_op jit(solution)/shard_map/ppermute | solution.py:445
  27.5 22.2 %collective-permute-done.1.refs_2_ = bf16[3,128,640]{2,1,0:T(8,128)(2,1)S(1)} collective-permute-done((bf16[3,128,640]{2,1,0:T(8,128)(2,1)S(1)}, bf16[3,128,640]{2,1,0:T(8,128)(2,1)S(1)}, u32[]{:S(2)}, u32[]{:S(2)}) %collective-permute-start.1) | collective-permute-done | bytes 491552 | tf_op jit(solution)/shard_map/ppermute | solution.py:445
  56.7 3.4 %attention_heads.1 = (bf16[256,640]{1,0:T(8,128)(2,1)S(1)}, bf16[256,640]{1,0:T(8,128)(2,1)S(1)}) custom-call(s32[3]{0:T(128)S(1)} %pad_add_fusion.place_ref, bf16[3,128,640]{2,1,0:T(8,128)(2,1)S(1)} %copy-done.7, bf16[3,128,640]{2,1,0:T(8,128)(2,1)S(1)} %copy-done.10, bf16[3,128,640]{2,1,0:T(8,128)(2,1)S(1)} %copy-done.13, bf16[3,128,640]{2,1,0:T(8,128)(2,1)S(1)} %copy-done.16), custom_call_target="tpu_custom_call" | custom-call | flops 671088640 | bytes 2621440 | tf_op jit(solution)/shard_map/attention_heads/pallas_call | solution.py:108
  61.4 12.8 %collective-permute-start.3 = (bf16[256,640]{1,0:T(8,128)(2,1)S(1)}, bf16[256,640]{1,0:T(8,128)(2,1)S(1)}, u32[]{:S(2)}, u32[]{:S(2)}) collective-permute-start(bf16[256,640]{1,0:T(8,128)(2,1)S(1)} %get-tuple-element.63.refs_0_.refs_1_.refs_4_), channel_id=1, source_target_pairs={{0,1},{1,2},{2,3},{5,4},{6,5},{7,6},{8,9},{9,10},{10,11},{13,12},{... | collective-permute-start | bytes 983048 | tf_op jit(solution)/shard_map/ppermute | solution.py:465
  75.6 4.6 %collective-permute-start.13 = (bf16[256,640]{1,0:T(8,128)(2,1)S(1)}, bf16[256,640]{1,0:T(8,128)(2,1)S(1)}, u32[]{:S(2)}, u32[]{:S(2)}) collective-permute-start(bf16[256,640]{1,0:T(8,128)(2,1)S(1)} %get-tuple-element.75.refs_2_.refs_3_.refs_5_.refs_1_), channel_id=1, source_target_pairs={{0,1},{1,2},{2,3},{5,4},{6,5},{7,6},{8,9},{9,10},{10,11},{13,12},{... | collective-permute-start | bytes 983048 | tf_op jit(solution)/shard_map/ppermute | solution.py:465
  82.3 8.8 %d_attn_parts.1 = (bf16[256,640]{1,0:T(8,128)(2,1)S(1)}, bf16[256,640]{1,0:T(8,128)(2,1)S(1)}, bf16[256,640]{1,0:T(8,128)(2,1)S(1)}, bf16[256,640]{1,0:T(8,128)(...) custom-call(s32[3]{0:T(128)S(1)} %pad_add_fusion.place_ref, ...), custom_call_target="tpu_custom_call" | custom-call | flops 3355443200 | bytes 10485760 | tf_op jit(solution)/shard_map/d_attn_parts/pallas_call | solution.py:271
  91.8 3.0 %collective-permute-start.10 = (bf16[256,640]{1,0:T(8,128)(2,1)S(1)}, bf16[256,640]{1,0:T(8,128)(2,1)S(1)}, u32[]{:S(2)}, u32[]{:S(2)}) collective-permute-start(bf16[256,640]{1,0:T(8,128)(2,1)S(1)} %get-tuple-element.71), channel_id=1, source_target_pairs={{0,1},{1,2},{2,3},{5,4},{6,5},{7,6},{8,9},{9,10},{10,11},{13,12},{... | collective-permute-start | bytes 983048 | tf_op jit(solution)/shard_map/ppermute | solution.py:465
  96.9 4.5 %collective-permute-start.15 = (bf16[256,640]{1,0:T(8,128)(2,1)S(1)}, bf16[256,640]{1,0:T(8,128)(2,1)S(1)}, u32[]{:S(2)}, u32[]{:S(2)}) collective-permute-start(bf16[256,640]{1,0:T(8,128)(2,1)S(1)} %get-tuple-element.78), channel_id=1, source_target_pairs={{0,1},{1,2},{2,3},{5,4},{6,5},{7,6},{8,9},{9,10},{10,11},{13,12},{... | collective-permute-start | bytes 983048 | tf_op jit(solution)/shard_map/ppermute | solution.py:465
  102.7 2.9 %collective-permute-done.11.back.refs_5_.refs_9_ = bf16[256,640]{1,0:T(8,128)(2,1)S(1)} collective-permute-done((bf16[256,640]{1,0:T(8,128)(2,1)S(1)}, bf16[256,640]{1,0:T(8,128)(2,1)S(1)}, u32[]{:S(2)}, u32[]{:S(2)}) %collective-permute-start.11) | collective-permute-done | bytes 327712 | tf_op jit(solution)/shard_map/ppermute | solution.py:465
  106.2 3.5 %collective-permute-start.12 = (bf16[256,640]{1,0:T(8,128)(2,1)S(1)}, bf16[256,640]{1,0:T(8,128)(2,1)S(1)}, u32[]{:S(2)}, u32[]{:S(2)}) collective-permute-start(bf16[256,640]{1,0:T(8,128)(2,1)S(1)} %get-tuple-element.74), channel_id=1, source_target_pairs={{0,1},{1,2},{2,3},{5,4},{6,5},{7,6},{8,9},{9,10},{10,11},{13,12},{... | collective-permute-start | bytes 983048 | tf_op jit(solution)/shard_map/ppermute | solution.py:465
  112.9 3.6 %collective-permute-start.17 = (bf16[256,640]{1,0:T(8,128)(2,1)S(1)}, bf16[256,640]{1,0:T(8,128)(2,1)S(1)}, u32[]{:S(2)}, u32[]{:S(2)}) collective-permute-start(bf16[256,640]{1,0:T(8,128)(2,1)S(1)} %get-tuple-element.81), channel_id=1, source_target_pairs={{0,1},{1,2},{2,3},{5,4},{6,5},{7,6},{8,9},{9,10},{10,11},{13,12},{... | collective-permute-start | bytes 983048 | tf_op jit(solution)/shard_map/ppermute | solution.py:465
  118.0 3.5 %weight_grad.2 = (bf16[4,320,1280]{2,1,0:T(8,128)(2,1)S(1)}, bf16[4,320,1280]{2,1,0:T(8,128)(2,1)S(1)}) custom-call(s32[3]{0:T(128)S(1)} %pad_add_fusion.place_ref, bf16[512,1280]{1,0:T(8,128)(2,1)S(1)} %bitcast.23, f32[1,1280]{1,0:T(1,128)S(1)} %constant_dynamic-slice_fusion.gate_ref, bf16[256,640]{1,0:T(8,128)(2,1)S(1)} %get-tuple-element.63.refs_0_.refs_1_.refs_4_, ...), custom_call_target="tpu_custom_call" | custom-call | flops 1677721600 | bytes 7208960 | tf_op jit(solution)/shard_map/weight_grad/pallas_call | solution.py:389
  121.5 3.1 %collective-permute-done.17.refs_2_.forward.refs_7_ = bf16[256,640]{1,0:T(8,128)(2,1)S(1)} collective-permute-done((bf16[256,640]{1,0:T(8,128)(2,1)S(1)}, bf16[256,640]{1,0:T(8,128)(2,1)S(1)}, u32[]{:S(2)}, u32[]{:S(2)}) %collective-permute-start.17) | collective-permute-done | bytes 327712 | tf_op jit(solution)/shard_map/ppermute | solution.py:465
  125.7 3.5 %weight_grad.3 = (bf16[4,320,1280]{2,1,0:T(8,128)(2,1)S(1)}, bf16[4,320,1280]{2,1,0:T(8,128)(2,1)S(1)}) custom-call(s32[3]{0:T(128)S(1)} %pad_add_fusion.place_ref, bf16[512,1280]{1,0:T(8,128)(2,1)S(1)} %bitcast.24, f32[1,1280]{1,0:T(1,128)S(1)} %constant_dynamic-slice_fusion.gate_ref, ...), custom_call_target="tpu_custom_call", output_to_operand_aliasing={{0}: (11, {}), {1}: (12, {})} | custom-call | flops 1677721600 | bytes 7208960 | tf_op jit(solution)/shard_map/weight_grad/pallas_call | solution.py:389
  129.3 5.8 %collective-permute-done.20 = bf16[4,320,1280]{2,1,0:T(8,128)(2,1)S(1)} collective-permute-done((bf16[4,320,1280]{2,1,0:T(8,128)(2,1)S(1)}, bf16[4,320,1280]{2,1,0:T(8,128)(2,1)S(1)}, u32[]{:S(2)}, u32[]{:S(2)}) %collective-permute-start.20) | collective-permute-done | bytes 3276832 | tf_op jit(solution)/shard_map/ppermute | solution.py:450
  136.3 3.3 %collective-permute-start.22 = (bf16[256,640]{1,0:T(8,128)(2,1)S(1)}, bf16[256,640]{1,0:T(8,128)(2,1)S(1)}, u32[]{:S(2)}, u32[]{:S(2)}) collective-permute-start(bf16[256,640]{1,0:T(8,128)(2,1)S(1)} %get-tuple-element.90), channel_id=1, source_target_pairs={{0,1},{1,2},{2,3},{5,4},{6,5},{7,6},{8,9},{9,10},{10,11},{13,12},{... | collective-permute-start | bytes 983048 | tf_op jit(solution)/shard_map/ppermute | solution.py:465
  141.6 4.6 %collective-permute-start.23 = (bf16[256,640]{1,0:T(8,128)(2,1)S(1)}, bf16[256,640]{1,0:T(8,128)(2,1)S(1)}, u32[]{:S(2)}, u32[]{:S(2)}) collective-permute-start(bf16[256,640]{1,0:T(8,128)(2,1)S(1)} %get-tuple-element.91), channel_id=1, source_target_pairs={{0,1},{1,2},{2,3},{5,4},{6,5},{7,6},{8,9},{9,10},{10,11},{13,12},{... | collective-permute-start | bytes 983048 | tf_op jit(solution)/shard_map/ppermute | solution.py:465
  147.6 2.6 %collective-permute-done.24.refs_10_ = bf16[256,640]{1,0:T(8,128)(2,1)S(1)} collective-permute-done((bf16[256,640]{1,0:T(8,128)(2,1)S(1)}, bf16[256,640]{1,0:T(8,128)(2,1)S(1)}, u32[]{:S(2)}, u32[]{:S(2)}) %collective-permute-start.24) | collective-permute-done | bytes 327712 | tf_op jit(solution)/shard_map/ppermute | solution.py:465
  150.2 4.1 %collective-permute-done.23.refs_9_ = bf16[256,640]{1,0:T(8,128)(2,1)S(1)} collective-permute-done((bf16[256,640]{1,0:T(8,128)(2,1)S(1)}, bf16[256,640]{1,0:T(8,128)(2,1)S(1)}, u32[]{:S(2)}, u32[]{:S(2)}) %collective-permute-start.23) | collective-permute-done | bytes 327712 | tf_op jit(solution)/shard_map/ppermute | solution.py:465
  155.7 6.1 %attention_heads_grad.1 = (bf16[3,128,640]{2,1,0:T(8,128)(2,1)S(1)}, bf16[3,128,640]{2,1,0:T(8,128)(2,1)S(1)}, bf16[3,128,640]{2,1,0:T(8,128)(2,1)S(1)}, bf16[3,128,640]{2,1,0:T(8,128)(2,1)S(1)}) custom-call(s32[3]{0:T(128)S(1)} %pad_add_fusion.place_ref, bf16[3,128,640]{2,1,0:T(8,128)(2,1)S(1)} %copy-done.8, bf16[3,128,640]{2,1,0:T(8,128)(2,1)S(1)} %copy-done.11, ...), custom_call_target="tpu_custom_call" | custom-call | flops 1677721600 | bytes 7864320 | tf_op jit(solution)/shard_map/attention_heads_grad/pallas_call | solution.py:167
  162.8 22.8 %collective-permute-done.26.refs_2_ = bf16[3,128,640]{2,1,0:T(8,128)(2,1)S(1)} collective-permute-done((bf16[3,128,640]{2,1,0:T(8,128)(2,1)S(1)}, bf16[3,128,640]{2,1,0:T(8,128)(2,1)S(1)}, u32[]{:S(2)}, u32[]{:S(2)}) %collective-permute-start.26) | collective-permute-done | bytes 491552 | tf_op jit(solution)/shard_map/ppermute | solution.py:445
  189.2 9.7 %projection.1 = bf16[512,1280]{1,0:T(8,128)(2,1)} custom-call(s32[3]{0:T(128)S(1)} %pad_add_fusion.place_ref, f32[1,1280]{1,0:T(1,128)S(1)} %constant_dynamic-slice_fusion.gate_ref, bf16[256,640]{1,0:T(8,128)(2,1)S(1)} %get-tuple-element.63.refs_0_.refs_1_.refs_4_, bf16[256,640]{1,0:T(8,128)(2,1)S(1)} %get-tuple-element.75.refs_2_.refs_3_.refs_5_.refs_1_, ...), custom_call_target="tpu_custom_call" | custom-call | flops 3355443200 | bytes 10485760 | tf_op jit(solution)/shard_map/projection/pallas_call | solution.py:320
  200.8 10.1 %collective-permute-done.28.refs_3_ = bf16[3,128,640]{2,1,0:T(8,128)(2,1)S(1)} collective-permute-done((bf16[3,128,640]{2,1,0:T(8,128)(2,1)S(1)}, bf16[3,128,640]{2,1,0:T(8,128)(2,1)S(1)}, u32[]{:S(2)}, u32[]{:S(2)}) %collective-permute-start.28) | collective-permute-done | bytes 491552 | tf_op jit(solution)/shard_map/ppermute | solution.py:445
  (93 shorter events, 46.5 us)
Async XLA Ops:
  5.2 18.4 %collective-permute-start.5 = (bf16[320,1280]{1,0:T(8,128)(2,1)}, bf16[320,1280]{1,0:T(8,128)(2,1)S(1)}, u32[]{:S(2)}, u32[]{:S(2)}) collective-permute-start(bf16[320,1280]{1,0:T(8,128)(2,1)} %refs_14_), channel_id=1, source_target_pairs={{0,8},{4,20},{8,0},{12,28},{16,24},{20,4},{24,16},{28,12},{1,9},{5... | collective-permute-start | bytes 2457608 | tf_op jit(solution)/shard_map/ppermute | solution.py:455
  8.2 14.6 %collective-permute-start = (bf16[3,128,640]{2,1,0:T(8,128)(2,1)S(1)}, bf16[3,128,640]{2,1,0:T(8,128)(2,1)S(1)}, u32[]{:S(2)}, u32[]{:S(2)}) collective-permute-start(bf16[3,128,640]{2,1,0:T(8,128)(2,1)S(1)} %get-tuple-element.60), channel_id=1, source_target_pairs={{0,1},{1,2},{2,3},{3,0},{4,5},{5,6},{6,7},{7,4},{8,9},{9,10},{10,1... | collective-permute-start | bytes 1474568 | tf_op jit(solution)/shard_map/ppermute | solution.py:445
  24.9 26.4 %collective-permute-start.6 = (bf16[2,320,1280]{2,1,0:T(8,128)(2,1)S(1)}, bf16[2,320,1280]{2,1,0:T(8,128)(2,1)S(1)}, u32[]{:S(2)}, u32[]{:S(2)}) collective-permute-start(bf16[2,320,1280]{2,1,0:T(8,128)(2,1)S(1)} %pad_maximum_fusion), channel_id=1, source_target_pairs={{0,16},{4,12},{8,24},{12,4},{16,0},{20,28},{24,8},{28,20},{1,17},{... | collective-permute-start | bytes 4915208 | tf_op jit(solution)/shard_map/ppermute | solution.py:455
  25.5 24.3 %collective-permute-start.1 = (bf16[3,128,640]{2,1,0:T(8,128)(2,1)S(1)}, bf16[3,128,640]{2,1,0:T(8,128)(2,1)S(1)}, u32[]{:S(2)}, u32[]{:S(2)}) collective-permute-start(bf16[3,128,640]{2,1,0:T(8,128)(2,1)S(1)} %get-tuple-element.61), channel_id=1, source_target_pairs={{0,2},{1,3},{2,0},{3,1},{4,6},{5,7},{6,4},{7,5},{8,10},{9,11},{10,... | collective-permute-start | bytes 1474568 | tf_op jit(solution)/shard_map/ppermute | solution.py:445
  26.2 24.3 %collective-permute-start.2 = (bf16[3,128,640]{2,1,0:T(8,128)(2,1)S(1)}, bf16[3,128,640]{2,1,0:T(8,128)(2,1)S(1)}, u32[]{:S(2)}, u32[]{:S(2)}) collective-permute-start(bf16[3,128,640]{2,1,0:T(8,128)(2,1)S(1)} %get-tuple-element.62), channel_id=1, source_target_pairs={{0,3},{1,0},{2,1},{3,2},{4,7},{5,4},{6,5},{7,6},{8,11},{9,8},{10,9... | collective-permute-start | bytes 1474568 | tf_op jit(solution)/shard_map/ppermute | solution.py:445
  51.3 29.6 %collective-permute-start.9 = (bf16[2,320,1280]{2,1,0:T(8,128)(2,1)S(1)}, bf16[2,320,1280]{2,1,0:T(8,128)(2,1)}, u32[]{:S(2)}, u32[]{:S(2)}) collective-permute-start(bf16[2,320,1280]{2,1,0:T(8,128)(2,1)S(1)} %collective-permute-done.6.refs_2_.refs_16_), channel_id=1, source_target_pairs={{0,4},{4,0},{8,12},{12,8},{16,20},{20,16},{24,28},{28,24},{1,5},{5... | collective-permute-start | bytes 4915208 | tf_op jit(solution)/shard_map/ppermute | solution.py:450
  51.4 22.9 %collective-permute-start.7 = (bf16[320,1280]{1,0:T(8,128)(2,1)S(1)}, bf16[320,1280]{1,0:T(8,128)(2,1)}, u32[]{:S(2)}, u32[]{:S(2)}) collective-permute-start(bf16[320,1280]{1,0:T(8,128)(2,1)S(1)} %copy-done), channel_id=1, source_target_pairs={{0,4},{4,0},{8,12},{12,8},{16,20},{20,16},{24,28},{28,24},{1,5},{5... | collective-permute-start | bytes 2457608 | tf_op jit(solution)/shard_map/ppermute | solution.py:450
  51.8 23.7 %collective-permute-start.8 = (bf16[320,1280]{1,0:T(8,128)(2,1)S(1)}, bf16[320,1280]{1,0:T(8,128)(2,1)}, u32[]{:S(2)}, u32[]{:S(2)}) collective-permute-start(bf16[320,1280]{1,0:T(8,128)(2,1)S(1)} %collective-permute-done.5.refs_1_.refs_15_), channel_id=1, source_target_pairs={{0,4},{4,0},{8,12},{12,8},{16,20},{20,16},{24,28},{28,24},{1,5},{5... | collective-permute-start | bytes 2457608 | tf_op jit(solution)/shard_map/ppermute | solution.py:450
  60.1 31.0 %collective-permute-start.4 = (bf16[256,640]{1,0:T(8,128)(2,1)S(1)}, bf16[256,640]{1,0:T(8,128)(2,1)S(1)}, u32[]{:S(2)}, u32[]{:S(2)}) collective-permute-start(bf16[256,640]{1,0:T(8,128)(2,1)S(1)} %get-tuple-element.63.refs_0_.refs_1_.refs_4_), channel_id=1, source_target_pairs={{1,0},{2,1},{3,2},{4,5},{5,6},{6,7},{9,8},{10,9},{11,10},{12,13},{... | collective-permute-start | bytes 983048 | tf_op jit(solution)/shard_map/ppermute | solution.py:465
  61.4 29.7 %collective-permute-start.3 = (bf16[256,640]{1,0:T(8,128)(2,1)S(1)}, bf16[256,640]{1,0:T(8,128)(2,1)S(1)}, u32[]{:S(2)}, u32[]{:S(2)}) collective-permute-start(bf16[256,640]{1,0:T(8,128)(2,1)S(1)} %get-tuple-element.63.refs_0_.refs_1_.refs_4_), channel_id=1, source_target_pairs={{0,1},{1,2},{2,3},{5,4},{6,5},{7,6},{8,9},{9,10},{10,11},{13,12},{... | collective-permute-start | bytes 983048 | tf_op jit(solution)/shard_map/ppermute | solution.py:465
  74.3 21.9 %collective-permute-start.14 = (bf16[256,640]{1,0:T(8,128)(2,1)S(1)}, bf16[256,640]{1,0:T(8,128)(2,1)S(1)}, u32[]{:S(2)}, u32[]{:S(2)}) collective-permute-start(bf16[256,640]{1,0:T(8,128)(2,1)S(1)} %get-tuple-element.75.refs_2_.refs_3_.refs_5_.refs_1_), channel_id=1, source_target_pairs={{1,0},{2,1},{3,2},{4,5},{5,6},{6,7},{9,8},{10,9},{11,10},{12,13},{... | collective-permute-start | bytes 983048 | tf_op jit(solution)/shard_map/ppermute | solution.py:465
  75.6 20.6 %collective-permute-start.13 = (bf16[256,640]{1,0:T(8,128)(2,1)S(1)}, bf16[256,640]{1,0:T(8,128)(2,1)S(1)}, u32[]{:S(2)}, u32[]{:S(2)}) collective-permute-start(bf16[256,640]{1,0:T(8,128)(2,1)S(1)} %get-tuple-element.75.refs_2_.refs_3_.refs_5_.refs_1_), channel_id=1, source_target_pairs={{0,1},{1,2},{2,3},{5,4},{6,5},{7,6},{8,9},{9,10},{10,11},{13,12},{... | collective-permute-start | bytes 983048 | tf_op jit(solution)/shard_map/ppermute | solution.py:465
  96.9 14.2 %collective-permute-start.15 = (bf16[256,640]{1,0:T(8,128)(2,1)S(1)}, bf16[256,640]{1,0:T(8,128)(2,1)S(1)}, u32[]{:S(2)}, u32[]{:S(2)}) collective-permute-start(bf16[256,640]{1,0:T(8,128)(2,1)S(1)} %get-tuple-element.78), channel_id=1, source_target_pairs={{0,1},{1,2},{2,3},{5,4},{6,5},{7,6},{8,9},{9,10},{10,11},{13,12},{... | collective-permute-start | bytes 983048 | tf_op jit(solution)/shard_map/ppermute | solution.py:465
  101.4 10.9 %collective-permute-start.16 = (bf16[256,640]{1,0:T(8,128)(2,1)S(1)}, bf16[256,640]{1,0:T(8,128)(2,1)S(1)}, u32[]{:S(2)}, u32[]{:S(2)}) collective-permute-start(bf16[256,640]{1,0:T(8,128)(2,1)S(1)} %get-tuple-element.79), channel_id=1, source_target_pairs={{1,0},{2,1},{3,2},{4,5},{5,6},{6,7},{9,8},{10,9},{11,10},{12,13},{... | collective-permute-start | bytes 983048 | tf_op jit(solution)/shard_map/ppermute | solution.py:465
  106.2 15.3 %collective-permute-start.12 = (bf16[256,640]{1,0:T(8,128)(2,1)S(1)}, bf16[256,640]{1,0:T(8,128)(2,1)S(1)}, u32[]{:S(2)}, u32[]{:S(2)}) collective-permute-start(bf16[256,640]{1,0:T(8,128)(2,1)S(1)} %get-tuple-element.74), channel_id=1, source_target_pairs={{0,1},{1,2},{2,3},{5,4},{6,5},{7,6},{8,9},{9,10},{10,11},{13,12},{... | collective-permute-start | bytes 983048 | tf_op jit(solution)/shard_map/ppermute | solution.py:465
  109.8 11.8 %collective-permute-start.18 = (bf16[256,640]{1,0:T(8,128)(2,1)S(1)}, bf16[256,640]{1,0:T(8,128)(2,1)S(1)}, u32[]{:S(2)}, u32[]{:S(2)}) collective-permute-start(bf16[256,640]{1,0:T(8,128)(2,1)S(1)} %get-tuple-element.82), channel_id=1, source_target_pairs={{1,0},{2,1},{3,2},{4,5},{5,6},{6,7},{9,8},{10,9},{11,10},{12,13},{... | collective-permute-start | bytes 983048 | tf_op jit(solution)/shard_map/ppermute | solution.py:465
  112.9 11.7 %collective-permute-start.17 = (bf16[256,640]{1,0:T(8,128)(2,1)S(1)}, bf16[256,640]{1,0:T(8,128)(2,1)S(1)}, u32[]{:S(2)}, u32[]{:S(2)}) collective-permute-start(bf16[256,640]{1,0:T(8,128)(2,1)S(1)} %get-tuple-element.81), channel_id=1, source_target_pairs={{0,1},{1,2},{2,3},{5,4},{6,5},{7,6},{8,9},{9,10},{10,11},{13,12},{... | collective-permute-start | bytes 983048 | tf_op jit(solution)/shard_map/ppermute | solution.py:465
  135.6 50.1 %collective-permute-start.21 = (bf16[2,320,1280]{2,1,0:T(8,128)(2,1)S(1)}, bf16[2,320,1280]{2,1,0:T(8,128)(2,1)S(1)}, u32[]{:S(2)}, u32[]{:S(2)}) collective-permute-start(bf16[2,320,1280]{2,1,0:T(8,128)(2,1)S(1)} %add_convert_fusion), channel_id=1, source_target_pairs={{0,8},{4,20},{8,0},{12,28},{16,24},{20,4},{24,16},{28,12},{1,9},{5... | collective-permute-start | bytes 4915208 | tf_op jit(solution)/shard_map/ppermute | solution.py:455
  136.3 11.2 %collective-permute-start.22 = (bf16[256,640]{1,0:T(8,128)(2,1)S(1)}, bf16[256,640]{1,0:T(8,128)(2,1)S(1)}, u32[]{:S(2)}, u32[]{:S(2)}) collective-permute-start(bf16[256,640]{1,0:T(8,128)(2,1)S(1)} %get-tuple-element.90), channel_id=1, source_target_pairs={{0,1},{1,2},{2,3},{5,4},{6,5},{7,6},{8,9},{9,10},{10,11},{13,12},{... | collective-permute-start | bytes 983048 | tf_op jit(solution)/shard_map/ppermute | solution.py:465
  141.6 12.7 %collective-permute-start.23 = (bf16[256,640]{1,0:T(8,128)(2,1)S(1)}, bf16[256,640]{1,0:T(8,128)(2,1)S(1)}, u32[]{:S(2)}, u32[]{:S(2)}) collective-permute-start(bf16[256,640]{1,0:T(8,128)(2,1)S(1)} %get-tuple-element.91), channel_id=1, source_target_pairs={{0,1},{1,2},{2,3},{5,4},{6,5},{7,6},{8,9},{9,10},{10,11},{13,12},{... | collective-permute-start | bytes 983048 | tf_op jit(solution)/shard_map/ppermute | solution.py:465
  161.8 23.8 %collective-permute-start.26 = (bf16[3,128,640]{2,1,0:T(8,128)(2,1)S(1)}, bf16[3,128,640]{2,1,0:T(8,128)(2,1)S(1)}, u32[]{:S(2)}, u32[]{:S(2)}) collective-permute-start(bf16[3,128,640]{2,1,0:T(8,128)(2,1)S(1)} %get-tuple-element.100), channel_id=1, source_target_pairs={{0,2},{1,3},{2,0},{3,1},{4,6},{5,7},{6,4},{7,5},{8,10},{9,11},{10,... | collective-permute-start | bytes 1474568 | tf_op jit(solution)/shard_map/ppermute | solution.py:445
  186.2 12.7 %collective-permute-start.29 = (bf16[320,1280]{1,0:T(8,128)(2,1)S(1)}, bf16[320,1280]{1,0:T(8,128)(2,1)S(1)}, u32[]{:S(2)}, u32[]{:S(2)}) collective-permute-start(bf16[320,1280]{1,0:T(8,128)(2,1)S(1)} %fusion.1), channel_id=1, source_target_pairs={{0,16},{4,12},{8,24},{12,4},{16,0},{20,28},{24,8},{28,20},{1,17},{... | collective-permute-start | bytes 2457608 | tf_op jit(solution)/shard_map/ppermute | solution.py:455
  186.7 14.1 %collective-permute-start.27 = (bf16[3,128,640]{2,1,0:T(8,128)(2,1)S(1)}, bf16[3,128,640]{2,1,0:T(8,128)(2,1)S(1)}, u32[]{:S(2)}, u32[]{:S(2)}) collective-permute-start(bf16[3,128,640]{2,1,0:T(8,128)(2,1)S(1)} %get-tuple-element.104), channel_id=1, source_target_pairs={{0,3},{1,0},{2,1},{3,2},{4,7},{5,4},{6,5},{7,6},{8,11},{9,8},{10,9... | collective-permute-start | bytes 1474568 | tf_op jit(solution)/shard_map/ppermute | solution.py:445
  189.2 21.8 %collective-permute-start.28 = (bf16[3,128,640]{2,1,0:T(8,128)(2,1)S(1)}, bf16[3,128,640]{2,1,0:T(8,128)(2,1)S(1)}, u32[]{:S(2)}, u32[]{:S(2)}) collective-permute-start(bf16[3,128,640]{2,1,0:T(8,128)(2,1)S(1)} %get-tuple-element.105), channel_id=1, source_target_pairs={{0,1},{1,2},{2,3},{3,0},{4,5},{5,6},{6,7},{7,4},{8,9},{9,10},{10,1... | collective-permute-start | bytes 1474568 | tf_op jit(solution)/shard_map/ppermute | solution.py:445
  (24 other events, 273.5 us)

commit v3 on v2

--- a/solution.py
+++ b/solution.py
@@ -51,37 +51,45 @@
     return [slice(i, i + HEAD_DIM) for i in range(0, width, HEAD_DIM)]
 
 
-def pack_call(place, query, key_in, value, n, widths):
-    rows, width = query.shape[1], sum(widths)
+def pack_call(place, query, key_in, value, n):
+    rows, width = query.shape[1], query.shape[2] // n
 
     def body(place_ref, *refs):
-        for s in range(n):
-
-            @pl.when(pl.program_id(0) == s)
-            def _():
-                start = 0
-                for g in range(len(widths)):
-                    for t in range(3):
-                        refs[3 + g * n + s][t] = refs[t][0, :, start : start + widths[g]]
-                    start += widths[g]
-
-    block = pl.BlockSpec((1, rows, width), lambda s, p: (0, 0, lax.rem(p[0] + s, n)))
-    outs = pl.pallas_call(
+        inputs, outs, (held, sems, out_sems) = refs[:3], refs[3:-3], refs[-3:]
+        order = [*range(1, n), 0]
+        for s in order:
+            first = lax.rem(place_ref[0] + s, n) * width
+            lanes = pl.ds(pl.multiple_of(first, HEAD_DIM), width)
+            for t in range(3):
+                source = inputs[t].at[0, :, lanes]
+                pltpu.make_async_copy(source, held.at[s, t], sems.at[s, t]).start()
+        for s in order:
+            for t in range(3):
+                source = inputs[t].at[0, :, pl.ds(0, width)]
+                pltpu.make_async_copy(source, held.at[s, t], sems.at[s, t]).wait()
+                pltpu.make_async_copy(held.at[s, t], outs[s].at[t], out_sems.at[s, t]).start()
+        for s in order:
+            for t in range(3):
+                pltpu.make_async_copy(held.at[s, t], outs[s].at[t], out_sems.at[s, t]).wait()
+
+    return pl.pallas_call(
         body,
         grid_spec=pltpu.PrefetchScalarGridSpec(
             num_scalar_prefetch=1,
-            grid=(n,),
-            in_specs=[block] * 3,
-            out_specs=[
-                pl.BlockSpec((3, rows, w), lambda s, p: (0, 0, 0)) for w in widths for _ in range(n)
+            grid=(1,),
+            in_specs=any_specs(3),
+            out_specs=any_specs(n),
+            scratch_shapes=[
+                pltpu.VMEM((n, 3, rows, width), BF16),
+                pltpu.SemaphoreType.DMA((n, 3)),
+                pltpu.SemaphoreType.DMA((n, 3)),
             ],
         ),
-        out_shape=[jax.ShapeDtypeStruct((3, rows, w), BF16) for w in widths for _ in range(n)],
-        compiler_params=params(),
+        out_shape=[jax.ShapeDtypeStruct((3, rows, width), BF16)] * n,
+        compiler_params=params(60),
         cost_estimate=cost(0, 12 * n * rows * width),
         name="pack_heads",
     )(place, query, key_in, value)
-    return [list(outs[g * n : (g + 1) * n]) for g in range(len(widths))]
 
 
 def attention_call(place, pieces):
@@ -91,12 +99,13 @@
     block = length // PARTS
 
     def body(place_ref, *refs):
-        piece_refs, out_refs, out_ref = refs[:n], refs[n:-1], refs[-1]
+        piece_refs, out_refs, kept_refs, out_ref = refs[:n], refs[n:-4], refs[-4:-1], refs[-1]
         places = slab_rows(place_ref[0], n, rows)
+        for t in range(3):
+            for s in range(n):
+                kept_refs[t][s * rows : (s + 1) * rows] = piece_refs[s][t]
         for lanes in head_lanes(width):
-            q, k, v = (
-                jnp.concatenate([r[t, :, lanes] for r in piece_refs], axis=0) for t in range(3)
-            )
+            q, k, v = (r[:, lanes] for r in kept_refs)
             shifted, inverse = exponentials(q, k)
             out = dot(v, shifted.astype(BF16), ((0,), (0,))) * inverse
             out = out.T.astype(BF16)
@@ -105,36 +114,39 @@
         for i in range(PARTS):
             out_refs[i][...] = out_ref[i * block : (i + 1) * block]
 
-    return pl.pallas_call(
+    def spec(*shape):
+        return pl.BlockSpec(shape, lambda i, p: (0,) * len(shape))
+
+    outs = pl.pallas_call(
         body,
         grid_spec=pltpu.PrefetchScalarGridSpec(
             num_scalar_prefetch=1,
             grid=(1,),
-            in_specs=[pl.BlockSpec((3, rows, width), lambda i, p: (0, 0, 0))] * n,
-            out_specs=[pl.BlockSpec((block, width), lambda i, p: (0, 0))] * PARTS,
+            in_specs=[spec(3, rows, width)] * n,
+            out_specs=[spec(block, width)] * PARTS + [spec(length, width)] * 3,
             scratch_shapes=[pltpu.VMEM((length, width), BF16)],
         ),
-        out_shape=[jax.ShapeDtypeStruct((block, width), BF16)] * PARTS,
-        compiler_params=params(32),
+        out_shape=[jax.ShapeDtypeStruct((block, width), BF16)] * PARTS
+        + [jax.ShapeDtypeStruct((length, width), BF16)] * 3,
+        compiler_params=params(),
         cost_estimate=cost(
-            4 * length * length * width, 8 * length * width, length * length * width // HEAD_DIM
+            4 * length * length * width, 14 * length * width, length * length * width // HEAD_DIM
         ),
         name="attention_heads",
     )(place, *pieces)
-
-
-def attention_grad_call(place, pieces, attention, d_terms):
-    n = len(pieces)
-    _, rows, width = pieces[0].shape
-    length = n * rows
-    block = length // PARTS
+    return list(outs[:PARTS]), list(outs[PARTS:])
+
+
+def attention_grad_call(place, kept, attention, d_terms, n):
+    length, width = kept[0].shape
+    rows, block = length // n, length // PARTS
     n_terms = len(d_terms)
     scale = HEAD_DIM ** (-0.5)
 
     def body(place_ref, *refs):
-        piece_refs, attn_refs = refs[:n], refs[n : n + PARTS]
-        term_refs = refs[n + PARTS : n + PARTS * (1 + n_terms)]
-        out_refs, (attn_held, d_held) = refs[n + PARTS * (1 + n_terms) : -2], refs[-2:]
+        kept_refs, attn_refs = refs[:3], refs[3 : 3 + PARTS]
+        term_refs = refs[3 + PARTS : 3 + PARTS * (1 + n_terms)]
+        out_refs, (attn_held, d_held) = refs[3 + PARTS * (1 + n_terms) : -2], refs[-2:]
         places = slab_rows(place_ref[0], n, rows)
         for i in range(PARTS):
             here = slice(i * block, (i + 1) * block)
@@ -142,9 +154,7 @@
             terms = [term_refs[t * PARTS + i][...].astype(F32) for t in range(n_terms)]
             d_held[here] = sum(terms).astype(BF16)
         for lanes in head_lanes(width):
-            q, k, v = (
-                jnp.concatenate([r[t, :, lanes] for r in piece_refs], axis=0) for t in range(3)
-            )
+            q, k, v = (r[:, lanes] for r in kept_refs)
             attn = jnp.concatenate([attn_held[p, lanes] for p in places], axis=0).astype(F32)
             d_attn = jnp.concatenate([d_held[p, lanes] for p in places], axis=0)
             shifted, inverse = exponentials(q, k)
@@ -162,24 +172,25 @@
                 for s in range(n):
                     out_refs[s][t, :, lanes] = g[s * rows : (s + 1) * rows]
 
-    piece = pl.BlockSpec((3, rows, width), lambda i, p: (0, 0, 0))
-    part = pl.BlockSpec((block, width), lambda i, p: (0, 0))
+    def spec(*shape):
+        return pl.BlockSpec(shape, lambda i, p: (0,) * len(shape))
+
     return pl.pallas_call(
         body,
         grid_spec=pltpu.PrefetchScalarGridSpec(
             num_scalar_prefetch=1,
             grid=(1,),
-            in_specs=[piece] * n + [part] * (PARTS * (1 + n_terms)),
-            out_specs=[piece] * n,
+            in_specs=[spec(length, width)] * 3 + [spec(block, width)] * (PARTS * (1 + n_terms)),
+            out_specs=[spec(3, rows, width)] * n,
             scratch_shapes=[pltpu.VMEM((length, width), BF16)] * 2,
         ),
         out_shape=[jax.ShapeDtypeStruct((3, rows, width), BF16)] * n,
-        compiler_params=params(32),
+        compiler_params=params(),
         cost_estimate=cost(
-            10 * length * length * width, 24 * length * width, length * length * width // HEAD_DIM
+            200 * length * length * width, 24 * length * width, length * length * width // HEAD_DIM
         ),
         name="attention_heads_grad",
-    )(place, *pieces, *attention, *sum(d_terms, []))
+    )(place, *kept, *attention, *sum(d_terms, []))
 
 
 def ahead(place_ref, s, n):
@@ -505,20 +516,17 @@
     me = lax.axis_index("ctx").astype(jnp.int32)
     index = lax.axis_index("dp").astype(jnp.int32)
     place = jnp.stack([me, index % 2, index])
-    width = query.shape[2] // n
-    heads = width // HEAD_DIM
-    widths = [heads * HEAD_DIM]
-
-    packed = pack_call(place, query, key_in, value, n, widths)
-    pieces = [p[:1] + [shift(p[s], "ctx", s) for s in range(1, n)] for p in packed][0]
+
+    packed = pack_call(place, query, key_in, value, n)
+    pieces = [packed[0]] + [shift(packed[s], "ctx", s) for s in range(1, n)]
     gate_row = lax.dynamic_slice_in_dim(gate_table, timestep[0], 1, 0)
 
-    one = after(chip_swap(after(out_weight, packed), "dp", 0), pieces[1])
-    two = chip_swap(jnp.stack([out_weight, one]), "dp", 1)
-    shards = after([out_weight, one, two], pieces)
+    one = chip_swap(after(out_weight, packed), "dp", 0)
+    two = chip_swap(after(jnp.stack([out_weight, one]), pieces[1]), "dp", 1)
+    shards = [out_weight, one, after(two, pieces[2])]
     shards = shards + [swap(x, "dp", 1) for x in shards]
     parts = d_attn_parts_call(place, grad_out[0], gate_row, shards, n)
-    attention = attention_call(place, pieces)
+    attention, kept = attention_call(place, after(pieces, parts))
 
     def both_ways(forward, back):
         return line_move(forward, "dp", "ctx", True), line_move(back, "dp", "ctx", False)
@@ -547,8 +555,9 @@
     d_terms = [[parts[g][0] for g in range(PARTS)]]
     d_terms += [[got[g][-1][i] for g in range(PARTS)] for i in range(2)]
 
+    grads = attention_grad_call(place, kept, attention, d_terms, n)
+    received = after(received, grads)
     far = add_rounded(keep[2:], received[2:])
-    grads = attention_grad_call(place, pieces, attention, after(d_terms, far))
     grads = [grads[0]] + [shift(grads[s], "ctx", -s) for s in range(1, n)]
     far = after(chip_swap(far, "dp", 0), grads[n // 2])
     near = keep[:2].astype(F32) + received[:2].astype(F32) + far.astype(F32)

time: 214 us -> 195 us (0.911)
  local copies, waits for them, and re-layouts: 12 us -> 3.78 us
  waiting for transfers between devices: 91 us -> 83.7 us
  starting transfers between devices: 62.4 us -> 55.4 us
  Pallas kernels: 42.1 us -> 45.3 us
    ppermute x16, starting transfers between devices: 50.5 us -> 39.7 us  [line_move(): return lax.ppermute(x, (dp_axis, axis), pairs)]
    ppermute x6, waiting for transfers between devices: 68.8 us -> 58.7 us  [shift(): return lax.ppermute(x, axis, [(i, (i + by) % n) for i in range(n)])]
    ppermute x4, waiting for transfers between devices: 0.01 us -> 8.96 us  [chip_swap(): lax.ppermute(x, axis, [(i, i ^ (2 if (i + step) % 2 == 0 else 4)) for i i...]
    unnamed x36 -> x20, local copies, waits for them, and re-layouts: 11.1 us -> 2.9 us
    ppermute x4, waiting for transfers between devices: 5.84 us -> 1.48 us  [swap(): return lax.ppermute(x, axis, [(i, i ^ mask) for i in range(n)])]
    ppermute x6, starting transfers between devices: 7.15 us -> 9.96 us  [shift(): return lax.ppermute(x, axis, [(i, (i + by) % n) for i in range(n)])]
  transfers between devices with their start and end apart: 30 -> 30, of which waited for: 13 -> 15; matrix products, arithmetic and copies ran while one was open for 1% -> 2% of each run, Pallas kernels for 17% -> 18%
where the time goes in v3:
time: 195 us; the launch traced here: 194 us
  waiting for transfers between devices  83.7 us (43%)
  starting transfers between devices  55.4 us (28%)
  Pallas kernels  45.3 us (23%)
  other arithmetic  4.28 us (2%)
  local copies, waits for them, and re-layouts  3.78 us (2%)
    ppermute x6, waiting for transfers between devices, shift(): return lax.ppermute(x, axis, [(i, (i + by) % n) for i in range(n)])  58.7 us
    ppermute x16, starting transfers between devices, line_move(): return lax.ppermute(x, (dp_axis, axis), pairs)  39.7 us
    ppermute x16, waiting for transfers between devices, line_move(): return lax.ppermute(x, (dp_axis, axis), pairs)  14.6 us
    ppermute x6, starting transfers between devices, shift(): return lax.ppermute(x, axis, [(i, (i + by) % n) for i in range(n)])  9.96 us
    pallas_call x1, Pallas kernels, projection_call(): pl.pallas_call(body, grid_spec=pltpu.PrefetchScalarGridSpec(num_scalar_pr...  9.66 us
    ppermute x4, waiting for transfers between devices, chip_swap(): lax.ppermute(x, axis, [(i, i ^ (2 if (i + step) % 2 == 0 else 4)) for i i...  8.96 us
    pallas_call x1, Pallas kernels, d_attn_parts_call(): pl.pallas_call(body, grid_spec=pltpu.PrefetchScalarGridSpec(num_scalar_pr...  8.83 us
    pallas_call x2, Pallas kernels, weight_grad_call(): pl.pallas_call(body, grid_spec=pltpu.PrefetchScalarGridSpec(num_scalar_pr...  6.94 us
  transfers between devices with their start and end apart: 30, of which 15 were waited for; matrix products, arithmetic and copies ran while one was open for 2% of the time, Pallas kernels for 18%

profile of v3, /device:TPU:0, one launch (start us, length us, event | category | flops | bytes accessed | tf_op | source)
XLA Modules:
  0.0 194.2 jit_solution(808912919434140893)
XLA Ops:
  1.2 3.3 %pack_heads.1 = (bf16[3,128,640]{2,1,0:T(8,128)(2,1)}, bf16[3,128,640]{2,1,0:T(8,128)(2,1)}, bf16[3,128,640]{2,1,0:T(8,128)(2,1)}, bf16[3,128,640]{2,1,0:T(8,128)(2,1)}) custom-call(s32[3]{0:T(128)} %pad_add_fusion.place_ref, bf16[1,128,2560]{2,1,0:T(8,128)(2,1)} %refs_0_.2, bf16[1,128,2560]{2,1,0:T(8,128)(2,1)} %refs_1_.1, bf16[1,128,2560]{2,1,0:T(8,128)(2,1)} %refs_2_.1), custom_call_target="tpu_custom_call" | custom-call | bytes 3932160 | tf_op jit(solution)/shard_map/pack_heads/pallas_call | solution.py:75
  4.6 3.0 %collective-permute-start.3 = (bf16[320,1280]{1,0:T(8,128)(2,1)}, bf16[320,1280]{1,0:T(8,128)(2,1)S(1)}, u32[]{:S(2)}, u32[]{:S(2)}) collective-permute-start(bf16[320,1280]{1,0:T(8,128)(2,1)} %refs_14_.1), channel_id=1, source_target_pairs={{0,8},{4,20},{8,0},{12,28},{16,24},{20,4},{24,16},{28,12},{1,9},{5... | collective-permute-start | bytes 2457608 | tf_op jit(solution)/shard_map/ppermute | solution.py:466
  9.1 9.0 %collective-permute-done.3.refs_1_.refs_15_ = bf16[320,1280]{1,0:T(8,128)(2,1)S(1)} collective-permute-done((bf16[320,1280]{1,0:T(8,128)(2,1)}, bf16[320,1280]{1,0:T(8,128)(2,1)S(1)}, u32[]{:S(2)}, u32[]{:S(2)}) %collective-permute-start.3) | collective-permute-done | bytes 819232 | tf_op jit(solution)/shard_map/ppermute | solution.py:466
  19.4 2.9 %collective-permute-done.refs_1_ = bf16[3,128,640]{2,1,0:T(8,128)(2,1)S(1)} collective-permute-done((bf16[3,128,640]{2,1,0:T(8,128)(2,1)}, bf16[3,128,640]{2,1,0:T(8,128)(2,1)S(1)}, u32[]{:S(2)}, u32[]{:S(2)}) %collective-permute-start) | collective-permute-done | bytes 491552 | tf_op jit(solution)/shard_map/ppermute | solution.py:456
  24.8 23.0 %collective-permute-done.1.refs_2_ = bf16[3,128,640]{2,1,0:T(8,128)(2,1)S(1)} collective-permute-done((bf16[3,128,640]{2,1,0:T(8,128)(2,1)S(1)}, bf16[3,128,640]{2,1,0:T(8,128)(2,1)S(1)}, u32[]{:S(2)}, u32[]{:S(2)}) %collective-permute-start.1) | collective-permute-done | bytes 491552 | tf_op jit(solution)/shard_map/ppermute | solution.py:456
  55.9 8.8 %d_attn_parts.1 = (bf16[256,640]{1,0:T(8,128)(2,1)S(1)}, bf16[256,640]{1,0:T(8,128)(2,1)S(1)}, bf16[256,640]{1,0:T(8,128)(2,1)S(1)}, bf16[256,640]{1,0:T(8,128)(...) custom-call(s32[3]{0:T(128)S(1)} %copy-done.3, ...), custom_call_target="tpu_custom_call" | custom-call | flops 3355443200 | bytes 10485760 | tf_op jit(solution)/shard_map/d_attn_parts/pallas_call | solution.py:282
  64.8 4.6 %attention_heads.1 = (bf16[256,640]{1,0:T(8,128)(2,1)S(1)}, bf16[256,640]{1,0:T(8,128)(2,1)S(1)}, bf16[512,640]{1,0:T(8,128)(2,1)S(1)}, bf16[512,640]{1,0:T(8,128)(2,1)S(1)}, bf16[512,640]{1,0:T(8,128)(2,1)S(1)}) custom-call(s32[3]{0:T(128)S(1)} %copy-done.3, bf16[3,128,640]{2,1,0:T(8,128)(2,1)S(1)} %copy-done.4, bf16[3,128,640]{2,1,0:T(8,128)(2,1)S(1)} %copy-done.6, ...), custom_call_target="tpu_custom_call" | custom-call | flops 671088640 | bytes 4587520 | tf_op jit(solution)/shard_map/attention_heads/pallas_call | solution.py:120
  72.0 4.6 %collective-permute-start.8 = (bf16[256,640]{1,0:T(8,128)(2,1)S(1)}, bf16[256,640]{1,0:T(8,128)(2,1)S(1)}, u32[]{:S(2)}, u32[]{:S(2)}) collective-permute-start(bf16[256,640]{1,0:T(8,128)(2,1)S(1)} %get-tuple-element.78.refs_0_.refs_1_.refs_3_), channel_id=1, source_target_pairs={{0,1},{1,2},{2,3},{5,4},{6,5},{7,6},{8,9},{9,10},{10,11},{13,12},{... | collective-permute-start | bytes 983048 | tf_op jit(solution)/shard_map/ppermute | solution.py:476
  77.9 4.2 %collective-permute-done.14.back.refs_3_.refs_11_ = bf16[256,640]{1,0:T(8,128)(2,1)S(1)} collective-permute-done((bf16[256,640]{1,0:T(8,128)(2,1)S(1)}, bf16[256,640]{1,0:T(8,128)(2,1)S(1)}, u32[]{:S(2)}, u32[]{:S(2)}) %collective-permute-start.14) | collective-permute-done | bytes 327712 | tf_op jit(solution)/shard_map/ppermute | solution.py:476
  82.8 4.6 %collective-permute-start.15 = (bf16[256,640]{1,0:T(8,128)(2,1)S(1)}, bf16[256,640]{1,0:T(8,128)(2,1)S(1)}, u32[]{:S(2)}, u32[]{:S(2)}) collective-permute-start(bf16[256,640]{1,0:T(8,128)(2,1)S(1)} %get-tuple-element.83), channel_id=1, source_target_pairs={{0,1},{1,2},{2,3},{5,4},{6,5},{7,6},{8,9},{9,10},{10,11},{13,12},{... | collective-permute-start | bytes 983048 | tf_op jit(solution)/shard_map/ppermute | solution.py:476
  89.8 4.5 %collective-permute-start.10 = (bf16[256,640]{1,0:T(8,128)(2,1)S(1)}, bf16[256,640]{1,0:T(8,128)(2,1)S(1)}, u32[]{:S(2)}, u32[]{:S(2)}) collective-permute-start(bf16[256,640]{1,0:T(8,128)(2,1)S(1)} %get-tuple-element.79), channel_id=1, source_target_pairs={{0,1},{1,2},{2,3},{5,4},{6,5},{7,6},{8,9},{9,10},{10,11},{13,12},{... | collective-permute-start | bytes 983048 | tf_op jit(solution)/shard_map/ppermute | solution.py:476
  95.7 3.4 %collective-permute-done.16.back.refs_7_.refs_12_ = bf16[256,640]{1,0:T(8,128)(2,1)S(1)} collective-permute-done((bf16[256,640]{1,0:T(8,128)(2,1)S(1)}, bf16[256,640]{1,0:T(8,128)(2,1)S(1)}, u32[]{:S(2)}, u32[]{:S(2)}) %collective-permute-start.16) | collective-permute-done | bytes 327712 | tf_op jit(solution)/shard_map/ppermute | solution.py:476
  99.8 3.5 %collective-permute-start.17 = (bf16[256,640]{1,0:T(8,128)(2,1)S(1)}, bf16[256,640]{1,0:T(8,128)(2,1)S(1)}, u32[]{:S(2)}, u32[]{:S(2)}) collective-permute-start(bf16[256,640]{1,0:T(8,128)(2,1)S(1)} %get-tuple-element.85), channel_id=1, source_target_pairs={{0,1},{1,2},{2,3},{5,4},{6,5},{7,6},{8,9},{9,10},{10,11},{13,12},{... | collective-permute-start | bytes 983048 | tf_op jit(solution)/shard_map/ppermute | solution.py:476
  106.7 3.5 %collective-permute-start.12 = (bf16[256,640]{1,0:T(8,128)(2,1)S(1)}, bf16[256,640]{1,0:T(8,128)(2,1)S(1)}, u32[]{:S(2)}, u32[]{:S(2)}) collective-permute-start(bf16[256,640]{1,0:T(8,128)(2,1)S(1)} %get-tuple-element.81), channel_id=1, source_target_pairs={{0,1},{1,2},{2,3},{5,4},{6,5},{7,6},{8,9},{9,10},{10,11},{13,12},{... | collective-permute-start | bytes 983048 | tf_op jit(solution)/shard_map/ppermute | solution.py:476
  111.6 2.5 %collective-permute-done.19.refs_7_.back.refs_13_ = bf16[256,640]{1,0:T(8,128)(2,1)S(1)} collective-permute-done((bf16[256,640]{1,0:T(8,128)(2,1)S(1)}, bf16[256,640]{1,0:T(8,128)(2,1)S(1)}, u32[]{:S(2)}, u32[]{:S(2)}) %collective-permute-start.19) | collective-permute-done | bytes 327712 | tf_op jit(solution)/shard_map/ppermute | solution.py:476
  114.7 3.6 %collective-permute-start.22 = (bf16[256,640]{1,0:T(8,128)(2,1)S(1)}, bf16[256,640]{1,0:T(8,128)(2,1)S(1)}, u32[]{:S(2)}, u32[]{:S(2)}) collective-permute-start(bf16[256,640]{1,0:T(8,128)(2,1)S(1)} %get-tuple-element.96), channel_id=1, source_target_pairs={{0,1},{1,2},{2,3},{5,4},{6,5},{7,6},{8,9},{9,10},{10,11},{13,12},{... | collective-permute-start | bytes 983048 | tf_op jit(solution)/shard_map/ppermute | solution.py:476
  122.6 3.4 %collective-permute-start.21 = (bf16[256,640]{1,0:T(8,128)(2,1)S(1)}, bf16[256,640]{1,0:T(8,128)(2,1)S(1)}, u32[]{:S(2)}, u32[]{:S(2)}) collective-permute-start(bf16[256,640]{1,0:T(8,128)(2,1)S(1)} %get-tuple-element.95), channel_id=1, source_target_pairs={{0,1},{1,2},{2,3},{5,4},{6,5},{7,6},{8,9},{9,10},{10,11},{13,12},{... | collective-permute-start | bytes 983048 | tf_op jit(solution)/shard_map/ppermute | solution.py:476
  127.5 3.5 %weight_grad.2 = (bf16[4,320,1280]{2,1,0:T(8,128)(2,1)S(1)}, bf16[4,320,1280]{2,1,0:T(8,128)(2,1)S(1)}) custom-call(s32[3]{0:T(128)S(1)} %copy-done.3, bf16[512,1280]{1,0:T(8,128)(2,1)S(1)} %bitcast.23, f32[1,1280]{1,0:T(1,128)S(1)} %constant_dynamic-slice_fusion.gate_ref, bf16[256,640]{1,0:T(8,128)(2,1)S(1)} %get-tuple-element.78.refs_0_.refs_1_.refs_3_, ...), custom_call_target="tpu_custom_call" | custom-call | flops 1677721600 | bytes 7208960 | tf_op jit(solution)/shard_map/weight_grad/pallas_call | solution.py:400
  130.9 3.5 %weight_grad.3 = (bf16[4,320,1280]{2,1,0:T(8,128)(2,1)S(1)}, bf16[4,320,1280]{2,1,0:T(8,128)(2,1)S(1)}) custom-call(s32[3]{0:T(128)S(1)} %copy-done.3, bf16[512,1280]{1,0:T(8,128)(2,1)S(1)} %bitcast.24, f32[1,1280]{1,0:T(1,128)S(1)} %constant_dynamic-slice_fusion.gate_ref, ...), custom_call_target="tpu_custom_call", output_to_operand_aliasing={{0}: (11, {}), {1}: (12, {})} | custom-call | flops 1677721600 | bytes 7208960 | tf_op jit(solution)/shard_map/weight_grad/pallas_call | solution.py:400
  134.9 6.1 %attention_heads_grad.1 = (bf16[3,128,640]{2,1,0:T(8,128)(2,1)S(1)}, bf16[3,128,640]{2,1,0:T(8,128)(2,1)S(1)}, bf16[3,128,640]{2,1,0:T(8,128)(2,1)S(1)}, bf16[3,128,640]{2,1,0:T(8,128)(2,1)S(1)}) custom-call(s32[3]{0:T(128)S(1)} %copy-done.3, bf16[512,640]{1,0:T(8,128)(2,1)S(1)} %get-tuple-element.92.refs_0_, ...), custom_call_target="tpu_custom_call" | custom-call | flops 33554432000 | bytes 7864320 | tf_op jit(solution)/shard_map/attention_heads_grad/pallas_call | solution.py:178
  141.8 2.7 %collective-permute-start.26 = (bf16[3,128,640]{2,1,0:T(8,128)(2,1)S(1)}, bf16[3,128,640]{2,1,0:T(8,128)(2,1)S(1)}, u32[]{:S(2)}, u32[]{:S(2)}) collective-permute-start(bf16[3,128,640]{2,1,0:T(8,128)(2,1)S(1)} %get-tuple-element.101), channel_id=1, source_target_pairs={{0,2},{1,3},{2,0},{3,1},{4,6},{5,7},{6,4},{7,5},{8,10},{9,11},{10,... | collective-permute-start | bytes 1474568 | tf_op jit(solution)/shard_map/ppermute | solution.py:456
  144.5 22.8 %collective-permute-done.26.refs_2_ = bf16[3,128,640]{2,1,0:T(8,128)(2,1)S(1)} collective-permute-done((bf16[3,128,640]{2,1,0:T(8,128)(2,1)S(1)}, bf16[3,128,640]{2,1,0:T(8,128)(2,1)S(1)}, u32[]{:S(2)}, u32[]{:S(2)}) %collective-permute-start.26) | collective-permute-done | bytes 491552 | tf_op jit(solution)/shard_map/ppermute | solution.py:456
  171.2 9.7 %projection.1 = bf16[512,1280]{1,0:T(8,128)(2,1)} custom-call(s32[3]{0:T(128)S(1)} %copy-done.3, f32[1,1280]{1,0:T(1,128)S(1)} %constant_dynamic-slice_fusion.gate_ref, bf16[256,640]{1,0:T(8,128)(2,1)S(1)} %get-tuple-element.78.refs_0_.refs_1_.refs_3_, bf16[256,640]{1,0:T(8,128)(2,1)S(1)} %get-tuple-element.82.refs_2_.refs_3_.refs_4_.refs_1_, ...), custom_call_target="tpu_custom_call" | custom-call | flops 3355443200 | bytes 10485760 | tf_op jit(solution)/shard_map/projection/pallas_call | solution.py:331
  182.6 9.6 %collective-permute-done.28.refs_3_ = bf16[3,128,640]{2,1,0:T(8,128)(2,1)S(1)} collective-permute-done((bf16[3,128,640]{2,1,0:T(8,128)(2,1)S(1)}, bf16[3,128,640]{2,1,0:T(8,128)(2,1)S(1)}, u32[]{:S(2)}, u32[]{:S(2)}) %collective-permute-start.28) | collective-permute-done | bytes 491552 | tf_op jit(solution)/shard_map/ppermute | solution.py:456
  (77 shorter events, 42.1 us)
Async XLA Ops:
  4.6 13.5 %collective-permute-start.3 = (bf16[320,1280]{1,0:T(8,128)(2,1)}, bf16[320,1280]{1,0:T(8,128)(2,1)S(1)}, u32[]{:S(2)}, u32[]{:S(2)}) collective-permute-start(bf16[320,1280]{1,0:T(8,128)(2,1)} %refs_14_.1), channel_id=1, source_target_pairs={{0,8},{4,20},{8,0},{12,28},{16,24},{20,4},{24,16},{28,12},{1,9},{5... | collective-permute-start | bytes 2457608 | tf_op jit(solution)/shard_map/ppermute | solution.py:466
  7.6 14.8 %collective-permute-start = (bf16[3,128,640]{2,1,0:T(8,128)(2,1)}, bf16[3,128,640]{2,1,0:T(8,128)(2,1)S(1)}, u32[]{:S(2)}, u32[]{:S(2)}) collective-permute-start(bf16[3,128,640]{2,1,0:T(8,128)(2,1)} %get-tuple-element.60), channel_id=1, source_target_pairs={{0,1},{1,2},{2,3},{3,0},{4,5},{5,6},{6,7},{7,4},{8,9},{9,10},{10,1... | collective-permute-start | bytes 1474568 | tf_op jit(solution)/shard_map/ppermute | solution.py:456
  23.1 25.5 %collective-permute-start.4 = (bf16[2,320,1280]{2,1,0:T(8,128)(2,1)S(1)}, bf16[2,320,1280]{2,1,0:T(8,128)(2,1)S(1)}, u32[]{:S(2)}, u32[]{:S(2)}) collective-permute-start(bf16[2,320,1280]{2,1,0:T(8,128)(2,1)S(1)} %pad_maximum_fusion), channel_id=1, source_target_pairs={{0,16},{4,12},{8,24},{12,4},{16,0},{20,28},{24,8},{28,20},{1,17},{... | collective-permute-start | bytes 4915208 | tf_op jit(solution)/shard_map/ppermute | solution.py:466
  23.6 24.2 %collective-permute-start.1 = (bf16[3,128,640]{2,1,0:T(8,128)(2,1)S(1)}, bf16[3,128,640]{2,1,0:T(8,128)(2,1)S(1)}, u32[]{:S(2)}, u32[]{:S(2)}) collective-permute-start(bf16[3,128,640]{2,1,0:T(8,128)(2,1)S(1)} %copy-done.9), channel_id=1, source_target_pairs={{0,2},{1,3},{2,0},{3,1},{4,6},{5,7},{6,4},{7,5},{8,10},{9,11},{10,... | collective-permute-start | bytes 1474568 | tf_op jit(solution)/shard_map/ppermute | solution.py:456
  49.2 15.5 %collective-permute-start.2 = (bf16[3,128,640]{2,1,0:T(8,128)(2,1)}, bf16[3,128,640]{2,1,0:T(8,128)(2,1)}, u32[]{:S(2)}, u32[]{:S(2)}) collective-permute-start(bf16[3,128,640]{2,1,0:T(8,128)(2,1)} %get-tuple-element.62), channel_id=1, source_target_pairs={{0,3},{1,0},{2,1},{3,2},{4,7},{5,4},{6,5},{7,6},{8,11},{9,8},{10,9... | collective-permute-start | bytes 1474568 | tf_op jit(solution)/shard_map/ppermute | solution.py:456
  70.7 11.4 %collective-permute-start.14 = (bf16[256,640]{1,0:T(8,128)(2,1)S(1)}, bf16[256,640]{1,0:T(8,128)(2,1)S(1)}, u32[]{:S(2)}, u32[]{:S(2)}) collective-permute-start(bf16[256,640]{1,0:T(8,128)(2,1)S(1)} %get-tuple-element.82.refs_2_.refs_3_.refs_4_.refs_1_), channel_id=1, source_target_pairs={{1,0},{2,1},{3,2},{4,5},{5,6},{6,7},{9,8},{10,9},{11,10},{12,13},{... | collective-permute-start | bytes 983048 | tf_op jit(solution)/shard_map/ppermute | solution.py:476
  72.0 16.9 %collective-permute-start.8 = (bf16[256,640]{1,0:T(8,128)(2,1)S(1)}, bf16[256,640]{1,0:T(8,128)(2,1)S(1)}, u32[]{:S(2)}, u32[]{:S(2)}) collective-permute-start(bf16[256,640]{1,0:T(8,128)(2,1)S(1)} %get-tuple-element.78.refs_0_.refs_1_.refs_3_), channel_id=1, source_target_pairs={{0,1},{1,2},{2,3},{5,4},{6,5},{7,6},{8,9},{9,10},{10,11},{13,12},{... | collective-permute-start | bytes 983048 | tf_op jit(solution)/shard_map/ppermute | solution.py:476
  76.6 12.6 %collective-permute-start.9 = (bf16[256,640]{1,0:T(8,128)(2,1)S(1)}, bf16[256,640]{1,0:T(8,128)(2,1)S(1)}, u32[]{:S(2)}, u32[]{:S(2)}) collective-permute-start(bf16[256,640]{1,0:T(8,128)(2,1)S(1)} %get-tuple-element.78.refs_0_.refs_1_.refs_3_), channel_id=1, source_target_pairs={{1,0},{2,1},{3,2},{4,5},{5,6},{6,7},{9,8},{10,9},{11,10},{12,13},{... | collective-permute-start | bytes 983048 | tf_op jit(solution)/shard_map/ppermute | solution.py:476
  82.8 12.9 %collective-permute-start.15 = (bf16[256,640]{1,0:T(8,128)(2,1)S(1)}, bf16[256,640]{1,0:T(8,128)(2,1)S(1)}, u32[]{:S(2)}, u32[]{:S(2)}) collective-permute-start(bf16[256,640]{1,0:T(8,128)(2,1)S(1)} %get-tuple-element.83), channel_id=1, source_target_pairs={{0,1},{1,2},{2,3},{5,4},{6,5},{7,6},{8,9},{9,10},{10,11},{13,12},{... | collective-permute-start | bytes 983048 | tf_op jit(solution)/shard_map/ppermute | solution.py:476
  87.4 11.7 %collective-permute-start.16 = (bf16[256,640]{1,0:T(8,128)(2,1)S(1)}, bf16[256,640]{1,0:T(8,128)(2,1)S(1)}, u32[]{:S(2)}, u32[]{:S(2)}) collective-permute-start(bf16[256,640]{1,0:T(8,128)(2,1)S(1)} %get-tuple-element.84), channel_id=1, source_target_pairs={{1,0},{2,1},{3,2},{4,5},{5,6},{6,7},{9,8},{10,9},{11,10},{12,13},{... | collective-permute-start | bytes 983048 | tf_op jit(solution)/shard_map/ppermute | solution.py:476
  89.8 14.8 %collective-permute-start.10 = (bf16[256,640]{1,0:T(8,128)(2,1)S(1)}, bf16[256,640]{1,0:T(8,128)(2,1)S(1)}, u32[]{:S(2)}, u32[]{:S(2)}) collective-permute-start(bf16[256,640]{1,0:T(8,128)(2,1)S(1)} %get-tuple-element.79), channel_id=1, source_target_pairs={{0,1},{1,2},{2,3},{5,4},{6,5},{7,6},{8,9},{9,10},{10,11},{13,12},{... | collective-permute-start | bytes 983048 | tf_op jit(solution)/shard_map/ppermute | solution.py:476
  94.3 11.7 %collective-permute-start.11 = (bf16[256,640]{1,0:T(8,128)(2,1)S(1)}, bf16[256,640]{1,0:T(8,128)(2,1)S(1)}, u32[]{:S(2)}, u32[]{:S(2)}) collective-permute-start(bf16[256,640]{1,0:T(8,128)(2,1)S(1)} %get-tuple-element.80), channel_id=1, source_target_pairs={{1,0},{2,1},{3,2},{4,5},{5,6},{6,7},{9,8},{10,9},{11,10},{12,13},{... | collective-permute-start | bytes 983048 | tf_op jit(solution)/shard_map/ppermute | solution.py:476
  99.8 11.8 %collective-permute-start.17 = (bf16[256,640]{1,0:T(8,128)(2,1)S(1)}, bf16[256,640]{1,0:T(8,128)(2,1)S(1)}, u32[]{:S(2)}, u32[]{:S(2)}) collective-permute-start(bf16[256,640]{1,0:T(8,128)(2,1)S(1)} %get-tuple-element.85), channel_id=1, source_target_pairs={{0,1},{1,2},{2,3},{5,4},{6,5},{7,6},{8,9},{9,10},{10,11},{13,12},{... | collective-permute-start | bytes 983048 | tf_op jit(solution)/shard_map/ppermute | solution.py:476
  103.3 10.8 %collective-permute-start.19 = (bf16[256,640]{1,0:T(8,128)(2,1)S(1)}, bf16[256,640]{1,0:T(8,128)(2,1)S(1)}, u32[]{:S(2)}, u32[]{:S(2)}) collective-permute-start(bf16[256,640]{1,0:T(8,128)(2,1)S(1)} %get-tuple-element.87), channel_id=1, source_target_pairs={{1,0},{2,1},{3,2},{4,5},{5,6},{6,7},{9,8},{10,9},{11,10},{12,13},{... | collective-permute-start | bytes 983048 | tf_op jit(solution)/shard_map/ppermute | solution.py:476
  106.7 12.9 %collective-permute-start.12 = (bf16[256,640]{1,0:T(8,128)(2,1)S(1)}, bf16[256,640]{1,0:T(8,128)(2,1)S(1)}, u32[]{:S(2)}, u32[]{:S(2)}) collective-permute-start(bf16[256,640]{1,0:T(8,128)(2,1)S(1)} %get-tuple-element.81), channel_id=1, source_target_pairs={{0,1},{1,2},{2,3},{5,4},{6,5},{7,6},{8,9},{9,10},{10,11},{13,12},{... | collective-permute-start | bytes 983048 | tf_op jit(solution)/shard_map/ppermute | solution.py:476
  110.3 11.6 %collective-permute-start.18 = (bf16[256,640]{1,0:T(8,128)(2,1)S(1)}, bf16[256,640]{1,0:T(8,128)(2,1)S(1)}, u32[]{:S(2)}, u32[]{:S(2)}) collective-permute-start(bf16[256,640]{1,0:T(8,128)(2,1)S(1)} %get-tuple-element.86), channel_id=1, source_target_pairs={{1,0},{2,1},{3,2},{4,5},{5,6},{6,7},{9,8},{10,9},{11,10},{12,13},{... | collective-permute-start | bytes 983048 | tf_op jit(solution)/shard_map/ppermute | solution.py:476
  114.7 19.8 %collective-permute-start.22 = (bf16[256,640]{1,0:T(8,128)(2,1)S(1)}, bf16[256,640]{1,0:T(8,128)(2,1)S(1)}, u32[]{:S(2)}, u32[]{:S(2)}) collective-permute-start(bf16[256,640]{1,0:T(8,128)(2,1)S(1)} %get-tuple-element.96), channel_id=1, source_target_pairs={{0,1},{1,2},{2,3},{5,4},{6,5},{7,6},{8,9},{9,10},{10,11},{13,12},{... | collective-permute-start | bytes 983048 | tf_op jit(solution)/shard_map/ppermute | solution.py:476
  118.3 16.2 %collective-permute-start.24 = (bf16[256,640]{1,0:T(8,128)(2,1)S(1)}, bf16[256,640]{1,0:T(8,128)(2,1)S(1)}, u32[]{:S(2)}, u32[]{:S(2)}) collective-permute-start(bf16[256,640]{1,0:T(8,128)(2,1)S(1)} %get-tuple-element.98), channel_id=1, source_target_pairs={{1,0},{2,1},{3,2},{4,5},{5,6},{6,7},{9,8},{10,9},{11,10},{12,13},{... | collective-permute-start | bytes 983048 | tf_op jit(solution)/shard_map/ppermute | solution.py:476
  122.6 12.0 %collective-permute-start.21 = (bf16[256,640]{1,0:T(8,128)(2,1)S(1)}, bf16[256,640]{1,0:T(8,128)(2,1)S(1)}, u32[]{:S(2)}, u32[]{:S(2)}) collective-permute-start(bf16[256,640]{1,0:T(8,128)(2,1)S(1)} %get-tuple-element.95), channel_id=1, source_target_pairs={{0,1},{1,2},{2,3},{5,4},{6,5},{7,6},{8,9},{9,10},{10,11},{13,12},{... | collective-permute-start | bytes 983048 | tf_op jit(solution)/shard_map/ppermute | solution.py:476
  141.5 25.9 %collective-permute-start.25 = (bf16[2,320,1280]{2,1,0:T(8,128)(2,1)S(1)}, bf16[2,320,1280]{2,1,0:T(8,128)(2,1)S(1)}, u32[]{:S(2)}, u32[]{:S(2)}) collective-permute-start(bf16[2,320,1280]{2,1,0:T(8,128)(2,1)S(1)} %add_convert_fusion), channel_id=1, source_target_pairs={{0,8},{4,20},{8,0},{12,28},{16,24},{20,4},{24,16},{28,12},{1,9},{5... | collective-permute-start | bytes 4915208 | tf_op jit(solution)/shard_map/ppermute | solution.py:466
  141.8 25.5 %collective-permute-start.26 = (bf16[3,128,640]{2,1,0:T(8,128)(2,1)S(1)}, bf16[3,128,640]{2,1,0:T(8,128)(2,1)S(1)}, u32[]{:S(2)}, u32[]{:S(2)}) collective-permute-start(bf16[3,128,640]{2,1,0:T(8,128)(2,1)S(1)} %get-tuple-element.101), channel_id=1, source_target_pairs={{0,2},{1,3},{2,0},{3,1},{4,6},{5,7},{6,4},{7,5},{8,10},{9,11},{10,... | collective-permute-start | bytes 1474568 | tf_op jit(solution)/shard_map/ppermute | solution.py:456
  168.1 12.8 %collective-permute-start.29 = (bf16[320,1280]{1,0:T(8,128)(2,1)S(1)}, bf16[320,1280]{1,0:T(8,128)(2,1)S(1)}, u32[]{:S(2)}, u32[]{:S(2)}) collective-permute-start(bf16[320,1280]{1,0:T(8,128)(2,1)S(1)} %fusion.1), channel_id=1, source_target_pairs={{0,16},{4,12},{8,24},{12,4},{16,0},{20,28},{24,8},{28,20},{1,17},{... | collective-permute-start | bytes 2457608 | tf_op jit(solution)/shard_map/ppermute | solution.py:466
  169.2 13.4 %collective-permute-start.27 = (bf16[3,128,640]{2,1,0:T(8,128)(2,1)S(1)}, bf16[3,128,640]{2,1,0:T(8,128)(2,1)S(1)}, u32[]{:S(2)}, u32[]{:S(2)}) collective-permute-start(bf16[3,128,640]{2,1,0:T(8,128)(2,1)S(1)} %get-tuple-element.100), channel_id=1, source_target_pairs={{0,3},{1,0},{2,1},{3,2},{4,7},{5,4},{6,5},{7,6},{8,11},{9,8},{10,9... | collective-permute-start | bytes 1474568 | tf_op jit(solution)/shard_map/ppermute | solution.py:456
  170.9 21.3 %collective-permute-start.28 = (bf16[3,128,640]{2,1,0:T(8,128)(2,1)S(1)}, bf16[3,128,640]{2,1,0:T(8,128)(2,1)S(1)}, u32[]{:S(2)}, u32[]{:S(2)}) collective-permute-start(bf16[3,128,640]{2,1,0:T(8,128)(2,1)S(1)} %get-tuple-element.102), channel_id=1, source_target_pairs={{0,1},{1,2},{2,3},{3,0},{4,5},{5,6},{6,7},{7,4},{8,9},{9,10},{10,1... | collective-permute-start | bytes 1474568 | tf_op jit(solution)/shard_map/ppermute | solution.py:456
  (16 other events, 230.2 us)

commit v4 on v3

--- a/solution.py
+++ b/solution.py
@@ -51,14 +51,16 @@
     return [slice(i, i + HEAD_DIM) for i in range(0, width, HEAD_DIM)]
 
 
-def pack_call(place, query, key_in, value, n):
+def pack_call(query, key_in, value, axis):
+    n = lax.axis_size(axis)
     rows, width = query.shape[1], query.shape[2] // n
 
-    def body(place_ref, *refs):
+    def body(*refs):
+        me = lax.axis_index(axis)
         inputs, outs, (held, sems, out_sems) = refs[:3], refs[3:-3], refs[-3:]
         order = [*range(1, n), 0]
         for s in order:
-            first = lax.rem(place_ref[0] + s, n) * width
+            first = lax.rem(me + s, n) * width
             lanes = pl.ds(pl.multiple_of(first, HEAD_DIM), width)
             for t in range(3):
                 source = inputs[t].at[0, :, lanes]
@@ -74,70 +76,71 @@
 
     return pl.pallas_call(
         body,
+        in_specs=any_specs(3),
+        out_specs=any_specs(n),
+        scratch_shapes=[
+            pltpu.VMEM((n, 3, rows, width), BF16),
+            pltpu.SemaphoreType.DMA((n, 3)),
+            pltpu.SemaphoreType.DMA((n, 3)),
+        ],
+        out_shape=[jax.ShapeDtypeStruct((3, rows, width), BF16)] * n,
+        compiler_params=pltpu.CompilerParams(vmem_limit_bytes=60 * MIB),
+        cost_estimate=cost(0, 12 * n * rows * width),
+        name="pack_heads",
+    )(query, key_in, value)
+
+
+def attention_call(place, inputs, block, n):
+    first = len(inputs) == n
+    rows, width = inputs[0].shape[-2:] if first else (inputs[0].shape[0] // n, inputs[0].shape[1])
+    length = n * rows
+    slabs = n // PARTS
+
+    def body(place_ref, *refs):
+        in_refs, out_ref = refs[: len(inputs)], refs[len(inputs)]
+        kept_refs = refs[len(inputs) + 1 :] if first else in_refs
+        if first:
+            for t in range(3):
+                for s in range(n):
+                    kept_refs[t][s * rows : (s + 1) * rows] = in_refs[s][t]
+        wanted = [
+            pl.ds(pl.multiple_of(lax.rem(place_ref[0] + n - slab, n) * rows, rows), rows)
+            for slab in range(block * slabs, (block + 1) * slabs)
+        ]
+        for lanes in head_lanes(width):
+            q = jnp.concatenate([kept_refs[0][w, lanes] for w in wanted], axis=0)
+            shifted, inverse = exponentials(q, kept_refs[1][:, lanes])
+            out = dot(kept_refs[2][:, lanes], shifted.astype(BF16), ((0,), (0,))) * inverse
+            out_ref[:, lanes] = out.T.astype(BF16)
+
+    def spec(*shape):
+        return pl.BlockSpec(shape, lambda i, p: (0,) * len(shape))
+
+    def out_of(*shape):
+        return jax.ShapeDtypeStruct(shape, BF16)
+
+    kept = [(length, width)] * (3 * first)
+    outs = pl.pallas_call(
+        body,
         grid_spec=pltpu.PrefetchScalarGridSpec(
             num_scalar_prefetch=1,
             grid=(1,),
-            in_specs=any_specs(3),
-            out_specs=any_specs(n),
-            scratch_shapes=[
-                pltpu.VMEM((n, 3, rows, width), BF16),
-                pltpu.SemaphoreType.DMA((n, 3)),
-                pltpu.SemaphoreType.DMA((n, 3)),
-            ],
-        ),
-        out_shape=[jax.ShapeDtypeStruct((3, rows, width), BF16)] * n,
-        compiler_params=params(60),
-        cost_estimate=cost(0, 12 * n * rows * width),
-        name="pack_heads",
-    )(place, query, key_in, value)
-
-
-def attention_call(place, pieces):
-    n = len(pieces)
-    _, rows, width = pieces[0].shape
-    length = n * rows
-    block = length // PARTS
-
-    def body(place_ref, *refs):
-        piece_refs, out_refs, kept_refs, out_ref = refs[:n], refs[n:-4], refs[-4:-1], refs[-1]
-        places = slab_rows(place_ref[0], n, rows)
-        for t in range(3):
-            for s in range(n):
-                kept_refs[t][s * rows : (s + 1) * rows] = piece_refs[s][t]
-        for lanes in head_lanes(width):
-            q, k, v = (r[:, lanes] for r in kept_refs)
-            shifted, inverse = exponentials(q, k)
-            out = dot(v, shifted.astype(BF16), ((0,), (0,))) * inverse
-            out = out.T.astype(BF16)
-            for s in range(n):
-                out_ref[places[s], lanes] = out[s * rows : (s + 1) * rows]
-        for i in range(PARTS):
-            out_refs[i][...] = out_ref[i * block : (i + 1) * block]
-
-    def spec(*shape):
-        return pl.BlockSpec(shape, lambda i, p: (0,) * len(shape))
-
-    outs = pl.pallas_call(
-        body,
-        grid_spec=pltpu.PrefetchScalarGridSpec(
-            num_scalar_prefetch=1,
-            grid=(1,),
-            in_specs=[spec(3, rows, width)] * n,
-            out_specs=[spec(block, width)] * PARTS + [spec(length, width)] * 3,
-            scratch_shapes=[pltpu.VMEM((length, width), BF16)],
-        ),
-        out_shape=[jax.ShapeDtypeStruct((block, width), BF16)] * PARTS
-        + [jax.ShapeDtypeStruct((length, width), BF16)] * 3,
+            in_specs=[spec(*x.shape) for x in inputs],
+            out_specs=[spec(length // PARTS, width)] + [spec(*k) for k in kept],
+        ),
+        out_shape=[out_of(length // PARTS, width)] + [out_of(*k) for k in kept],
         compiler_params=params(),
         cost_estimate=cost(
-            4 * length * length * width, 14 * length * width, length * length * width // HEAD_DIM
+            4 * length * length * width // PARTS,
+            10 * length * width,
+            length * length * width // HEAD_DIM // PARTS,
         ),
         name="attention_heads",
-    )(place, *pieces)
-    return list(outs[:PARTS]), list(outs[PARTS:])
-
-
-def attention_grad_call(place, kept, attention, d_terms, n):
+    )(place, *inputs)
+    return outs[0], list(outs[1:])
+
+
+def attention_grad_call(place, kept, attention, parts, d_terms, n):
     length, width = kept[0].shape
     rows, block = length // n, length // PARTS
     n_terms = len(d_terms)
@@ -145,14 +148,14 @@
 
     def body(place_ref, *refs):
         kept_refs, attn_refs = refs[:3], refs[3 : 3 + PARTS]
-        term_refs = refs[3 + PARTS : 3 + PARTS * (1 + n_terms)]
-        out_refs, (attn_held, d_held) = refs[3 + PARTS * (1 + n_terms) : -2], refs[-2:]
+        part_ref, term_refs = refs[3 + PARTS], refs[4 + PARTS : 4 + PARTS * (1 + n_terms)]
+        out_refs, (attn_held, d_held) = refs[4 + PARTS * (1 + n_terms) : -2], refs[-2:]
         places = slab_rows(place_ref[0], n, rows)
         for i in range(PARTS):
             here = slice(i * block, (i + 1) * block)
             attn_held[here] = attn_refs[i][...]
             terms = [term_refs[t * PARTS + i][...].astype(F32) for t in range(n_terms)]
-            d_held[here] = sum(terms).astype(BF16)
+            d_held[here] = sum(terms, part_ref[i, 0].astype(F32)).astype(BF16)
         for lanes in head_lanes(width):
             q, k, v = (r[:, lanes] for r in kept_refs)
             attn = jnp.concatenate([attn_held[p, lanes] for p in places], axis=0).astype(F32)
@@ -180,7 +183,10 @@
         grid_spec=pltpu.PrefetchScalarGridSpec(
             num_scalar_prefetch=1,
             grid=(1,),
-            in_specs=[spec(length, width)] * 3 + [spec(block, width)] * (PARTS * (1 + n_terms)),
+            in_specs=[spec(length, width)] * 3
+            + [spec(block, width)] * PARTS
+            + [spec(PARTS, 1, block, width)]
+            + [spec(block, width)] * (PARTS * n_terms),
             out_specs=[spec(3, rows, width)] * n,
             scratch_shapes=[pltpu.VMEM((length, width), BF16)] * 2,
         ),
@@ -190,7 +196,7 @@
             200 * length * length * width, 24 * length * width, length * length * width // HEAD_DIM
         ),
         name="attention_heads_grad",
-    )(place, *kept, *attention, *sum(d_terms, []))
+    )(place, *kept, *attention, parts, *sum(d_terms, []))
 
 
 def ahead(place_ref, s, n):
@@ -202,28 +208,40 @@
     return jnp.where(place_ref[1] == 0, place_ref[0], n - 1 - place_ref[0])
 
 
-def fetch_weight(shard_refs, held, sems, place_ref):
+def weight_steps(place_ref, shard_refs, held, sems, n):
     core, index = place_ref[1], place_ref[2]
     own, one, two, own_o, one_o, two_o = shard_refs
-    first, second = jnp.where(core == 0, 2, 4), jnp.where(core == 0, 4, 2)
-    places = [
-        (own, 0),
-        (own_o, 1),
-        (one, first),
-        (one_o, second + 1),
-        (two.at[0], second),
-        (two_o.at[0], first + 1),
-        (two.at[1], 6),
-        (two_o.at[1], 7),
+    first, second = jnp.where(core == 0, 1, 2), jnp.where(core == 0, 2, 1)
+    pairs = [
+        (own, own_o, 0),
+        (one, two_o.at[0], first),
+        (two.at[0], one_o, second),
+        (two.at[1], two_o.at[1], 3),
     ]
-    for ref, step in places:
-        owner = index ^ step
-        pltpu.make_async_copy(ref, held.at[owner], sems.at[owner]).start()
-
-
-def wait_weight(shard_refs, held, sems, first, count):
-    for i in range(count):
-        pltpu.make_async_copy(shard_refs[0], held.at[first + i], sems.at[first + i]).wait()
+
+    def copies(i):
+        mine, other, _ = pairs[i]
+        return [
+            pltpu.make_async_copy(mine, held.at[i, core], sems.at[i, 0]),
+            pltpu.make_async_copy(other, held.at[i, 1 - core], sems.at[i, 1]),
+        ]
+
+    for i in range(2):
+        for c in copies(i):
+            c.start()
+    for i in range(n):
+        for c in copies(i):
+            c.wait()
+        if i + 2 < n:
+            for c in copies(i + 2):
+                c.start()
+        chip = (index // 2) ^ pairs[i][2]
+        me = place_ref[0]
+        yield i, lax.rem(jnp.where(core == 0, chip + n - me, me + n - chip), n)
+
+
+def weight_scratch(n, rows, cols):
+    return [pltpu.VMEM((n, 2, rows, cols), BF16), pltpu.SemaphoreType.DMA((n, 2))]
 
 
 def fetch_heads(own, left, right, held, sems, pos, n):
@@ -258,74 +276,65 @@
     return own, lists[:groups], lists[groups:]
 
 
-def gated(d_ref, gate_ref):
-    return (d_ref[...].astype(F32) * gate_ref[...]).astype(BF16)
-
-
-def d_attn_parts_call(place, grad_out, gate_row, shards, n):
-    length, cols = grad_out.shape
+def d_attn_parts_call(place, d_proj, shards, n):
+    length, cols = d_proj.shape
     rows, n_shards = shards[0].shape[0], len(shards)
-    width = 2 * rows
-    dp, per, block = 2 * n, 2, length // PARTS
-
-    def body(place_ref, d_ref, gate_ref, *refs):
-        shard_refs, out_refs, (held, sems) = refs[:n_shards], refs[n_shards:-2], refs[-2:]
-        fetch_weight(shard_refs, held, sems, place_ref)
-        d_proj = gated(d_ref, gate_ref)
-        for s in (n - 1, *range(1, n - 1), 0):
-            first = ahead(place_ref, s, n) * per
-            wait_weight(shard_refs, held, sems, first, per)
-            part = dot(d_proj, held[pl.ds(first, per)].reshape(width, cols), ((1,), (1,)))
+    width, block = 2 * rows, length // PARTS
+
+    def body(place_ref, d_ref, *refs):
+        shard_refs, (out_ref, held, sems, ready, out_sems) = refs[:n_shards], refs[n_shards:]
+        copies = []
+        for i, s in weight_steps(place_ref, shard_refs, held, sems, n):
+            rows_here = held[i].reshape(width, cols)
+            for j in range(0, width, 256):
+                part = dot(d_ref[...], rows_here[j : j + 256], ((1,), (1,)))
+                ready[i, :, j : min(j + 256, width)] = part.astype(BF16)
             for g in range(PARTS):
-                out_refs[g * n + s][...] = part[g * block : (g + 1) * block].astype(BF16)
-
-    outs = pl.pallas_call(
+                source = ready.at[i, pl.ds(g * block, block)]
+                copies.append(pltpu.make_async_copy(source, out_ref.at[g, s], out_sems.at[i, g]))
+                copies[-1].start()
+        for c in copies:
+            c.wait()
+
+    return pl.pallas_call(
         body,
         grid_spec=pltpu.PrefetchScalarGridSpec(
             num_scalar_prefetch=1,
             grid=(1,),
-            in_specs=[
-                pl.BlockSpec((length, cols), lambda i, p: (0, 0)),
-                pl.BlockSpec((1, cols), lambda i, p: (0, 0)),
-            ]
-            + any_specs(n_shards),
-            out_specs=[pl.BlockSpec((block, width), lambda i, p: (0, 0))] * (PARTS * n),
-            scratch_shapes=[pltpu.VMEM((dp, rows, cols), BF16), pltpu.SemaphoreType.DMA((dp,))],
-        ),
-        out_shape=[jax.ShapeDtypeStruct((block, width), BF16)] * (PARTS * n),
+            in_specs=[pl.BlockSpec((length, cols), lambda i, p: (0, 0))] + any_specs(n_shards),
+            out_specs=pl.BlockSpec(memory_space=pl.ANY),
+            scratch_shapes=weight_scratch(n, rows, cols)
+            + [
+                pltpu.VMEM((n, length, width), BF16),
+                pltpu.SemaphoreType.DMA((n, PARTS)),
+            ],
+        ),
+        out_shape=jax.ShapeDtypeStruct((PARTS, n, block, width), BF16),
         compiler_params=params(),
         cost_estimate=cost(
             2 * length * cols * width * n, 2 * (length * cols + n * width * (cols + length))
         ),
         name="d_attn_parts",
-    )(place, grad_out, gate_row, *shards)
-    return [outs[g * n : (g + 1) * n] for g in range(PARTS)]
-
-
-def heads_scratch(n, length, width):
-    return [pltpu.VMEM((n, length, width), BF16), pltpu.SemaphoreType.DMA((n, PARTS))]
+    )(place, d_proj, *shards)
 
 
 def projection_call(place, own, behind, front, shards, gate_row, n):
-    groups = len(own)
-    length, width = groups * own[0].shape[0], own[0].shape[1]
+    length, width = PARTS * own[0].shape[0], own[0].shape[1]
     n_shards, (rows, cols) = len(shards), shards[0].shape
-    dp, per, count = n * width // rows, width // rows, groups * (2 * n - 1)
+    count = PARTS * (2 * n - 1)
 
     def body(place_ref, gate_ref, *refs):
-        heads = split_heads_refs(refs[:count], groups, n)
+        heads = split_heads_refs(refs[:count], PARTS, n)
         shard_refs = refs[count : count + n_shards]
         out_ref, w_held, w_sems, held, sems = refs[count + n_shards :]
         fetch_heads(*heads, held, sems, position(place_ref, n), n)
-        fetch_weight(shard_refs, w_held, w_sems, place_ref)
         total = None
-        for s in range(n):
-            first = ahead(place_ref, s, n) * per
-            wait_heads(heads[0], held, sems, s)
-            wait_weight(shard_refs, w_held, w_sems, first, per)
-            block = w_held[pl.ds(first, per)].reshape(width, cols)
-            term = dot(held[s], block, ((1,), (0,)))
-            total = term if s == 0 else total + term
+        for i, s in weight_steps(place_ref, shard_refs, w_held, w_sems, n):
+            if i == 0:
+                for j in range(n):
+                    wait_heads(heads[0], held, sems, j)
+            term = dot(held[s], w_held[i].reshape(width, cols), ((1,), (0,)))
+            total = term if i == 0 else total + term
         out_ref[...] = (total * gate_ref[...]).astype(BF16)
 
     return pl.pallas_call(
@@ -335,11 +344,10 @@
             grid=(1,),
             in_specs=[pl.BlockSpec((1, cols), lambda i, p: (0, 0))] + any_specs(count + n_shards),
             out_specs=pl.BlockSpec((length, cols), lambda i, p: (0, 0)),
-            scratch_shapes=[
-                pltpu.VMEM((dp, rows, cols), BF16),
-                pltpu.SemaphoreType.DMA((dp,)),
+            scratch_shapes=weight_scratch(n, rows, cols)
+            + [
                 pltpu.VMEM((n, length, width), BF16),
-                pltpu.SemaphoreType.DMA((n, groups)),
+                pltpu.SemaphoreType.DMA((n, PARTS)),
             ],
         ),
         out_shape=jax.ShapeDtypeStruct((length, cols), BF16),
@@ -351,13 +359,13 @@
     )(place, gate_row, *own, *sum(behind, []), *sum(front, []), *shards)
 
 
-def weight_grad_call(place, steps, items, grad_out, gate_row, n, begun=None):
+def weight_grad_call(place, steps, items, d_proj, n):
     block, width = items[0][0][0].shape
-    length, cols = PARTS * block, grad_out.shape[1]
+    length, cols = PARTS * block, d_proj.shape[1]
     rows, many = width // 2, len(steps)
 
-    def body(place_ref, d_ref, gate_ref, *refs):
-        keep_ref, send_ref, d_proj, held, sems = refs[-5:]
+    def body(place_ref, d_ref, *refs):
+        keep_ref, send_ref, held, sems = refs[-4:]
         i = pl.program_id(0)
         pos = position(place_ref, n)
 
@@ -376,12 +384,10 @@
                     def _():
                         pltpu.make_async_copy(behind, there, sems.at[j, g]).start()
 
-            d_proj[...] = gated(d_ref, gate_ref)
-
         for g in range(PARTS):
             there = held.at[i, pl.ds(g * block, block)]
             pltpu.make_async_copy(refs[0], there, sems.at[i, g]).wait()
-        term = dot(held[i], d_proj[...], ((0,), (0,))).astype(BF16)
+        term = dot(held[i], d_ref[...], ((0,), (0,))).astype(BF16)
         first = place_ref[1] == 0
         keep_ref[0] = jnp.where(first, term[:rows], term[rows:])
         send_ref[0] = jnp.where(first, term[rows:], term[:rows])
@@ -396,33 +402,27 @@
         return pl.BlockSpec((1, rows, cols), slot)
 
     flat = [x for item in items for pair in item for x in pair]
-    begun = list(begun or ())
     return pl.pallas_call(
         body,
         grid_spec=pltpu.PrefetchScalarGridSpec(
             num_scalar_prefetch=1,
             grid=(many,),
-            in_specs=[
-                pl.BlockSpec((length, cols), lambda s, p: (0, 0)),
-                pl.BlockSpec((1, cols), lambda s, p: (0, 0)),
-            ]
-            + any_specs(len(flat) + len(begun)),
+            in_specs=[pl.BlockSpec((length, cols), lambda s, p: (0, 0))]
+            + any_specs(len(flat)),
             out_specs=[out_spec(0), out_spec(1)],
             scratch_shapes=[
-                pltpu.VMEM((length, cols), BF16),
                 pltpu.VMEM((many, length, width), BF16),
                 pltpu.SemaphoreType.DMA((many, PARTS)),
             ],
         ),
         out_shape=[jax.ShapeDtypeStruct((n, rows, cols), BF16)] * 2,
-        input_output_aliases={3 + len(flat) + i: i for i in range(len(begun))},
         compiler_params=params(),
         cost_estimate=cost(
             2 * length * cols * width * many,
             2 * (length * cols + many * width * (cols + 2 * length)),
         ),
         name="weight_grad",
-    )(place, grad_out, gate_row, *flat, *begun)
+    )(place, d_proj, *flat)
 
 
 def assemble_call(place, pieces):
@@ -430,22 +430,30 @@
     _, rows, width = pieces[0].shape
 
     def body(place_ref, *refs):
-        for t in range(3):
-            for s in range(n):
-                start = lax.rem(place_ref[0] + s, n) * width
-                lanes = pl.ds(pl.multiple_of(start, HEAD_DIM), width)
-                refs[n + t][:, lanes] = refs[s][t]
+        outs, sems = refs[n : n + 3], refs[n + 3]
+        copies = []
+        for s in range(n):
+            start = lax.rem(place_ref[0] + s, n) * width
+            lanes = pl.ds(pl.multiple_of(start, HEAD_DIM), width)
+            for t in range(3):
+                copies.append(
+                    pltpu.make_async_copy(refs[s].at[t], outs[t].at[:, lanes], sems.at[s, t])
+                )
+                copies[-1].start()
+        for c in copies:
+            c.wait()
 
     return pl.pallas_call(
         body,
         grid_spec=pltpu.PrefetchScalarGridSpec(
             num_scalar_prefetch=1,
             grid=(1,),
-            in_specs=[pl.BlockSpec((3, rows, width), lambda i, p: (0, 0, 0))] * n,
-            out_specs=[pl.BlockSpec((rows, n * width), lambda i, p: (0, 0))] * 3,
+            in_specs=[pl.BlockSpec((3, rows, width), lambda i, me: (0, 0, 0))] * n,
+            out_specs=any_specs(3),
+            scratch_shapes=[pltpu.SemaphoreType.DMA((n, 3))],
         ),
         out_shape=[jax.ShapeDtypeStruct((rows, n * width), BF16)] * 3,
-        compiler_params=params(32),
+        compiler_params=params(),
         cost_estimate=cost(0, 12 * n * rows * width),
         name="assemble_heads",
     )(place, *pieces)
@@ -476,7 +484,7 @@
     return lax.ppermute(x, (dp_axis, axis), pairs)
 
 
-def line_payload(place, got, parts, t, n):
+def line_payload(place, got, parts, g, t, n):
     shape = got[0].shape
 
     def body(place_ref, forward, back, part_f, part_b, out_f, out_b):
@@ -492,19 +500,26 @@
 
             @pl.when(jnp.logical_not(passes))
             def _():
-                out[...] = add_rounded(part[...], x[...])
+                out[...] = add_rounded(part[0, 0], x[...])
 
     block = pl.BlockSpec(shape, lambda i, p: (0, 0))
+
+    def term(s):
+        return pl.BlockSpec((1, 1, *shape), lambda i, p: (g, s, 0, 0))
+
     return pl.pallas_call(
         body,
         grid_spec=pltpu.PrefetchScalarGridSpec(
-            num_scalar_prefetch=1, grid=(1,), in_specs=[block] * 4, out_specs=[block] * 2
+            num_scalar_prefetch=1,
+            grid=(1,),
+            in_specs=[block, block, term(n - t), term(t)],
+            out_specs=[block] * 2,
         ),
         out_shape=[jax.ShapeDtypeStruct(shape, BF16)] * 2,
         compiler_params=params(8),
         cost_estimate=cost(0, 12 * got[0].size),
         name="line_payload",
-    )(place, *got, parts[n - t], parts[t])
+    )(place, *got, parts, parts)
 
 
 def after(x, done):
@@ -517,16 +532,18 @@
     index = lax.axis_index("dp").astype(jnp.int32)
     place = jnp.stack([me, index % 2, index])
 
-    packed = pack_call(place, query, key_in, value, n)
+    packed = pack_call(query, key_in, value, "ctx")
     pieces = [packed[0]] + [shift(packed[s], "ctx", s) for s in range(1, n)]
     gate_row = lax.dynamic_slice_in_dim(gate_table, timestep[0], 1, 0)
 
     one = chip_swap(after(out_weight, packed), "dp", 0)
     two = chip_swap(after(jnp.stack([out_weight, one]), pieces[1]), "dp", 1)
-    shards = [out_weight, one, after(two, pieces[2])]
+    d_proj = (grad_out[0].astype(F32) * gate_row).astype(BF16)
+    shards = [out_weight, one, after(two, (pieces[2], d_proj))]
     shards = shards + [swap(x, "dp", 1) for x in shards]
-    parts = d_attn_parts_call(place, grad_out[0], gate_row, shards, n)
-    attention, kept = attention_call(place, after(pieces, parts))
+    parts = d_attn_parts_call(place, d_proj, shards, n)
+    attended, kept = attention_call(place, after(pieces, parts), 0, n)
+    attention = [attended] + [attention_call(place, kept, g, n)[0] for g in range(1, PARTS)]
 
     def both_ways(forward, back):
         return line_move(forward, "dp", "ctx", True), line_move(back, "dp", "ctx", False)
@@ -537,25 +554,18 @@
         return [(got[g][n - s - 1][0], got[g][s - 1][1]) for g in range(PARTS)]
 
     got = [[both_ways(a, a)] for a in attention]
-    begun = None
     for t in range(1, n):
-        sent = [line_payload(place, got[g][-1], parts[g], t, n) for g in range(PARTS)]
+        sent = [line_payload(place, got[g][-1], parts, g, t, n) for g in range(PARTS)]
         for g in range(PARTS):
             got[g].append(both_ways(*sent[g]))
-        if t > 1:
-            steps = [s for s in range(n) if max(s, n - s) <= t and max(s, n - s) > t - 1]
-            steps = [0] * (t == 2) + steps
-            begun = weight_grad_call(
-                place, steps, [items(s) for s in steps], grad_out[0], gate_row, n, begun
-            )
-    keep, send = begun
+    steps = sorted(range(n), key=lambda s: max(s, n - s) if s else 0)
+    keep, send = weight_grad_call(place, steps, [items(s) for s in steps], d_proj, n)
     received = swap(send, "dp", 1)
     behind = [[got[g][i][0] for i in range(n - 1)] for g in range(PARTS)]
     front = [[got[g][i][1] for i in range(n - 1)] for g in range(PARTS)]
-    d_terms = [[parts[g][0] for g in range(PARTS)]]
-    d_terms += [[got[g][-1][i] for g in range(PARTS)] for i in range(2)]
-
-    grads = attention_grad_call(place, kept, attention, d_terms, n)
+    d_terms = [[got[g][-1][i] for g in range(PARTS)] for i in range(2)]
+
+    grads = attention_grad_call(place, kept, attention, parts, d_terms, n)
     received = after(received, grads)
     far = add_rounded(keep[2:], received[2:])
     grads = [grads[0]] + [shift(grads[s], "ctx", -s) for s in range(1, n)]

time: 195 us -> 189 us (0.969)
  starting transfers between devices: 55.4 us -> 47.3 us
  other arithmetic: 4.28 us -> 7.48 us
    ppermute x16, starting transfers between devices: 39.7 us -> 31.6 us  [line_move(): return lax.ppermute(x, (dp_axis, axis), pairs)]
    ppermute x6, waiting for transfers between devices: 58.7 us -> 52.5 us  [shift(): return lax.ppermute(x, axis, [(i, (i + by) % n) for i in range(n)])]
    ppermute x16, waiting for transfers between devices: 14.6 us -> 18.7 us  [line_move(): return lax.ppermute(x, (dp_axis, axis), pairs)]
    convert_element_type x0 -> x1, other arithmetic: none -> 2.59 us  [by_heads(): d_proj = (grad_out[0].astype(F32) * gate_row).astype(BF16)]
    pallas_call x1 -> x2, Pallas kernels: 4.58 us -> 6.99 us  [attention_call(): pl.pallas_call(body, grid_spec=pltpu.PrefetchScalarGridSpec(num_scalar_pr...]
    pallas_call x2 -> x1, Pallas kernels: 6.94 us -> 6.01 us  [weight_grad_call(): pl.pallas_call(body, grid_spec=pltpu.PrefetchScalarGridSpec(num_scalar_pr...]
  transfers between devices with their start and end apart: 30 -> 30, of which waited for: 15 -> 15; matrix products, arithmetic and copies ran while one was open for 2% -> 4% of each run, Pallas kernels for 18% -> 20%
where the time goes in v4:
time: 189 us
  waiting for transfers between devices  82.9 us (44%)
  starting transfers between devices  47.3 us (25%)
  Pallas kernels  46 us (24%)
  other arithmetic  7.48 us (4%)
  local copies, waits for them, and re-layouts  3 us (2%)
    ppermute x6, waiting for transfers between devices, shift(): return lax.ppermute(x, axis, [(i, (i + by) % n) for i in range(n)])  52.5 us
    ppermute x16, starting transfers between devices, line_move(): return lax.ppermute(x, (dp_axis, axis), pairs)  31.6 us
    ppermute x16, waiting for transfers between devices, line_move(): return lax.ppermute(x, (dp_axis, axis), pairs)  18.7 us
    ppermute x6, starting transfers between devices, shift(): return lax.ppermute(x, axis, [(i, (i + by) % n) for i in range(n)])  10.3 us
    pallas_call x1, Pallas kernels, projection_call(): pl.pallas_call(body, grid_spec=pltpu.PrefetchScalarGridSpec(num_scalar_pr...  9.48 us
    pallas_call x1, Pallas kernels, d_attn_parts_call(): pl.pallas_call(body, grid_spec=pltpu.PrefetchScalarGridSpec(num_scalar_pr...  9.08 us
    ppermute x4, waiting for transfers between devices, chip_swap(): lax.ppermute(x, axis, [(i, i ^ (2 if (i + step) % 2 == 0 else 4)) for i i...  8.96 us
    pallas_call x2, Pallas kernels, attention_call(): pl.pallas_call(body, grid_spec=pltpu.PrefetchScalarGridSpec(num_scalar_pr...  6.99 us
  transfers between devices with their start and end apart: 30, of which 15 were waited for; matrix products, arithmetic and copies ran while one was open for 4% of the time, Pallas kernels for 20%

profile of v4, /device:TPU:0, one launch (start us, length us, event | category | flops | bytes accessed | tf_op | source)
XLA Modules:
  0.0 188.6 jit_solution(15243826626472031682)
XLA Ops:
  0.6 2.5 %pack_heads.1 = (bf16[3,128,640]{2,1,0:T(8,128)(2,1)}, bf16[3,128,640]{2,1,0:T(8,128)(2,1)}, bf16[3,128,640]{2,1,0:T(8,128)(2,1)}, bf16[3,128,640]{2,1,0:T(8,128)(2,1)}) custom-call(bf16[1,128,2560]{2,1,0:T(8,128)(2,1)} %refs_0_.2, bf16[1,128,2560]{2,1,0:T(8,128)(2,1)} %refs_1_.1, bf16[1,128,2560]{2,1,0:T(8,128)(2,1)} %refs_2_.1), custom_call_target="tpu_custom_call" | custom-call | bytes 3932160 | tf_op jit(solution)/shard_map/pack_heads/pallas_call | solution.py:77
  3.1 3.0 %collective-permute-start.3 = (bf16[320,1280]{1,0:T(8,128)(2,1)}, bf16[320,1280]{1,0:T(8,128)(2,1)S(1)}, u32[]{:S(2)}, u32[]{:S(2)}) collective-permute-start(bf16[320,1280]{1,0:T(8,128)(2,1)} %refs_14_.1), channel_id=1, source_target_pairs={{0,8},{4,20},{8,0},{12,28},{16,24},{20,4},{24,16},{28,12},{1,9},{5... | collective-permute-start | bytes 2457608 | tf_op jit(solution)/shard_map/ppermute | solution.py:474
  7.7 9.0 %collective-permute-done.3.refs_1_.refs_15_ = bf16[320,1280]{1,0:T(8,128)(2,1)S(1)} collective-permute-done((bf16[320,1280]{1,0:T(8,128)(2,1)}, bf16[320,1280]{1,0:T(8,128)(2,1)S(1)}, u32[]{:S(2)}, u32[]{:S(2)}) %collective-permute-start.3) | collective-permute-done | bytes 819232 | tf_op jit(solution)/shard_map/ppermute | solution.py:474
  16.7 2.5 %pad_maximum_fusion = bf16[2,320,1280]{2,1,0:T(8,128)(2,1)} fusion(bf16[1,320,1280]{2,1,0:T(8,128)(2,1)S(1)} %bitcast.23, bf16[1,320,1280]{2,1,0:T(8,128)(2,1)} %bitcast.22), kind=kLoop, calls=%fused_computation.7 | loop fusion | flops 819200 | bytes 3276800 | tf_op jit(solution)/shard_map/stack | solution.py:540
  22.2 2.4 %collective-permute-start.1 = (bf16[3,128,640]{2,1,0:T(8,128)(2,1)}, bf16[3,128,640]{2,1,0:T(8,128)(2,1)}, u32[]{:S(2)}, u32[]{:S(2)}) collective-permute-start(bf16[3,128,640]{2,1,0:T(8,128)(2,1)} %get-tuple-element.50), channel_id=1, source_target_pairs={{0,2},{1,3},{2,0},{3,1},{4,6},{5,7},{6,4},{7,5},{8,10},{9,11},{10,... | collective-permute-start | bytes 1474568 | tf_op jit(solution)/shard_map/ppermute | solution.py:464
  26.1 2.6 %fusion.d_ref = bf16[512,1280]{1,0:T(8,128)(2,1)} fusion(bf16[1,512,1280]{2,1,0:T(8,128)(2,1)} %param.13, f32[1280]{0:T(1024)S(1)} %get-tuple-element.91), kind=kLoop, calls=%fused_computation.3 | loop fusion | flops 1966080 | bytes 2626560 | tf_op jit(solution)/shard_map/convert_element_type | solution.py:541
  28.7 18.0 %collective-permute-done.1.refs_2_ = bf16[3,128,640]{2,1,0:T(8,128)(2,1)} collective-permute-done((bf16[3,128,640]{2,1,0:T(8,128)(2,1)}, bf16[3,128,640]{2,1,0:T(8,128)(2,1)}, u32[]{:S(2)}, u32[]{:S(2)}) %collective-permute-start.1) | collective-permute-done | bytes 491552 | tf_op jit(solution)/shard_map/ppermute | solution.py:464
  47.3 2.5 %collective-permute-start.2 = (bf16[3,128,640]{2,1,0:T(8,128)(2,1)}, bf16[3,128,640]{2,1,0:T(8,128)(2,1)}, u32[]{:S(2)}, u32[]{:S(2)}) collective-permute-start(bf16[3,128,640]{2,1,0:T(8,128)(2,1)} %get-tuple-element.51), channel_id=1, source_target_pairs={{0,3},{1,0},{2,1},{3,2},{4,7},{5,4},{6,5},{7,6},{8,11},{9,8},{10,9... | collective-permute-start | bytes 1474568 | tf_op jit(solution)/shard_map/ppermute | solution.py:464
  54.0 9.1 %d_attn_parts.1.part_f.part_b.refs_5_ = bf16[2,4,256,640]{3,2,1,0:T(8,128)(2,1)S(1)} custom-call(s32[3]{0:T(128)S(1)} %pad_add_fusion.place_ref, bf16[512,1280]{1,0:T(8,128)(2,1)S(1)} %copy-done.1, bf16[320,1280]{1,0:T(8,128)(2,1)S(1)} %copy-done, bf16[320,1280]{1,0:T(8,128)(2,1)S(1)} %collective-permute-done.3.refs_1_.refs_15_, ...), custom_call_target="tpu_custom_call" | custom-call | flops 3355443200 | bytes 10485760 | tf_op jit(solution)/shard_map/d_attn_parts/pallas_call | solution.py:299
  63.1 4.1 %attention_heads.2 = (bf16[256,640]{1,0:T(8,128)(2,1)S(1)}, bf16[512,640]{1,0:T(8,128)(2,1)S(1)}, bf16[512,640]{1,0:T(8,128)(2,1)S(1)}, bf16[512,640]{1,0:T(8,128)(2,1)S(1)}) custom-call(s32[3]{0:T(128)S(1)} %pad_add_fusion.place_ref, bf16[3,128,640]{2,1,0:T(8,128)(2,1)S(1)} %copy-done.3, bf16[3,128,640]{2,1,0:T(8,128)(2,1)S(1)} %copy-done.5, ...), custom_call_target="tpu_custom_call" | custom-call | flops 335544320 | bytes 3276800 | tf_op jit(solution)/shard_map/attention_heads/pallas_call | solution.py:123
  68.6 4.6 %collective-permute-start.8 = (bf16[256,640]{1,0:T(8,128)(2,1)S(1)}, bf16[256,640]{1,0:T(8,128)(2,1)S(1)}, u32[]{:S(2)}, u32[]{:S(2)}) collective-permute-start(bf16[256,640]{1,0:T(8,128)(2,1)S(1)} %get-tuple-element.59.refs_0_.refs_1_.refs_3_), channel_id=1, source_target_pairs={{0,1},{1,2},{2,3},{5,4},{6,5},{7,6},{8,9},{9,10},{10,11},{13,12},{... | collective-permute-start | bytes 983048 | tf_op jit(solution)/shard_map/ppermute | solution.py:484
  73.2 2.9 %attention_heads.3.refs_2_.refs_3_.refs_4_.refs_1_ = bf16[256,640]{1,0:T(8,128)(2,1)S(1)} custom-call(s32[3]{0:T(128)S(1)} %pad_add_fusion.place_ref, bf16[512,640]{1,0:T(8,128)(2,1)S(1)} %get-tuple-element.60.refs_0_, bf16[512,640]{1,0:T(8,128)(2,1)S(1)} %get-tuple-element.61.refs_1_, bf16[512,640]{1,0:T(8,128)(2,1)S(1)} %get-tuple-element.62.refs_2_), custom_call_target="tpu_custom_call" | custom-call | flops 335544320 | bytes 3276800 | tf_op jit(solution)/shard_map/attention_heads/pallas_call | solution.py:123
  77.3 4.6 %collective-permute-start.12 = (bf16[256,640]{1,0:T(8,128)(2,1)S(1)}, bf16[256,640]{1,0:T(8,128)(2,1)S(1)}, u32[]{:S(2)}, u32[]{:S(2)}) collective-permute-start(bf16[256,640]{1,0:T(8,128)(2,1)S(1)} %attention_heads.3.refs_2_.refs_3_.refs_4_.refs_1_), channel_id=1, source_target_pairs={{0,1},{1,2},{2,3},{5,4},{6,5},{7,6},{8,9},{9,10},{10,11},{13,12},{... | collective-permute-start | bytes 983048 | tf_op jit(solution)/shard_map/ppermute | solution.py:484
  85.8 2.5 %collective-permute-done.13.back.refs_11_ = bf16[256,640]{1,0:T(8,128)(2,1)S(1)} collective-permute-done((bf16[256,640]{1,0:T(8,128)(2,1)S(1)}, bf16[256,640]{1,0:T(8,128)(2,1)S(1)}, u32[]{:S(2)}, u32[]{:S(2)}) %collective-permute-start.13) | collective-permute-done | bytes 327712 | tf_op jit(solution)/shard_map/ppermute | solution.py:484
  88.9 3.0 %collective-permute-start.14 = (bf16[256,640]{1,0:T(8,128)(2,1)S(1)}, bf16[256,640]{1,0:T(8,128)(2,1)S(1)}, u32[]{:S(2)}, u32[]{:S(2)}) collective-permute-start(bf16[256,640]{1,0:T(8,128)(2,1)S(1)} %get-tuple-element.65), channel_id=1, source_target_pairs={{0,1},{1,2},{2,3},{5,4},{6,5},{7,6},{8,9},{9,10},{10,11},{13,12},{... | collective-permute-start | bytes 983048 | tf_op jit(solution)/shard_map/ppermute | solution.py:484
  93.5 3.5 %collective-permute-done.11.back.refs_5_.refs_9_ = bf16[256,640]{1,0:T(8,128)(2,1)S(1)} collective-permute-done((bf16[256,640]{1,0:T(8,128)(2,1)S(1)}, bf16[256,640]{1,0:T(8,128)(2,1)S(1)}, u32[]{:S(2)}, u32[]{:S(2)}) %collective-permute-start.11) | collective-permute-done | bytes 327712 | tf_op jit(solution)/shard_map/ppermute | solution.py:484
  101.2 3.3 %collective-permute-done.15.back.refs_7_.refs_12_ = bf16[256,640]{1,0:T(8,128)(2,1)S(1)} collective-permute-done((bf16[256,640]{1,0:T(8,128)(2,1)S(1)}, bf16[256,640]{1,0:T(8,128)(2,1)S(1)}, u32[]{:S(2)}, u32[]{:S(2)}) %collective-permute-start.15) | collective-permute-done | bytes 327712 | tf_op jit(solution)/shard_map/ppermute | solution.py:484
  108.2 4.2 %collective-permute-done.18.refs_13_.back.refs_10_ = bf16[256,640]{1,0:T(8,128)(2,1)S(1)} collective-permute-done((bf16[256,640]{1,0:T(8,128)(2,1)S(1)}, bf16[256,640]{1,0:T(8,128)(2,1)S(1)}, u32[]{:S(2)}, u32[]{:S(2)}) %collective-permute-start.18) | collective-permute-done | bytes 327712 | tf_op jit(solution)/shard_map/ppermute | solution.py:484
  116.0 3.4 %collective-permute-done.19.refs_15_.back.refs_13_ = bf16[256,640]{1,0:T(8,128)(2,1)S(1)} collective-permute-done((bf16[256,640]{1,0:T(8,128)(2,1)S(1)}, bf16[256,640]{1,0:T(8,128)(2,1)S(1)}, u32[]{:S(2)}, u32[]{:S(2)}) %collective-permute-start.19) | collective-permute-done | bytes 327712 | tf_op jit(solution)/shard_map/ppermute | solution.py:484
  123.1 6.0 %weight_grad.1 = (bf16[4,320,1280]{2,1,0:T(8,128)(2,1)S(1)}, bf16[4,320,1280]{2,1,0:T(8,128)(2,1)S(1)}) custom-call(s32[3]{0:T(128)S(1)} %pad_add_fusion.place_ref, bf16[512,1280]{1,0:T(8,128)(2,1)S(1)} %copy-done.2, bf16[256,640]{1,0:T(8,128)(2,1)S(1)} %get-tuple-element.59.refs_0_.refs_1_.refs_3_, ...), custom_call_target="tpu_custom_call" | custom-call | flops 3355443200 | bytes 13107200 | tf_op jit(solution)/shard_map/weight_grad/pallas_call | solution.py:405
  130.7 6.1 %attention_heads_grad.1 = (bf16[3,128,640]{2,1,0:T(8,128)(2,1)S(1)}, bf16[3,128,640]{2,1,0:T(8,128)(2,1)S(1)}, bf16[3,128,640]{2,1,0:T(8,128)(2,1)S(1)}, bf16[3,128,640]{2,1,0:T(8,128)(2,1)S(1)}) custom-call(s32[3]{0:T(128)S(1)} %pad_add_fusion.place_ref, bf16[512,640]{1,0:T(8,128)(2,1)S(1)} %get-tuple-element.60.refs_0_, ...), custom_call_target="tpu_custom_call" | custom-call | flops 33554432000 | bytes 7864320 | tf_op jit(solution)/shard_map/attention_heads_grad/pallas_call | solution.py:181
  139.3 22.7 %collective-permute-done.26.refs_2_ = bf16[3,128,640]{2,1,0:T(8,128)(2,1)S(1)} collective-permute-done((bf16[3,128,640]{2,1,0:T(8,128)(2,1)S(1)}, bf16[3,128,640]{2,1,0:T(8,128)(2,1)S(1)}, u32[]{:S(2)}, u32[]{:S(2)}) %collective-permute-start.26) | collective-permute-done | bytes 491552 | tf_op jit(solution)/shard_map/ppermute | solution.py:464
  165.7 9.5 %projection.1 = bf16[512,1280]{1,0:T(8,128)(2,1)} custom-call(s32[3]{0:T(128)S(1)} %pad_add_fusion.place_ref, f32[1,1280]{1,0:T(1,128)S(1)} %get-tuple-element.83.gate_ref, bf16[256,640]{1,0:T(8,128)(2,1)S(1)} %get-tuple-element.59.refs_0_.refs_1_.refs_3_, bf16[256,640]{1,0:T(8,128)(2,1)S(1)} %attention_heads.3.refs_2_.refs_3_.refs_4_.refs_1_, ...), custom_call_target="tpu_custom_call" | custom-call | flops 3355443200 | bytes 10485760 | tf_op jit(solution)/shard_map/projection/pallas_call | solution.py:340
  177.4 9.1 %collective-permute-done.28.refs_3_ = bf16[3,128,640]{2,1,0:T(8,128)(2,1)S(1)} collective-permute-done((bf16[3,128,640]{2,1,0:T(8,128)(2,1)S(1)}, bf16[3,128,640]{2,1,0:T(8,128)(2,1)S(1)}, u32[]{:S(2)}, u32[]{:S(2)}) %collective-permute-start.28) | collective-permute-done | bytes 491552 | tf_op jit(solution)/shard_map/ppermute | solution.py:464
  (70 shorter events, 45.7 us)
Async XLA Ops:
  3.1 13.5 %collective-permute-start.3 = (bf16[320,1280]{1,0:T(8,128)(2,1)}, bf16[320,1280]{1,0:T(8,128)(2,1)S(1)}, u32[]{:S(2)}, u32[]{:S(2)}) collective-permute-start(bf16[320,1280]{1,0:T(8,128)(2,1)} %refs_14_.1), channel_id=1, source_target_pairs={{0,8},{4,20},{8,0},{12,28},{16,24},{20,4},{24,16},{28,12},{1,9},{5... | collective-permute-start | bytes 2457608 | tf_op jit(solution)/shard_map/ppermute | solution.py:474
  6.2 14.8 %collective-permute-start = (bf16[3,128,640]{2,1,0:T(8,128)(2,1)}, bf16[3,128,640]{2,1,0:T(8,128)(2,1)S(1)}, u32[]{:S(2)}, u32[]{:S(2)}) collective-permute-start(bf16[3,128,640]{2,1,0:T(8,128)(2,1)} %get-tuple-element.49), channel_id=1, source_target_pairs={{0,1},{1,2},{2,3},{3,0},{4,5},{5,6},{6,7},{7,4},{8,9},{9,10},{10,1... | collective-permute-start | bytes 1474568 | tf_op jit(solution)/shard_map/ppermute | solution.py:464
  21.7 25.0 %collective-permute-start.4 = (bf16[2,320,1280]{2,1,0:T(8,128)(2,1)}, bf16[2,320,1280]{2,1,0:T(8,128)(2,1)S(1)}, u32[]{:S(2)}, u32[]{:S(2)}) collective-permute-start(bf16[2,320,1280]{2,1,0:T(8,128)(2,1)} %pad_maximum_fusion), channel_id=1, source_target_pairs={{0,16},{4,12},{8,24},{12,4},{16,0},{20,28},{24,8},{28,20},{1,17},{... | collective-permute-start | bytes 4915208 | tf_op jit(solution)/shard_map/ppermute | solution.py:474
  22.2 24.5 %collective-permute-start.1 = (bf16[3,128,640]{2,1,0:T(8,128)(2,1)}, bf16[3,128,640]{2,1,0:T(8,128)(2,1)}, u32[]{:S(2)}, u32[]{:S(2)}) collective-permute-start(bf16[3,128,640]{2,1,0:T(8,128)(2,1)} %get-tuple-element.50), channel_id=1, source_target_pairs={{0,2},{1,3},{2,0},{3,1},{4,6},{5,7},{6,4},{7,5},{8,10},{9,11},{10,... | collective-permute-start | bytes 1474568 | tf_op jit(solution)/shard_map/ppermute | solution.py:464
  47.3 15.8 %collective-permute-start.2 = (bf16[3,128,640]{2,1,0:T(8,128)(2,1)}, bf16[3,128,640]{2,1,0:T(8,128)(2,1)}, u32[]{:S(2)}, u32[]{:S(2)}) collective-permute-start(bf16[3,128,640]{2,1,0:T(8,128)(2,1)} %get-tuple-element.51), channel_id=1, source_target_pairs={{0,3},{1,0},{2,1},{3,2},{4,7},{5,4},{6,5},{7,6},{8,11},{9,8},{10,9... | collective-permute-start | bytes 1474568 | tf_op jit(solution)/shard_map/ppermute | solution.py:464
  67.3 14.6 %collective-permute-start.9 = (bf16[256,640]{1,0:T(8,128)(2,1)S(1)}, bf16[256,640]{1,0:T(8,128)(2,1)S(1)}, u32[]{:S(2)}, u32[]{:S(2)}) collective-permute-start(bf16[256,640]{1,0:T(8,128)(2,1)S(1)} %get-tuple-element.59.refs_0_.refs_1_.refs_3_), channel_id=1, source_target_pairs={{1,0},{2,1},{3,2},{4,5},{5,6},{6,7},{9,8},{10,9},{11,10},{12,13},{... | collective-permute-start | bytes 983048 | tf_op jit(solution)/shard_map/ppermute | solution.py:484
  68.6 13.3 %collective-permute-start.8 = (bf16[256,640]{1,0:T(8,128)(2,1)S(1)}, bf16[256,640]{1,0:T(8,128)(2,1)S(1)}, u32[]{:S(2)}, u32[]{:S(2)}) collective-permute-start(bf16[256,640]{1,0:T(8,128)(2,1)S(1)} %get-tuple-element.59.refs_0_.refs_1_.refs_3_), channel_id=1, source_target_pairs={{0,1},{1,2},{2,3},{5,4},{6,5},{7,6},{8,9},{9,10},{10,11},{13,12},{... | collective-permute-start | bytes 983048 | tf_op jit(solution)/shard_map/ppermute | solution.py:484
  76.0 12.2 %collective-permute-start.13 = (bf16[256,640]{1,0:T(8,128)(2,1)S(1)}, bf16[256,640]{1,0:T(8,128)(2,1)S(1)}, u32[]{:S(2)}, u32[]{:S(2)}) collective-permute-start(bf16[256,640]{1,0:T(8,128)(2,1)S(1)} %attention_heads.3.refs_2_.refs_3_.refs_4_.refs_1_), channel_id=1, source_target_pairs={{1,0},{2,1},{3,2},{4,5},{5,6},{6,7},{9,8},{10,9},{11,10},{12,13},{... | collective-permute-start | bytes 983048 | tf_op jit(solution)/shard_map/ppermute | solution.py:484
  77.3 10.9 %collective-permute-start.12 = (bf16[256,640]{1,0:T(8,128)(2,1)S(1)}, bf16[256,640]{1,0:T(8,128)(2,1)S(1)}, u32[]{:S(2)}, u32[]{:S(2)}) collective-permute-start(bf16[256,640]{1,0:T(8,128)(2,1)S(1)} %attention_heads.3.refs_2_.refs_3_.refs_4_.refs_1_), channel_id=1, source_target_pairs={{0,1},{1,2},{2,3},{5,4},{6,5},{7,6},{8,9},{9,10},{10,11},{13,12},{... | collective-permute-start | bytes 983048 | tf_op jit(solution)/shard_map/ppermute | solution.py:484
  82.6 10.9 %collective-permute-start.10 = (bf16[256,640]{1,0:T(8,128)(2,1)S(1)}, bf16[256,640]{1,0:T(8,128)(2,1)S(1)}, u32[]{:S(2)}, u32[]{:S(2)}) collective-permute-start(bf16[256,640]{1,0:T(8,128)(2,1)S(1)} %get-tuple-element.63), channel_id=1, source_target_pairs={{0,1},{1,2},{2,3},{5,4},{6,5},{7,6},{8,9},{9,10},{10,11},{13,12},{... | collective-permute-start | bytes 983048 | tf_op jit(solution)/shard_map/ppermute | solution.py:484
  84.5 12.5 %collective-permute-start.11 = (bf16[256,640]{1,0:T(8,128)(2,1)S(1)}, bf16[256,640]{1,0:T(8,128)(2,1)S(1)}, u32[]{:S(2)}, u32[]{:S(2)}) collective-permute-start(bf16[256,640]{1,0:T(8,128)(2,1)S(1)} %get-tuple-element.64), channel_id=1, source_target_pairs={{1,0},{2,1},{3,2},{4,5},{5,6},{6,7},{9,8},{10,9},{11,10},{12,13},{... | collective-permute-start | bytes 983048 | tf_op jit(solution)/shard_map/ppermute | solution.py:484
  88.9 12.3 %collective-permute-start.14 = (bf16[256,640]{1,0:T(8,128)(2,1)S(1)}, bf16[256,640]{1,0:T(8,128)(2,1)S(1)}, u32[]{:S(2)}, u32[]{:S(2)}) collective-permute-start(bf16[256,640]{1,0:T(8,128)(2,1)S(1)} %get-tuple-element.65), channel_id=1, source_target_pairs={{0,1},{1,2},{2,3},{5,4},{6,5},{7,6},{8,9},{9,10},{10,11},{13,12},{... | collective-permute-start | bytes 983048 | tf_op jit(solution)/shard_map/ppermute | solution.py:484
  91.9 12.5 %collective-permute-start.15 = (bf16[256,640]{1,0:T(8,128)(2,1)S(1)}, bf16[256,640]{1,0:T(8,128)(2,1)S(1)}, u32[]{:S(2)}, u32[]{:S(2)}) collective-permute-start(bf16[256,640]{1,0:T(8,128)(2,1)S(1)} %get-tuple-element.66), channel_id=1, source_target_pairs={{1,0},{2,1},{3,2},{4,5},{5,6},{6,7},{9,8},{10,9},{11,10},{12,13},{... | collective-permute-start | bytes 983048 | tf_op jit(solution)/shard_map/ppermute | solution.py:484
  97.7 10.5 %collective-permute-start.16 = (bf16[256,640]{1,0:T(8,128)(2,1)S(1)}, bf16[256,640]{1,0:T(8,128)(2,1)S(1)}, u32[]{:S(2)}, u32[]{:S(2)}) collective-permute-start(bf16[256,640]{1,0:T(8,128)(2,1)S(1)} %get-tuple-element.67), channel_id=1, source_target_pairs={{0,1},{1,2},{2,3},{5,4},{6,5},{7,6},{8,9},{9,10},{10,11},{13,12},{... | collective-permute-start | bytes 983048 | tf_op jit(solution)/shard_map/ppermute | solution.py:484
  99.9 12.5 %collective-permute-start.18 = (bf16[256,640]{1,0:T(8,128)(2,1)S(1)}, bf16[256,640]{1,0:T(8,128)(2,1)S(1)}, u32[]{:S(2)}, u32[]{:S(2)}) collective-permute-start(bf16[256,640]{1,0:T(8,128)(2,1)S(1)} %get-tuple-element.69), channel_id=1, source_target_pairs={{1,0},{2,1},{3,2},{4,5},{5,6},{6,7},{9,8},{10,9},{11,10},{12,13},{... | collective-permute-start | bytes 983048 | tf_op jit(solution)/shard_map/ppermute | solution.py:484
  105.1 10.9 %collective-permute-start.17 = (bf16[256,640]{1,0:T(8,128)(2,1)S(1)}, bf16[256,640]{1,0:T(8,128)(2,1)S(1)}, u32[]{:S(2)}, u32[]{:S(2)}) collective-permute-start(bf16[256,640]{1,0:T(8,128)(2,1)S(1)} %get-tuple-element.68), channel_id=1, source_target_pairs={{0,1},{1,2},{2,3},{5,4},{6,5},{7,6},{8,9},{9,10},{10,11},{13,12},{... | collective-permute-start | bytes 983048 | tf_op jit(solution)/shard_map/ppermute | solution.py:484
  106.9 12.6 %collective-permute-start.19 = (bf16[256,640]{1,0:T(8,128)(2,1)S(1)}, bf16[256,640]{1,0:T(8,128)(2,1)S(1)}, u32[]{:S(2)}, u32[]{:S(2)}) collective-permute-start(bf16[256,640]{1,0:T(8,128)(2,1)S(1)} %get-tuple-element.70), channel_id=1, source_target_pairs={{1,0},{2,1},{3,2},{4,5},{5,6},{6,7},{9,8},{10,9},{11,10},{12,13},{... | collective-permute-start | bytes 983048 | tf_op jit(solution)/shard_map/ppermute | solution.py:484
  113.1 16.1 %collective-permute-start.21 = (bf16[256,640]{1,0:T(8,128)(2,1)S(1)}, bf16[256,640]{1,0:T(8,128)(2,1)S(1)}, u32[]{:S(2)}, u32[]{:S(2)}) collective-permute-start(bf16[256,640]{1,0:T(8,128)(2,1)S(1)} %get-tuple-element.73), channel_id=1, source_target_pairs={{0,1},{1,2},{2,3},{5,4},{6,5},{7,6},{8,9},{9,10},{10,11},{13,12},{... | collective-permute-start | bytes 983048 | tf_op jit(solution)/shard_map/ppermute | solution.py:484
  114.6 14.6 %collective-permute-start.23 = (bf16[256,640]{1,0:T(8,128)(2,1)S(1)}, bf16[256,640]{1,0:T(8,128)(2,1)S(1)}, u32[]{:S(2)}, u32[]{:S(2)}) collective-permute-start(bf16[256,640]{1,0:T(8,128)(2,1)S(1)} %get-tuple-element.75), channel_id=1, source_target_pairs={{1,0},{2,1},{3,2},{4,5},{5,6},{6,7},{9,8},{10,9},{11,10},{12,13},{... | collective-permute-start | bytes 983048 | tf_op jit(solution)/shard_map/ppermute | solution.py:484
  137.3 24.7 %collective-permute-start.25 = (bf16[2,320,1280]{2,1,0:T(8,128)(2,1)S(1)}, bf16[2,320,1280]{2,1,0:T(8,128)(2,1)S(1)}, u32[]{:S(2)}, u32[]{:S(2)}) collective-permute-start(bf16[2,320,1280]{2,1,0:T(8,128)(2,1)S(1)} %add_convert_fusion), channel_id=1, source_target_pairs={{0,8},{4,20},{8,0},{12,28},{16,24},{20,4},{24,16},{28,12},{1,9},{5... | collective-permute-start | bytes 4915208 | tf_op jit(solution)/shard_map/ppermute | solution.py:474
  137.8 24.2 %collective-permute-start.26 = (bf16[3,128,640]{2,1,0:T(8,128)(2,1)S(1)}, bf16[3,128,640]{2,1,0:T(8,128)(2,1)S(1)}, u32[]{:S(2)}, u32[]{:S(2)}) collective-permute-start(bf16[3,128,640]{2,1,0:T(8,128)(2,1)S(1)} %get-tuple-element.79), channel_id=1, source_target_pairs={{0,2},{1,3},{2,0},{3,1},{4,6},{5,7},{6,4},{7,5},{8,10},{9,11},{10,... | collective-permute-start | bytes 1474568 | tf_op jit(solution)/shard_map/ppermute | solution.py:464
  162.6 12.6 %collective-permute-start.29 = (bf16[320,1280]{1,0:T(8,128)(2,1)S(1)}, bf16[320,1280]{1,0:T(8,128)(2,1)S(1)}, u32[]{:S(2)}, u32[]{:S(2)}) collective-permute-start(bf16[320,1280]{1,0:T(8,128)(2,1)S(1)} %fusion.2), channel_id=1, source_target_pairs={{0,16},{4,12},{8,24},{12,4},{16,0},{20,28},{24,8},{28,20},{1,17},{... | collective-permute-start | bytes 2457608 | tf_op jit(solution)/shard_map/ppermute | solution.py:474
  163.3 14.1 %collective-permute-start.27 = (bf16[3,128,640]{2,1,0:T(8,128)(2,1)S(1)}, bf16[3,128,640]{2,1,0:T(8,128)(2,1)S(1)}, u32[]{:S(2)}, u32[]{:S(2)}) collective-permute-start(bf16[3,128,640]{2,1,0:T(8,128)(2,1)S(1)} %get-tuple-element.78), channel_id=1, source_target_pairs={{0,3},{1,0},{2,1},{3,2},{4,7},{5,4},{6,5},{7,6},{8,11},{9,8},{10,9... | collective-permute-start | bytes 1474568 | tf_op jit(solution)/shard_map/ppermute | solution.py:464
  165.7 20.8 %collective-permute-start.28 = (bf16[3,128,640]{2,1,0:T(8,128)(2,1)S(1)}, bf16[3,128,640]{2,1,0:T(8,128)(2,1)S(1)}, u32[]{:S(2)}, u32[]{:S(2)}) collective-permute-start(bf16[3,128,640]{2,1,0:T(8,128)(2,1)S(1)} %get-tuple-element.80), channel_id=1, source_target_pairs={{0,1},{1,2},{2,3},{3,0},{4,5},{5,6},{6,7},{7,4},{8,9},{9,10},{10,1... | collective-permute-start | bytes 1474568 | tf_op jit(solution)/shard_map/ppermute | solution.py:464
  (12 other events, 101.1 us)

commit v5 on v4

--- a/solution.py
+++ b/solution.py
@@ -12,13 +12,14 @@
 BF16 = jnp.bfloat16
 MIB = 1024 * 1024
 PARTS = 2
+FAR_PARTS = 2
 
 
 def dot(a, b, dims):
     return lax.dot_general(a, b, (dims, ((), ())), preferred_element_type=F32)
 
 
-def params(mib=32):
+def params(mib=20):
     return pltpu.CompilerParams(
         dimension_semantics=("arbitrary",), vmem_limit_bytes=mib * MIB
     )
@@ -210,21 +211,19 @@
 
 def weight_steps(place_ref, shard_refs, held, sems, n):
     core, index = place_ref[1], place_ref[2]
-    own, one, two, own_o, one_o, two_o = shard_refs
     first, second = jnp.where(core == 0, 1, 2), jnp.where(core == 0, 2, 1)
-    pairs = [
-        (own, own_o, 0),
-        (one, two_o.at[0], first),
-        (two.at[0], one_o, second),
-        (two.at[1], two_o.at[1], 3),
-    ]
+    mine, (own, one, two), far = shard_refs[:4], shard_refs[4:7], shard_refs[7:]
+    chips = [(mine[0], [own]), (mine[1], [two]), (mine[2], [one]), (mine[3], far)]
+    steps = (0, first, second, 3)
 
     def copies(i):
-        mine, other, _ = pairs[i]
-        return [
-            pltpu.make_async_copy(mine, held.at[i, core], sems.at[i, 0]),
-            pltpu.make_async_copy(other, held.at[i, 1 - core], sems.at[i, 1]),
-        ]
+        found = [pltpu.make_async_copy(chips[i][0], held.at[i, core], sems.at[i, 0])]
+        start = 0
+        for j, ref in enumerate(chips[i][1]):
+            there = held.at[i, 1 - core, pl.ds(start, ref.shape[0])]
+            start += ref.shape[0]
+            found.append(pltpu.make_async_copy(ref, there, sems.at[i, 1 + j]))
+        return found
 
     for i in range(2):
         for c in copies(i):
@@ -235,13 +234,13 @@
         if i + 2 < n:
             for c in copies(i + 2):
                 c.start()
-        chip = (index // 2) ^ pairs[i][2]
+        chip = (index // 2) ^ steps[i]
         me = place_ref[0]
         yield i, lax.rem(jnp.where(core == 0, chip + n - me, me + n - chip), n)
 
 
 def weight_scratch(n, rows, cols):
-    return [pltpu.VMEM((n, 2, rows, cols), BF16), pltpu.SemaphoreType.DMA((n, 2))]
+    return [pltpu.VMEM((n, 2, rows, cols), BF16), pltpu.SemaphoreType.DMA((n, 1 + FAR_PARTS))]
 
 
 def fetch_heads(own, left, right, held, sems, pos, n):
@@ -311,9 +310,7 @@
         ),
         out_shape=jax.ShapeDtypeStruct((PARTS, n, block, width), BF16),
         compiler_params=params(),
-        cost_estimate=cost(
-            2 * length * cols * width * n, 2 * (length * cols + n * width * (cols + length))
-        ),
+        cost_estimate=cost(0, 0),
         name="d_attn_parts",
     )(place, d_proj, *shards)
 
@@ -352,9 +349,7 @@
         ),
         out_shape=jax.ShapeDtypeStruct((length, cols), BF16),
         compiler_params=params(),
-        cost_estimate=cost(
-            2 * length * cols * width * n, 2 * (length * cols + n * width * (cols + length))
-        ),
+        cost_estimate=cost(0, 0),
         name="projection",
     )(place, gate_row, *own, *sum(behind, []), *sum(front, []), *shards)
 
@@ -454,7 +449,7 @@
         ),
         out_shape=[jax.ShapeDtypeStruct((rows, n * width), BF16)] * 3,
         compiler_params=params(),
-        cost_estimate=cost(0, 12 * n * rows * width),
+        cost_estimate=cost(0, 48 * n * rows * width),
         name="assemble_heads",
     )(place, *pieces)
 
@@ -536,11 +531,14 @@
     pieces = [packed[0]] + [shift(packed[s], "ctx", s) for s in range(1, n)]
     gate_row = lax.dynamic_slice_in_dim(gate_table, timestep[0], 1, 0)
 
-    one = chip_swap(after(out_weight, packed), "dp", 0)
-    two = chip_swap(after(jnp.stack([out_weight, one]), pieces[1]), "dp", 1)
-    d_proj = (grad_out[0].astype(F32) * gate_row).astype(BF16)
-    shards = [out_weight, one, after(two, (pieces[2], d_proj))]
-    shards = shards + [swap(x, "dp", 1) for x in shards]
+    mine = after(out_weight, packed)
+    own = swap(mine, "dp", 1)
+    one = chip_swap(mine, "dp", 0)
+    two = chip_swap(after(mine, (one, pieces[1])), "dp", 1)
+    far = chip_swap(after(one, pieces[1]), "dp", 1)
+    d_proj = (after(grad_out[0], own).astype(F32) * gate_row).astype(BF16)
+    shards = [out_weight, one, two, far, own, swap(one, "dp", 1), swap(two, "dp", 1)]
+    shards += [swap(x, "dp", 1) for x in jnp.split(after(far, d_proj), FAR_PARTS)]
     parts = d_attn_parts_call(place, d_proj, shards, n)
     attended, kept = attention_call(place, after(pieces, parts), 0, n)
     attention = [attended] + [attention_call(place, kept, g, n)[0] for g in range(1, PARTS)]
@@ -569,13 +567,15 @@
     received = after(received, grads)
     far = add_rounded(keep[2:], received[2:])
     grads = [grads[0]] + [shift(grads[s], "ctx", -s) for s in range(1, n)]
-    far = after(chip_swap(far, "dp", 0), grads[n // 2])
+    far = chip_swap(far, "dp", 0)
     near = keep[:2].astype(F32) + received[:2].astype(F32) + far.astype(F32)
-    grad_weight = near[0] + chip_swap(near[1].astype(BF16), "dp", 1).astype(F32)
+    halves = jnp.split(near[1].astype(BF16), 2, axis=0)
+    last = jnp.concatenate([chip_swap(x, "dp", 1) for x in halves], axis=0)
+    grad_weight = near[0] + last.astype(F32)
 
     gate_row = after(gate_row, near)
     branch_out = projection_call(place, attention, behind, front, shards, gate_row, n)[None]
-    grad_query, grad_key, grad_value = assemble_call(place, after(grads, grad_weight))
+    grad_query, grad_key, grad_value = assemble_call(place, after(grads, branch_out))
     return (branch_out, grad_query[None], grad_key[None], grad_value[None], grad_weight)
 
 

time: 189 us -> 184 us (0.974)
  waiting for transfers between devices: 82.9 us -> 78.1 us
  local copies, waits for them, and re-layouts: 3 us -> 6.72 us
  other arithmetic: 7.48 us -> 4.05 us
    ppermute x6, waiting for transfers between devices: 52.5 us -> 27.1 us  [shift(): return lax.ppermute(x, axis, [(i, (i + by) % n) for i in range(n)])]
    ppermute x4 -> x6, waiting for transfers between devices: 8.96 us -> 30 us  [chip_swap(): lax.ppermute(x, axis, [(i, i ^ (2 if (i + step) % 2 == 0 else 4)) for i i...]
    ppermute x4 -> x6, starting transfers between devices: 4.73 us -> 7.75 us  [chip_swap(): lax.ppermute(x, axis, [(i, i ^ (2 if (i + step) % 2 == 0 else 4)) for i i...]
    unnamed x12 -> x20, local copies, waits for them, and re-layouts: 2.11 us -> 4.87 us
    ppermute x6, starting transfers between devices: 10.3 us -> 7.63 us  [shift(): return lax.ppermute(x, axis, [(i, (i + by) % n) for i in range(n)])]
  transfers between devices with their start and end apart: 30 -> 34, of which waited for: 15 -> 15; matrix products, arithmetic and copies ran while one was open for 4% -> 2% of each run, Pallas kernels for 20% -> 21%
where the time goes in v5:
time: 184 us; the launch traced here: 183 us
  waiting for transfers between devices  78.1 us (42%)
  starting transfers between devices  47.2 us (26%)
  Pallas kernels  45.6 us (25%)
  local copies, waits for them, and re-layouts  6.72 us (4%)
  other arithmetic  4.05 us (2%)
    ppermute x16, starting transfers between devices, line_move(): return lax.ppermute(x, (dp_axis, axis), pairs)  31.2 us
    ppermute x6, waiting for transfers between devices, chip_swap(): lax.ppermute(x, axis, [(i, i ^ (2 if (i + step) % 2 == 0 else 4)) for i i...  30 us
    ppermute x6, waiting for transfers between devices, shift(): return lax.ppermute(x, axis, [(i, (i + by) % n) for i in range(n)])  27.1 us
    ppermute x16, waiting for transfers between devices, line_move(): return lax.ppermute(x, (dp_axis, axis), pairs)  19 us
    pallas_call x1, Pallas kernels, projection_call(): pl.pallas_call(body, grid_spec=pltpu.PrefetchScalarGridSpec(num_scalar_pr...  9.82 us
    pallas_call x1, Pallas kernels, d_attn_parts_call(): pl.pallas_call(body, grid_spec=pltpu.PrefetchScalarGridSpec(num_scalar_pr...  8.28 us
    ppermute x6, starting transfers between devices, chip_swap(): lax.ppermute(x, axis, [(i, i ^ (2 if (i + step) % 2 == 0 else 4)) for i i...  7.75 us
    ppermute x6, starting transfers between devices, shift(): return lax.ppermute(x, axis, [(i, (i + by) % n) for i in range(n)])  7.63 us
  transfers between devices with their start and end apart: 34, of which 15 were waited for; matrix products, arithmetic and copies ran while one was open for 2% of the time, Pallas kernels for 21%

profile of v5, /device:TPU:0, one launch (start us, length us, event | category | flops | bytes accessed | tf_op | source)
XLA Modules:
  0.0 183.4 jit_solution(15201031199877115293)
XLA Ops:
  0.6 2.5 %pack_heads.1 = (bf16[3,128,640]{2,1,0:T(8,128)(2,1)}, bf16[3,128,640]{2,1,0:T(8,128)(2,1)}, bf16[3,128,640]{2,1,0:T(8,128)(2,1)}, bf16[3,128,640]{2,1,0:T(8,128)(2,1)}) custom-call(bf16[1,128,2560]{2,1,0:T(8,128)(2,1)} %refs_0_.2, bf16[1,128,2560]{2,1,0:T(8,128)(2,1)} %refs_1_.1, bf16[1,128,2560]{2,1,0:T(8,128)(2,1)} %refs_2_.1), custom_call_target="tpu_custom_call" | custom-call | bytes 3932160 | tf_op jit(solution)/shard_map/pack_heads/pallas_call | solution.py:78
  3.2 3.0 %collective-permute-start.4 = (bf16[320,1280]{1,0:T(8,128)(2,1)}, bf16[320,1280]{1,0:T(8,128)(2,1)}, u32[]{:S(2)}, u32[]{:S(2)}) collective-permute-start(bf16[320,1280]{1,0:T(8,128)(2,1)} %refs_14_.1), channel_id=1, source_target_pairs={{0,8},{4,20},{8,0},{12,28},{16,24},{20,4},{24,16},{28,12},{1,9},{5... | collective-permute-start | bytes 2457608 | tf_op jit(solution)/shard_map/ppermute | solution.py:469
  7.7 14.1 %collective-permute-done.1.refs_1_ = bf16[3,128,640]{2,1,0:T(8,128)(2,1)S(1)} collective-permute-done((bf16[3,128,640]{2,1,0:T(8,128)(2,1)}, bf16[3,128,640]{2,1,0:T(8,128)(2,1)S(1)}, u32[]{:S(2)}, u32[]{:S(2)}) %collective-permute-start.1) | collective-permute-done | bytes 491552 | tf_op jit(solution)/shard_map/ppermute | solution.py:459
  30.7 4.5 %collective-permute-done.6.refs_3_.refs_17_ = bf16[320,1280]{1,0:T(8,128)(2,1)S(1)} collective-permute-done((bf16[320,1280]{1,0:T(8,128)(2,1)}, bf16[320,1280]{1,0:T(8,128)(2,1)S(1)}, u32[]{:S(2)}, u32[]{:S(2)}) %collective-permute-start.6) | collective-permute-done | bytes 819232 | tf_op jit(solution)/shard_map/ppermute | solution.py:469
  35.2 8.9 %collective-permute-done.5.refs_2_.refs_16_ = bf16[320,1280]{1,0:T(8,128)(2,1)} collective-permute-done((bf16[320,1280]{1,0:T(8,128)(2,1)}, bf16[320,1280]{1,0:T(8,128)(2,1)}, u32[]{:S(2)}, u32[]{:S(2)}) %collective-permute-start.5) | collective-permute-done | bytes 819232 | tf_op jit(solution)/shard_map/ppermute | solution.py:469
  50.9 8.3 %d_attn_parts.1.part_f.part_b.refs_5_ = bf16[2,4,256,640]{3,2,1,0:T(8,128)(2,1)S(1)} custom-call(s32[3]{0:T(128)S(1)} %pad_add_fusion.place_ref, bf16[512,1280]{1,0:T(8,128)(2,1)S(1)} %multiply_convert_fusion.d_ref, bf16[320,1280]{1,0:T(8,128)(2,1)S(1)} %copy-done, bf16[320,1280]{1,0:T(8,128)(2,1)} %collective-permute-done.4.refs_1_.refs_15_, ...), custom_call_target="tpu_custom_call" | custom-call | tf_op jit(solution)/shard_map/d_attn_parts/pallas_call | solution.py:298
  59.2 4.1 %attention_heads.2 = (bf16[256,640]{1,0:T(8,128)(2,1)S(1)}, bf16[512,640]{1,0:T(8,128)(2,1)S(1)}, bf16[512,640]{1,0:T(8,128)(2,1)S(1)}, bf16[512,640]{1,0:T(8,128)(2,1)S(1)}) custom-call(s32[3]{0:T(128)S(1)} %pad_add_fusion.place_ref, bf16[3,128,640]{2,1,0:T(8,128)(2,1)S(1)} %copy-done.7, bf16[3,128,640]{2,1,0:T(8,128)(2,1)S(1)} %copy-done.9, ...), custom_call_target="tpu_custom_call" | custom-call | flops 335544320 | bytes 3276800 | tf_op jit(solution)/shard_map/attention_heads/pallas_call | solution.py:124
  64.6 4.6 %collective-permute-start.11 = (bf16[256,640]{1,0:T(8,128)(2,1)S(1)}, bf16[256,640]{1,0:T(8,128)(2,1)S(1)}, u32[]{:S(2)}, u32[]{:S(2)}) collective-permute-start(bf16[256,640]{1,0:T(8,128)(2,1)S(1)} %get-tuple-element.62.refs_0_.refs_1_.refs_3_), channel_id=1, source_target_pairs={{0,1},{1,2},{2,3},{5,4},{6,5},{7,6},{8,9},{9,10},{10,11},{13,12},{... | collective-permute-start | bytes 983048 | tf_op jit(solution)/shard_map/ppermute | solution.py:479
  69.2 2.9 %attention_heads.3.refs_2_.refs_3_.refs_4_.refs_1_ = bf16[256,640]{1,0:T(8,128)(2,1)S(1)} custom-call(s32[3]{0:T(128)S(1)} %pad_add_fusion.place_ref, bf16[512,640]{1,0:T(8,128)(2,1)S(1)} %get-tuple-element.63.refs_0_, bf16[512,640]{1,0:T(8,128)(2,1)S(1)} %get-tuple-element.64.refs_1_, bf16[512,640]{1,0:T(8,128)(2,1)S(1)} %get-tuple-element.65.refs_2_), custom_call_target="tpu_custom_call" | custom-call | flops 335544320 | bytes 3276800 | tf_op jit(solution)/shard_map/attention_heads/pallas_call | solution.py:124
  73.4 4.6 %collective-permute-start.15 = (bf16[256,640]{1,0:T(8,128)(2,1)S(1)}, bf16[256,640]{1,0:T(8,128)(2,1)S(1)}, u32[]{:S(2)}, u32[]{:S(2)}) collective-permute-start(bf16[256,640]{1,0:T(8,128)(2,1)S(1)} %attention_heads.3.refs_2_.refs_3_.refs_4_.refs_1_), channel_id=1, source_target_pairs={{0,1},{1,2},{2,3},{5,4},{6,5},{7,6},{8,9},{9,10},{10,11},{13,12},{... | collective-permute-start | bytes 983048 | tf_op jit(solution)/shard_map/ppermute | solution.py:479
  78.6 1.9 %collective-permute-start.13 = (bf16[256,640]{1,0:T(8,128)(2,1)S(1)}, bf16[256,640]{1,0:T(8,128)(2,1)S(1)}, u32[]{:S(2)}, u32[]{:S(2)}) collective-permute-start(bf16[256,640]{1,0:T(8,128)(2,1)S(1)} %get-tuple-element.66), channel_id=1, source_target_pairs={{0,1},{1,2},{2,3},{5,4},{6,5},{7,6},{8,9},{9,10},{10,11},{13,12},{... | collective-permute-start | bytes 983048 | tf_op jit(solution)/shard_map/ppermute | solution.py:479
  81.8 2.7 %collective-permute-done.16.back.refs_11_ = bf16[256,640]{1,0:T(8,128)(2,1)S(1)} collective-permute-done((bf16[256,640]{1,0:T(8,128)(2,1)S(1)}, bf16[256,640]{1,0:T(8,128)(2,1)S(1)}, u32[]{:S(2)}, u32[]{:S(2)}) %collective-permute-start.16) | collective-permute-done | bytes 327712 | tf_op jit(solution)/shard_map/ppermute | solution.py:479
  85.2 2.8 %collective-permute-start.17 = (bf16[256,640]{1,0:T(8,128)(2,1)S(1)}, bf16[256,640]{1,0:T(8,128)(2,1)S(1)}, u32[]{:S(2)}, u32[]{:S(2)}) collective-permute-start(bf16[256,640]{1,0:T(8,128)(2,1)S(1)} %get-tuple-element.68), channel_id=1, source_target_pairs={{0,1},{1,2},{2,3},{5,4},{6,5},{7,6},{8,9},{9,10},{10,11},{13,12},{... | collective-permute-start | bytes 983048 | tf_op jit(solution)/shard_map/ppermute | solution.py:479
  89.5 3.5 %collective-permute-done.14.back.refs_5_.refs_9_ = bf16[256,640]{1,0:T(8,128)(2,1)S(1)} collective-permute-done((bf16[256,640]{1,0:T(8,128)(2,1)S(1)}, bf16[256,640]{1,0:T(8,128)(2,1)S(1)}, u32[]{:S(2)}, u32[]{:S(2)}) %collective-permute-start.14) | collective-permute-done | bytes 327712 | tf_op jit(solution)/shard_map/ppermute | solution.py:479
  93.7 2.2 %collective-permute-start.19 = (bf16[256,640]{1,0:T(8,128)(2,1)S(1)}, bf16[256,640]{1,0:T(8,128)(2,1)S(1)}, u32[]{:S(2)}, u32[]{:S(2)}) collective-permute-start(bf16[256,640]{1,0:T(8,128)(2,1)S(1)} %get-tuple-element.70), channel_id=1, source_target_pairs={{0,1},{1,2},{2,3},{5,4},{6,5},{7,6},{8,9},{9,10},{10,11},{13,12},{... | collective-permute-start | bytes 983048 | tf_op jit(solution)/shard_map/ppermute | solution.py:479
  97.2 3.3 %collective-permute-done.18.back.refs_7_.refs_12_ = bf16[256,640]{1,0:T(8,128)(2,1)S(1)} collective-permute-done((bf16[256,640]{1,0:T(8,128)(2,1)S(1)}, bf16[256,640]{1,0:T(8,128)(2,1)S(1)}, u32[]{:S(2)}, u32[]{:S(2)}) %collective-permute-start.18) | collective-permute-done | bytes 327712 | tf_op jit(solution)/shard_map/ppermute | solution.py:479
  104.2 4.2 %collective-permute-done.21.refs_13_.back.refs_10_ = bf16[256,640]{1,0:T(8,128)(2,1)S(1)} collective-permute-done((bf16[256,640]{1,0:T(8,128)(2,1)S(1)}, bf16[256,640]{1,0:T(8,128)(2,1)S(1)}, u32[]{:S(2)}, u32[]{:S(2)}) %collective-permute-start.21) | collective-permute-done | bytes 327712 | tf_op jit(solution)/shard_map/ppermute | solution.py:479
  112.0 3.2 %collective-permute-done.22.refs_15_.back.refs_13_ = bf16[256,640]{1,0:T(8,128)(2,1)S(1)} collective-permute-done((bf16[256,640]{1,0:T(8,128)(2,1)S(1)}, bf16[256,640]{1,0:T(8,128)(2,1)S(1)}, u32[]{:S(2)}, u32[]{:S(2)}) %collective-permute-start.22) | collective-permute-done | bytes 327712 | tf_op jit(solution)/shard_map/ppermute | solution.py:479
  118.8 6.0 %weight_grad.1 = (bf16[4,320,1280]{2,1,0:T(8,128)(2,1)S(1)}, bf16[4,320,1280]{2,1,0:T(8,128)(2,1)S(1)}) custom-call(s32[3]{0:T(128)S(1)} %pad_add_fusion.place_ref, bf16[512,1280]{1,0:T(8,128)(2,1)S(1)} %multiply_convert_fusion.d_ref, bf16[256,640]{1,0:T(8,128)(2,1)S(1)} %get-tuple-element.62.refs_0_.refs_1_.refs_3_, ...), custom_call_target="tpu_custom_call" | custom-call | flops 3355443200 | bytes 13107200 | tf_op jit(solution)/shard_map/weight_grad/pallas_call | solution.py:400
  126.7 6.1 %attention_heads_grad.1 = (bf16[3,128,640]{2,1,0:T(8,128)(2,1)S(1)}, bf16[3,128,640]{2,1,0:T(8,128)(2,1)S(1)}, bf16[3,128,640]{2,1,0:T(8,128)(2,1)S(1)}, bf16[3,128,640]{2,1,0:T(8,128)(2,1)S(1)}) custom-call(s32[3]{0:T(128)S(1)} %pad_add_fusion.place_ref, bf16[512,640]{1,0:T(8,128)(2,1)S(1)} %get-tuple-element.63.refs_0_, ...), custom_call_target="tpu_custom_call" | custom-call | flops 33554432000 | bytes 7864320 | tf_op jit(solution)/shard_map/attention_heads_grad/pallas_call | solution.py:182
  137.9 16.6 %collective-permute-done.28 = bf16[2,320,1280]{2,1,0:T(8,128)(2,1)S(1)} collective-permute-done((bf16[2,320,1280]{2,1,0:T(8,128)(2,1)S(1)}, bf16[2,320,1280]{2,1,0:T(8,128)(2,1)S(1)}, u32[]{:S(2)}, u32[]{:S(2)}) %collective-permute-start.28) | collective-permute-done | bytes 1638432 | tf_op jit(solution)/shard_map/ppermute | solution.py:469
  157.3 9.8 %projection.1 = bf16[512,1280]{1,0:T(8,128)(2,1)} custom-call(s32[3]{0:T(128)S(1)} %pad_add_fusion.place_ref, f32[1,1280]{1,0:T(1,128)S(1)} %get-tuple-element.85.gate_ref, bf16[256,640]{1,0:T(8,128)(2,1)S(1)} %get-tuple-element.62.refs_0_.refs_1_.refs_3_, bf16[256,640]{1,0:T(8,128)(2,1)S(1)} %attention_heads.3.refs_2_.refs_3_.refs_4_.refs_1_, ...), custom_call_target="tpu_custom_call" | custom-call | tf_op jit(solution)/shard_map/projection/pallas_call | solution.py:337
  167.1 13.0 %collective-permute-done.30.refs_2_ = bf16[3,128,640]{2,1,0:T(8,128)(2,1)S(1)} collective-permute-done((bf16[3,128,640]{2,1,0:T(8,128)(2,1)S(1)}, bf16[3,128,640]{2,1,0:T(8,128)(2,1)S(1)}, u32[]{:S(2)}, u32[]{:S(2)}) %collective-permute-start.30) | collective-permute-done | bytes 491552 | tf_op jit(solution)/shard_map/ppermute | solution.py:459
  180.1 1.9 %assemble_heads.1 = (bf16[128,2560]{1,0:T(8,128)(2,1)}, bf16[128,2560]{1,0:T(8,128)(2,1)}, bf16[128,2560]{1,0:T(8,128)(2,1)}) custom-call(s32[3]{0:T(128)S(1)} %pad_add_fusion.place_ref, bf16[3,128,640]{2,1,0:T(8,128)(2,1)S(1)} %get-tuple-element.86.refs_0_, bf16[3,128,640]{2,1,0:T(8,128)(2,1)S(1)} %collective-permute-done.29.refs_1_, ...), custom_call_target="tpu_custom_call" | custom-call | bytes 15728640 | tf_op jit(solution)/shard_map/assemble_heads/pallas_call | solution.py:441
  (86 shorter events, 47.0 us)
Async XLA Ops:
  3.2 19.5 %collective-permute-start.4 = (bf16[320,1280]{1,0:T(8,128)(2,1)}, bf16[320,1280]{1,0:T(8,128)(2,1)}, u32[]{:S(2)}, u32[]{:S(2)}) collective-permute-start(bf16[320,1280]{1,0:T(8,128)(2,1)} %refs_14_.1), channel_id=1, source_target_pairs={{0,8},{4,20},{8,0},{12,28},{16,24},{20,4},{24,16},{28,12},{1,9},{5... | collective-permute-start | bytes 2457608 | tf_op jit(solution)/shard_map/ppermute | solution.py:469
  6.2 22.1 %collective-permute-start = (bf16[320,1280]{1,0:T(8,128)(2,1)}, bf16[320,1280]{1,0:T(8,128)(2,1)S(1)}, u32[]{:S(2)}, u32[]{:S(2)}) collective-permute-start(bf16[320,1280]{1,0:T(8,128)(2,1)} %refs_14_.1), channel_id=1, source_target_pairs={{0,4},{4,0},{8,12},{12,8},{16,20},{20,16},{24,28},{28,24},{1,5},{5... | collective-permute-start | bytes 2457608 | tf_op jit(solution)/shard_map/ppermute | solution.py:464
  6.2 15.7 %collective-permute-start.1 = (bf16[3,128,640]{2,1,0:T(8,128)(2,1)}, bf16[3,128,640]{2,1,0:T(8,128)(2,1)S(1)}, u32[]{:S(2)}, u32[]{:S(2)}) collective-permute-start(bf16[3,128,640]{2,1,0:T(8,128)(2,1)} %get-tuple-element.50), channel_id=1, source_target_pairs={{0,1},{1,2},{2,3},{3,0},{4,5},{5,6},{6,7},{7,4},{8,9},{9,10},{10,1... | collective-permute-start | bytes 1474568 | tf_op jit(solution)/shard_map/ppermute | solution.py:459
  22.7 12.6 %collective-permute-start.6 = (bf16[320,1280]{1,0:T(8,128)(2,1)}, bf16[320,1280]{1,0:T(8,128)(2,1)S(1)}, u32[]{:S(2)}, u32[]{:S(2)}) collective-permute-start(bf16[320,1280]{1,0:T(8,128)(2,1)} %collective-permute-done.4.refs_1_.refs_15_), channel_id=1, source_target_pairs={{0,16},{4,12},{8,24},{12,4},{16,0},{20,28},{24,8},{28,20},{1,17},{... | collective-permute-start | bytes 2457608 | tf_op jit(solution)/shard_map/ppermute | solution.py:469
  24.2 19.9 %collective-permute-start.5 = (bf16[320,1280]{1,0:T(8,128)(2,1)}, bf16[320,1280]{1,0:T(8,128)(2,1)}, u32[]{:S(2)}, u32[]{:S(2)}) collective-permute-start(bf16[320,1280]{1,0:T(8,128)(2,1)} %refs_14_.1), channel_id=1, source_target_pairs={{0,16},{4,12},{8,24},{12,4},{16,0},{20,28},{24,8},{28,20},{1,17},{... | collective-permute-start | bytes 2457608 | tf_op jit(solution)/shard_map/ppermute | solution.py:469
  24.7 34.5 %collective-permute-start.2 = (bf16[3,128,640]{2,1,0:T(8,128)(2,1)}, bf16[3,128,640]{2,1,0:T(8,128)(2,1)}, u32[]{:S(2)}, u32[]{:S(2)}) collective-permute-start(bf16[3,128,640]{2,1,0:T(8,128)(2,1)} %get-tuple-element.51), channel_id=1, source_target_pairs={{0,2},{1,3},{2,0},{3,1},{4,6},{5,7},{6,4},{7,5},{8,10},{9,11},{10,... | collective-permute-start | bytes 1474568 | tf_op jit(solution)/shard_map/ppermute | solution.py:459
  25.4 33.8 %collective-permute-start.3 = (bf16[3,128,640]{2,1,0:T(8,128)(2,1)}, bf16[3,128,640]{2,1,0:T(8,128)(2,1)}, u32[]{:S(2)}, u32[]{:S(2)}) collective-permute-start(bf16[3,128,640]{2,1,0:T(8,128)(2,1)} %get-tuple-element.52), channel_id=1, source_target_pairs={{0,3},{1,0},{2,1},{3,2},{4,7},{5,4},{6,5},{7,6},{8,11},{9,8},{10,9... | collective-permute-start | bytes 1474568 | tf_op jit(solution)/shard_map/ppermute | solution.py:459
  29.1 16.5 %collective-permute-start.7 = (bf16[320,1280]{1,0:T(8,128)(2,1)}, bf16[320,1280]{1,0:T(8,128)(2,1)S(1)}, u32[]{:S(2)}, u32[]{:S(2)}) collective-permute-start(bf16[320,1280]{1,0:T(8,128)(2,1)} %collective-permute-done.4.refs_1_.refs_15_), channel_id=1, source_target_pairs={{0,4},{4,0},{8,12},{12,8},{16,20},{20,16},{24,28},{28,24},{1,5},{5... | collective-permute-start | bytes 2457608 | tf_op jit(solution)/shard_map/ppermute | solution.py:464
  63.3 14.6 %collective-permute-start.12 = (bf16[256,640]{1,0:T(8,128)(2,1)S(1)}, bf16[256,640]{1,0:T(8,128)(2,1)S(1)}, u32[]{:S(2)}, u32[]{:S(2)}) collective-permute-start(bf16[256,640]{1,0:T(8,128)(2,1)S(1)} %get-tuple-element.62.refs_0_.refs_1_.refs_3_), channel_id=1, source_target_pairs={{1,0},{2,1},{3,2},{4,5},{5,6},{6,7},{9,8},{10,9},{11,10},{12,13},{... | collective-permute-start | bytes 983048 | tf_op jit(solution)/shard_map/ppermute | solution.py:479
  64.6 13.3 %collective-permute-start.11 = (bf16[256,640]{1,0:T(8,128)(2,1)S(1)}, bf16[256,640]{1,0:T(8,128)(2,1)S(1)}, u32[]{:S(2)}, u32[]{:S(2)}) collective-permute-start(bf16[256,640]{1,0:T(8,128)(2,1)S(1)} %get-tuple-element.62.refs_0_.refs_1_.refs_3_), channel_id=1, source_target_pairs={{0,1},{1,2},{2,3},{5,4},{6,5},{7,6},{8,9},{9,10},{10,11},{13,12},{... | collective-permute-start | bytes 983048 | tf_op jit(solution)/shard_map/ppermute | solution.py:479
  72.1 12.5 %collective-permute-start.16 = (bf16[256,640]{1,0:T(8,128)(2,1)S(1)}, bf16[256,640]{1,0:T(8,128)(2,1)S(1)}, u32[]{:S(2)}, u32[]{:S(2)}) collective-permute-start(bf16[256,640]{1,0:T(8,128)(2,1)S(1)} %attention_heads.3.refs_2_.refs_3_.refs_4_.refs_1_), channel_id=1, source_target_pairs={{1,0},{2,1},{3,2},{4,5},{5,6},{6,7},{9,8},{10,9},{11,10},{12,13},{... | collective-permute-start | bytes 983048 | tf_op jit(solution)/shard_map/ppermute | solution.py:479
  80.5 12.5 %collective-permute-start.14 = (bf16[256,640]{1,0:T(8,128)(2,1)S(1)}, bf16[256,640]{1,0:T(8,128)(2,1)S(1)}, u32[]{:S(2)}, u32[]{:S(2)}) collective-permute-start(bf16[256,640]{1,0:T(8,128)(2,1)S(1)} %get-tuple-element.67), channel_id=1, source_target_pairs={{1,0},{2,1},{3,2},{4,5},{5,6},{6,7},{9,8},{10,9},{11,10},{12,13},{... | collective-permute-start | bytes 983048 | tf_op jit(solution)/shard_map/ppermute | solution.py:479
  85.2 12.0 %collective-permute-start.17 = (bf16[256,640]{1,0:T(8,128)(2,1)S(1)}, bf16[256,640]{1,0:T(8,128)(2,1)S(1)}, u32[]{:S(2)}, u32[]{:S(2)}) collective-permute-start(bf16[256,640]{1,0:T(8,128)(2,1)S(1)} %get-tuple-element.68), channel_id=1, source_target_pairs={{0,1},{1,2},{2,3},{5,4},{6,5},{7,6},{8,9},{9,10},{10,11},{13,12},{... | collective-permute-start | bytes 983048 | tf_op jit(solution)/shard_map/ppermute | solution.py:479
  88.0 12.5 %collective-permute-start.18 = (bf16[256,640]{1,0:T(8,128)(2,1)S(1)}, bf16[256,640]{1,0:T(8,128)(2,1)S(1)}, u32[]{:S(2)}, u32[]{:S(2)}) collective-permute-start(bf16[256,640]{1,0:T(8,128)(2,1)S(1)} %get-tuple-element.69), channel_id=1, source_target_pairs={{1,0},{2,1},{3,2},{4,5},{5,6},{6,7},{9,8},{10,9},{11,10},{12,13},{... | collective-permute-start | bytes 983048 | tf_op jit(solution)/shard_map/ppermute | solution.py:479
  95.9 12.5 %collective-permute-start.21 = (bf16[256,640]{1,0:T(8,128)(2,1)S(1)}, bf16[256,640]{1,0:T(8,128)(2,1)S(1)}, u32[]{:S(2)}, u32[]{:S(2)}) collective-permute-start(bf16[256,640]{1,0:T(8,128)(2,1)S(1)} %get-tuple-element.72), channel_id=1, source_target_pairs={{1,0},{2,1},{3,2},{4,5},{5,6},{6,7},{9,8},{10,9},{11,10},{12,13},{... | collective-permute-start | bytes 983048 | tf_op jit(solution)/shard_map/ppermute | solution.py:479
  102.9 12.2 %collective-permute-start.22 = (bf16[256,640]{1,0:T(8,128)(2,1)S(1)}, bf16[256,640]{1,0:T(8,128)(2,1)S(1)}, u32[]{:S(2)}, u32[]{:S(2)}) collective-permute-start(bf16[256,640]{1,0:T(8,128)(2,1)S(1)} %get-tuple-element.73), channel_id=1, source_target_pairs={{1,0},{2,1},{3,2},{4,5},{5,6},{6,7},{9,8},{10,9},{11,10},{12,13},{... | collective-permute-start | bytes 983048 | tf_op jit(solution)/shard_map/ppermute | solution.py:479
  109.1 15.8 %collective-permute-start.24 = (bf16[256,640]{1,0:T(8,128)(2,1)S(1)}, bf16[256,640]{1,0:T(8,128)(2,1)S(1)}, u32[]{:S(2)}, u32[]{:S(2)}) collective-permute-start(bf16[256,640]{1,0:T(8,128)(2,1)S(1)} %get-tuple-element.76), channel_id=1, source_target_pairs={{0,1},{1,2},{2,3},{5,4},{6,5},{7,6},{8,9},{9,10},{10,11},{13,12},{... | collective-permute-start | bytes 983048 | tf_op jit(solution)/shard_map/ppermute | solution.py:479
  110.6 14.3 %collective-permute-start.26 = (bf16[256,640]{1,0:T(8,128)(2,1)S(1)}, bf16[256,640]{1,0:T(8,128)(2,1)S(1)}, u32[]{:S(2)}, u32[]{:S(2)}) collective-permute-start(bf16[256,640]{1,0:T(8,128)(2,1)S(1)} %get-tuple-element.78), channel_id=1, source_target_pairs={{1,0},{2,1},{3,2},{4,5},{5,6},{6,7},{9,8},{10,9},{11,10},{12,13},{... | collective-permute-start | bytes 983048 | tf_op jit(solution)/shard_map/ppermute | solution.py:479
  133.3 21.2 %collective-permute-start.28 = (bf16[2,320,1280]{2,1,0:T(8,128)(2,1)S(1)}, bf16[2,320,1280]{2,1,0:T(8,128)(2,1)S(1)}, u32[]{:S(2)}, u32[]{:S(2)}) collective-permute-start(bf16[2,320,1280]{2,1,0:T(8,128)(2,1)S(1)} %add_convert_fusion), channel_id=1, source_target_pairs={{0,8},{4,20},{8,0},{12,28},{16,24},{20,4},{24,16},{28,12},{1,9},{5... | collective-permute-start | bytes 4915208 | tf_op jit(solution)/shard_map/ppermute | solution.py:469
  133.9 33.2 %collective-permute-start.29 = (bf16[3,128,640]{2,1,0:T(8,128)(2,1)S(1)}, bf16[3,128,640]{2,1,0:T(8,128)(2,1)S(1)}, u32[]{:S(2)}, u32[]{:S(2)}) collective-permute-start(bf16[3,128,640]{2,1,0:T(8,128)(2,1)S(1)} %get-tuple-element.81), channel_id=1, source_target_pairs={{0,3},{1,0},{2,1},{3,2},{4,7},{5,4},{6,5},{7,6},{8,11},{9,8},{10,9... | collective-permute-start | bytes 1474568 | tf_op jit(solution)/shard_map/ppermute | solution.py:459
  134.7 45.4 %collective-permute-start.30 = (bf16[3,128,640]{2,1,0:T(8,128)(2,1)S(1)}, bf16[3,128,640]{2,1,0:T(8,128)(2,1)S(1)}, u32[]{:S(2)}, u32[]{:S(2)}) collective-permute-start(bf16[3,128,640]{2,1,0:T(8,128)(2,1)S(1)} %get-tuple-element.82), channel_id=1, source_target_pairs={{0,2},{1,3},{2,0},{3,1},{4,6},{5,7},{6,4},{7,5},{8,10},{9,11},{10,... | collective-permute-start | bytes 1474568 | tf_op jit(solution)/shard_map/ppermute | solution.py:459
  136.4 43.7 %collective-permute-start.31 = (bf16[3,128,640]{2,1,0:T(8,128)(2,1)S(1)}, bf16[3,128,640]{2,1,0:T(8,128)(2,1)S(1)}, u32[]{:S(2)}, u32[]{:S(2)}) collective-permute-start(bf16[3,128,640]{2,1,0:T(8,128)(2,1)S(1)} %get-tuple-element.83), channel_id=1, source_target_pairs={{0,1},{1,2},{2,3},{3,0},{4,5},{5,6},{6,7},{7,4},{8,9},{9,10},{10,1... | collective-permute-start | bytes 1474568 | tf_op jit(solution)/shard_map/ppermute | solution.py:459
  155.2 26.8 %collective-permute-start.32 = (bf16[160,1280]{1,0:T(8,128)(2,1)S(1)}, bf16[160,1280]{1,0:T(8,128)(2,1)S(1)}, u32[]{:S(2)}, u32[]{:S(2)}) collective-permute-start(bf16[160,1280]{1,0:T(8,128)(2,1)S(1)} %get-tuple-element.97), channel_id=1, source_target_pairs={{0,16},{4,12},{8,24},{12,4},{16,0},{20,28},{24,8},{28,20},{1,17},{... | collective-permute-start | bytes 1228808 | tf_op jit(solution)/shard_map/ppermute | solution.py:469
  156.8 25.3 %collective-permute-start.33 = (bf16[160,1280]{1,0:T(8,128)(2,1)S(1)}, bf16[160,1280]{1,0:T(8,128)(2,1)S(1)}, u32[]{:S(2)}, u32[]{:S(2)}) collective-permute-start(bf16[160,1280]{1,0:T(8,128)(2,1)S(1)} %get-tuple-element.98), channel_id=1, source_target_pairs={{0,16},{4,12},{8,24},{12,4},{16,0},{20,28},{24,8},{28,20},{1,17},{... | collective-permute-start | bytes 1228808 | tf_op jit(solution)/shard_map/ppermute | solution.py:469
  (20 other events, 193.7 us)

commit v6 on v5

--- a/solution.py
+++ b/solution.py
@@ -37,8 +37,7 @@
     return (a.astype(F32) + b.astype(F32)).astype(BF16)
 
 
-def exponentials(q, k):
-    scores = dot(k, q, ((1,), (1,)))
+def exponentials(scores):
     top = jnp.max(scores, axis=0, keepdims=True)
     shifted = jnp.exp2((scores - top) * (HEAD_DIM ** (-0.5) * math.log2(math.e)))
     return shifted, 1.0 / jnp.sum(shifted, axis=0, keepdims=True)
@@ -108,9 +107,17 @@
             pl.ds(pl.multiple_of(lax.rem(place_ref[0] + n - slab, n) * rows, rows), rows)
             for slab in range(block * slabs, (block + 1) * slabs)
         ]
-        for lanes in head_lanes(width):
+        def scores_of(lanes):
             q = jnp.concatenate([kept_refs[0][w, lanes] for w in wanted], axis=0)
-            shifted, inverse = exponentials(q, kept_refs[1][:, lanes])
+            return dot(kept_refs[1][:, lanes], q, ((1,), (1,)))
+
+        every = head_lanes(width)
+        ready = scores_of(every[0])
+        for h, lanes in enumerate(every):
+            scores = ready
+            if h + 1 < len(every):
+                ready = scores_of(every[h + 1])
+            shifted, inverse = exponentials(scores)
             out = dot(kept_refs[2][:, lanes], shifted.astype(BF16), ((0,), (0,))) * inverse
             out_ref[:, lanes] = out.T.astype(BF16)
 
@@ -157,14 +164,25 @@
             attn_held[here] = attn_refs[i][...]
             terms = [term_refs[t * PARTS + i][...].astype(F32) for t in range(n_terms)]
             d_held[here] = sum(terms, part_ref[i, 0].astype(F32)).astype(BF16)
-        for lanes in head_lanes(width):
+        def scores_of(lanes):
+            k = kept_refs[1][:, lanes]
+            return dot(k, kept_refs[0][:, lanes], ((1,), (1,)))
+
+        def d_of(lanes):
+            d_attn = jnp.concatenate([d_held[p, lanes] for p in places], axis=0)
+            return d_attn, dot(kept_refs[2][:, lanes], d_attn, ((1,), (1,)))
+
+        every = head_lanes(width)
+        ready = (scores_of(every[0]), d_of(every[0]))
+        for h, lanes in enumerate(every):
+            scores, (d_attn, d_prob) = ready
+            if h + 1 < len(every):
+                ready = (scores_of(every[h + 1]), d_of(every[h + 1]))
             q, k, v = (r[:, lanes] for r in kept_refs)
             attn = jnp.concatenate([attn_held[p, lanes] for p in places], axis=0).astype(F32)
-            d_attn = jnp.concatenate([d_held[p, lanes] for p in places], axis=0)
-            shifted, inverse = exponentials(q, k)
+            shifted, inverse = exponentials(scores)
             prob = shifted * inverse
             delta = jnp.sum(d_attn.astype(F32) * attn, axis=1, keepdims=True).T
-            d_prob = dot(v, d_attn, ((1,), (1,)))
             d_half = (prob * (d_prob - delta) * scale).astype(BF16)
             grads = (
                 dot(k, d_half, ((0,), (0,))).T,
@@ -536,7 +554,7 @@
     one = chip_swap(mine, "dp", 0)
     two = chip_swap(after(mine, (one, pieces[1])), "dp", 1)
     far = chip_swap(after(one, pieces[1]), "dp", 1)
-    d_proj = (after(grad_out[0], own).astype(F32) * gate_row).astype(BF16)
+    d_proj = (grad_out[0].astype(F32) * gate_row).astype(BF16)
     shards = [out_weight, one, two, far, own, swap(one, "dp", 1), swap(two, "dp", 1)]
     shards += [swap(x, "dp", 1) for x in jnp.split(after(far, d_proj), FAR_PARTS)]
     parts = d_attn_parts_call(place, d_proj, shards, n)

time: 184 us -> 180 us (0.978)
  waiting for transfers between devices: 78.1 us -> 75.6 us
  local copies, waits for them, and re-layouts: 6.72 us -> 4.69 us
    unnamed x20 -> x14, local copies, waits for them, and re-layouts: 4.87 us -> 2.83 us
    ppermute x6, waiting for transfers between devices: 27.1 us -> 25.1 us  [shift(): return lax.ppermute(x, axis, [(i, (i + by) % n) for i in range(n)])]
where the time goes in v6:
time: 180 us; the launch traced here: 179 us
  waiting for transfers between devices  75.6 us (42%)
  starting transfers between devices  48.6 us (27%)
  Pallas kernels  44.2 us (25%)
  local copies, waits for them, and re-layouts  4.69 us (3%)
  other arithmetic  4.13 us (2%)
    ppermute x16, starting transfers between devices, line_move(): return lax.ppermute(x, (dp_axis, axis), pairs)  30.8 us
    ppermute x6, waiting for transfers between devices, chip_swap(): lax.ppermute(x, axis, [(i, i ^ (2 if (i + step) % 2 == 0 else 4)) for i i...  29.1 us
    ppermute x6, waiting for transfers between devices, shift(): return lax.ppermute(x, axis, [(i, (i + by) % n) for i in range(n)])  25.1 us
    ppermute x16, waiting for transfers between devices, line_move(): return lax.ppermute(x, (dp_axis, axis), pairs)  19.4 us
    pallas_call x1, Pallas kernels, projection_call(): pl.pallas_call(body, grid_spec=pltpu.PrefetchScalarGridSpec(num_scalar_pr...  9.75 us
    pallas_call x1, Pallas kernels, d_attn_parts_call(): pl.pallas_call(body, grid_spec=pltpu.PrefetchScalarGridSpec(num_scalar_pr...  9.33 us
    ppermute x6, starting transfers between devices, chip_swap(): lax.ppermute(x, axis, [(i, i ^ (2 if (i + step) % 2 == 0 else 4)) for i i...  8.69 us
    ppermute x6, starting transfers between devices, shift(): return lax.ppermute(x, axis, [(i, (i + by) % n) for i in range(n)])  7.9 us
  transfers between devices with their start and end apart: 34, of which 15 were waited for; matrix products, arithmetic and copies ran while one was open for 2% of the time, Pallas kernels for 21%

profile of v6, /device:TPU:0, one launch (start us, length us, event | category | flops | bytes accessed | tf_op | source)
XLA Modules:
  0.0 179.0 jit_solution(5763606626017656728)
XLA Ops:
  0.6 2.5 %pack_heads.1 = (bf16[3,128,640]{2,1,0:T(8,128)(2,1)}, bf16[3,128,640]{2,1,0:T(8,128)(2,1)}, bf16[3,128,640]{2,1,0:T(8,128)(2,1)}, bf16[3,128,640]{2,1,0:T(8,128)(2,1)}) custom-call(bf16[1,128,2560]{2,1,0:T(8,128)(2,1)} %refs_0_.2, bf16[1,128,2560]{2,1,0:T(8,128)(2,1)} %refs_1_.1, bf16[1,128,2560]{2,1,0:T(8,128)(2,1)} %refs_2_.1), custom_call_target="tpu_custom_call" | custom-call | bytes 3932160 | tf_op jit(solution)/shard_map/pack_heads/pallas_call | solution.py:77
  3.2 3.0 %collective-permute-start.3 = (bf16[320,1280]{1,0:T(8,128)(2,1)}, bf16[320,1280]{1,0:T(8,128)(2,1)}, u32[]{:S(2)}, u32[]{:S(2)}) collective-permute-start(bf16[320,1280]{1,0:T(8,128)(2,1)} %refs_14_.1), channel_id=1, source_target_pairs={{0,8},{4,20},{8,0},{12,28},{16,24},{20,4},{24,16},{28,12},{1,9},{5... | collective-permute-start | bytes 2457608 | tf_op jit(solution)/shard_map/ppermute | solution.py:487
  7.7 13.2 %collective-permute-done.refs_1_ = bf16[3,128,640]{2,1,0:T(8,128)(2,1)S(1)} collective-permute-done((bf16[3,128,640]{2,1,0:T(8,128)(2,1)}, bf16[3,128,640]{2,1,0:T(8,128)(2,1)S(1)}, u32[]{:S(2)}, u32[]{:S(2)}) %collective-permute-start) | collective-permute-done | bytes 491552 | tf_op jit(solution)/shard_map/ppermute | solution.py:477
  28.1 6.2 %collective-permute-done.5.refs_3_.refs_17_ = bf16[320,1280]{1,0:T(8,128)(2,1)S(1)} collective-permute-done((bf16[320,1280]{1,0:T(8,128)(2,1)}, bf16[320,1280]{1,0:T(8,128)(2,1)S(1)}, u32[]{:S(2)}, u32[]{:S(2)}) %collective-permute-start.5) | collective-permute-done | bytes 819232 | tf_op jit(solution)/shard_map/ppermute | solution.py:487
  36.0 7.1 %collective-permute-done.4.refs_2_.refs_16_ = bf16[320,1280]{1,0:T(8,128)(2,1)} collective-permute-done((bf16[320,1280]{1,0:T(8,128)(2,1)}, bf16[320,1280]{1,0:T(8,128)(2,1)}, u32[]{:S(2)}, u32[]{:S(2)}) %collective-permute-start.4) | collective-permute-done | bytes 819232 | tf_op jit(solution)/shard_map/ppermute | solution.py:487
  48.8 9.3 %d_attn_parts.1.part_f.part_b.refs_5_ = bf16[2,4,256,640]{3,2,1,0:T(8,128)(2,1)S(1)} custom-call(s32[3]{0:T(128)S(1)} %pad_add_fusion.place_ref, bf16[512,1280]{1,0:T(8,128)(2,1)S(1)} %fusion.d_ref, bf16[320,1280]{1,0:T(8,128)(2,1)S(1)} %copy-done, bf16[320,1280]{1,0:T(8,128)(2,1)} %collective-permute-done.3.refs_1_.refs_15_, ...), custom_call_target="tpu_custom_call" | custom-call | tf_op jit(solution)/shard_map/d_attn_parts/pallas_call | solution.py:316
  58.2 3.2 %attention_heads.2 = (bf16[256,640]{1,0:T(8,128)(2,1)S(1)}, bf16[512,640]{1,0:T(8,128)(2,1)S(1)}, bf16[512,640]{1,0:T(8,128)(2,1)S(1)}, bf16[512,640]{1,0:T(8,128)(2,1)S(1)}) custom-call(s32[3]{0:T(128)S(1)} %pad_add_fusion.place_ref, bf16[3,128,640]{2,1,0:T(8,128)(2,1)S(1)} %copy-done.4, bf16[3,128,640]{2,1,0:T(8,128)(2,1)S(1)} %copy-done.6, ...), custom_call_target="tpu_custom_call" | custom-call | flops 335544320 | bytes 3276800 | tf_op jit(solution)/shard_map/attention_heads/pallas_call | solution.py:131
  62.7 4.6 %collective-permute-start.11 = (bf16[256,640]{1,0:T(8,128)(2,1)S(1)}, bf16[256,640]{1,0:T(8,128)(2,1)S(1)}, u32[]{:S(2)}, u32[]{:S(2)}) collective-permute-start(bf16[256,640]{1,0:T(8,128)(2,1)S(1)} %get-tuple-element.60.refs_0_.refs_1_.refs_3_), channel_id=1, source_target_pairs={{0,1},{1,2},{2,3},{5,4},{6,5},{7,6},{8,9},{9,10},{10,11},{13,12},{... | collective-permute-start | bytes 983048 | tf_op jit(solution)/shard_map/ppermute | solution.py:497
  67.3 2.0 %attention_heads.3.refs_2_.refs_3_.refs_4_.refs_1_ = bf16[256,640]{1,0:T(8,128)(2,1)S(1)} custom-call(s32[3]{0:T(128)S(1)} %pad_add_fusion.place_ref, bf16[512,640]{1,0:T(8,128)(2,1)S(1)} %get-tuple-element.61.refs_0_, bf16[512,640]{1,0:T(8,128)(2,1)S(1)} %get-tuple-element.62.refs_1_, bf16[512,640]{1,0:T(8,128)(2,1)S(1)} %get-tuple-element.63.refs_2_), custom_call_target="tpu_custom_call" | custom-call | flops 335544320 | bytes 3276800 | tf_op jit(solution)/shard_map/attention_heads/pallas_call | solution.py:131
  70.6 4.6 %collective-permute-start.15 = (bf16[256,640]{1,0:T(8,128)(2,1)S(1)}, bf16[256,640]{1,0:T(8,128)(2,1)S(1)}, u32[]{:S(2)}, u32[]{:S(2)}) collective-permute-start(bf16[256,640]{1,0:T(8,128)(2,1)S(1)} %attention_heads.3.refs_2_.refs_3_.refs_4_.refs_1_), channel_id=1, source_target_pairs={{0,1},{1,2},{2,3},{5,4},{6,5},{7,6},{8,9},{9,10},{10,11},{13,12},{... | collective-permute-start | bytes 983048 | tf_op jit(solution)/shard_map/ppermute | solution.py:497
  75.9 2.2 %collective-permute-start.13 = (bf16[256,640]{1,0:T(8,128)(2,1)S(1)}, bf16[256,640]{1,0:T(8,128)(2,1)S(1)}, u32[]{:S(2)}, u32[]{:S(2)}) collective-permute-start(bf16[256,640]{1,0:T(8,128)(2,1)S(1)} %get-tuple-element.64), channel_id=1, source_target_pairs={{0,1},{1,2},{2,3},{5,4},{6,5},{7,6},{8,9},{9,10},{10,11},{13,12},{... | collective-permute-start | bytes 983048 | tf_op jit(solution)/shard_map/ppermute | solution.py:497
  79.4 2.4 %collective-permute-done.16.back.refs_11_ = bf16[256,640]{1,0:T(8,128)(2,1)S(1)} collective-permute-done((bf16[256,640]{1,0:T(8,128)(2,1)S(1)}, bf16[256,640]{1,0:T(8,128)(2,1)S(1)}, u32[]{:S(2)}, u32[]{:S(2)}) %collective-permute-start.16) | collective-permute-done | bytes 327712 | tf_op jit(solution)/shard_map/ppermute | solution.py:497
  82.4 2.3 %collective-permute-start.17 = (bf16[256,640]{1,0:T(8,128)(2,1)S(1)}, bf16[256,640]{1,0:T(8,128)(2,1)S(1)}, u32[]{:S(2)}, u32[]{:S(2)}) collective-permute-start(bf16[256,640]{1,0:T(8,128)(2,1)S(1)} %get-tuple-element.66), channel_id=1, source_target_pairs={{0,1},{1,2},{2,3},{5,4},{6,5},{7,6},{8,9},{9,10},{10,11},{13,12},{... | collective-permute-start | bytes 983048 | tf_op jit(solution)/shard_map/ppermute | solution.py:497
  86.3 4.2 %collective-permute-done.14.back.refs_5_.refs_9_ = bf16[256,640]{1,0:T(8,128)(2,1)S(1)} collective-permute-done((bf16[256,640]{1,0:T(8,128)(2,1)S(1)}, bf16[256,640]{1,0:T(8,128)(2,1)S(1)}, u32[]{:S(2)}, u32[]{:S(2)}) %collective-permute-start.14) | collective-permute-done | bytes 327712 | tf_op jit(solution)/shard_map/ppermute | solution.py:497
  91.1 2.0 %collective-permute-start.19 = (bf16[256,640]{1,0:T(8,128)(2,1)S(1)}, bf16[256,640]{1,0:T(8,128)(2,1)S(1)}, u32[]{:S(2)}, u32[]{:S(2)}) collective-permute-start(bf16[256,640]{1,0:T(8,128)(2,1)S(1)} %get-tuple-element.68), channel_id=1, source_target_pairs={{0,1},{1,2},{2,3},{5,4},{6,5},{7,6},{8,9},{9,10},{10,11},{13,12},{... | collective-permute-start | bytes 983048 | tf_op jit(solution)/shard_map/ppermute | solution.py:497
  94.4 3.1 %collective-permute-done.18.back.refs_7_.refs_12_ = bf16[256,640]{1,0:T(8,128)(2,1)S(1)} collective-permute-done((bf16[256,640]{1,0:T(8,128)(2,1)S(1)}, bf16[256,640]{1,0:T(8,128)(2,1)S(1)}, u32[]{:S(2)}, u32[]{:S(2)}) %collective-permute-start.18) | collective-permute-done | bytes 327712 | tf_op jit(solution)/shard_map/ppermute | solution.py:497
  101.0 4.7 %collective-permute-done.21.refs_13_.back.refs_10_ = bf16[256,640]{1,0:T(8,128)(2,1)S(1)} collective-permute-done((bf16[256,640]{1,0:T(8,128)(2,1)S(1)}, bf16[256,640]{1,0:T(8,128)(2,1)S(1)}, u32[]{:S(2)}, u32[]{:S(2)}) %collective-permute-start.21) | collective-permute-done | bytes 327712 | tf_op jit(solution)/shard_map/ppermute | solution.py:497
  109.2 3.0 %collective-permute-done.22.refs_15_.back.refs_13_ = bf16[256,640]{1,0:T(8,128)(2,1)S(1)} collective-permute-done((bf16[256,640]{1,0:T(8,128)(2,1)S(1)}, bf16[256,640]{1,0:T(8,128)(2,1)S(1)}, u32[]{:S(2)}, u32[]{:S(2)}) %collective-permute-start.22) | collective-permute-done | bytes 327712 | tf_op jit(solution)/shard_map/ppermute | solution.py:497
  116.0 6.0 %weight_grad.1 = (bf16[4,320,1280]{2,1,0:T(8,128)(2,1)S(1)}, bf16[4,320,1280]{2,1,0:T(8,128)(2,1)S(1)}) custom-call(s32[3]{0:T(128)S(1)} %pad_add_fusion.place_ref, bf16[512,1280]{1,0:T(8,128)(2,1)S(1)} %fusion.d_ref, bf16[256,640]{1,0:T(8,128)(2,1)S(1)} %get-tuple-element.60.refs_0_.refs_1_.refs_3_, ...), custom_call_target="tpu_custom_call" | custom-call | flops 3355443200 | bytes 13107200 | tf_op jit(solution)/shard_map/weight_grad/pallas_call | solution.py:418
  123.9 5.6 %attention_heads_grad.1 = (bf16[3,128,640]{2,1,0:T(8,128)(2,1)S(1)}, bf16[3,128,640]{2,1,0:T(8,128)(2,1)S(1)}, bf16[3,128,640]{2,1,0:T(8,128)(2,1)S(1)}, bf16[3,128,640]{2,1,0:T(8,128)(2,1)S(1)}) custom-call(s32[3]{0:T(128)S(1)} %pad_add_fusion.place_ref, bf16[512,640]{1,0:T(8,128)(2,1)S(1)} %get-tuple-element.61.refs_0_, ...), custom_call_target="tpu_custom_call" | custom-call | flops 33554432000 | bytes 7864320 | tf_op jit(solution)/shard_map/attention_heads_grad/pallas_call | solution.py:200
  135.4 15.8 %collective-permute-done.28 = bf16[2,320,1280]{2,1,0:T(8,128)(2,1)S(1)} collective-permute-done((bf16[2,320,1280]{2,1,0:T(8,128)(2,1)S(1)}, bf16[2,320,1280]{2,1,0:T(8,128)(2,1)S(1)}, u32[]{:S(2)}, u32[]{:S(2)}) %collective-permute-start.28) | collective-permute-done | bytes 1638432 | tf_op jit(solution)/shard_map/ppermute | solution.py:487
  154.0 9.7 %projection.1 = bf16[512,1280]{1,0:T(8,128)(2,1)} custom-call(s32[3]{0:T(128)S(1)} %pad_add_fusion.place_ref, f32[1,1280]{1,0:T(1,128)S(1)} %get-tuple-element.83.gate_ref, bf16[256,640]{1,0:T(8,128)(2,1)S(1)} %get-tuple-element.60.refs_0_.refs_1_.refs_3_, bf16[256,640]{1,0:T(8,128)(2,1)S(1)} %attention_heads.3.refs_2_.refs_3_.refs_4_.refs_1_, ...), custom_call_target="tpu_custom_call" | custom-call | tf_op jit(solution)/shard_map/projection/pallas_call | solution.py:355
  163.8 11.9 %collective-permute-done.30.refs_2_ = bf16[3,128,640]{2,1,0:T(8,128)(2,1)S(1)} collective-permute-done((bf16[3,128,640]{2,1,0:T(8,128)(2,1)S(1)}, bf16[3,128,640]{2,1,0:T(8,128)(2,1)S(1)}, u32[]{:S(2)}, u32[]{:S(2)}) %collective-permute-start.30) | collective-permute-done | bytes 491552 | tf_op jit(solution)/shard_map/ppermute | solution.py:477
  175.7 1.9 %assemble_heads.1 = (bf16[128,2560]{1,0:T(8,128)(2,1)}, bf16[128,2560]{1,0:T(8,128)(2,1)}, bf16[128,2560]{1,0:T(8,128)(2,1)}) custom-call(s32[3]{0:T(128)S(1)} %pad_add_fusion.place_ref, bf16[3,128,640]{2,1,0:T(8,128)(2,1)S(1)} %get-tuple-element.84.refs_0_, bf16[3,128,640]{2,1,0:T(8,128)(2,1)S(1)} %collective-permute-done.29.refs_1_, ...), custom_call_target="tpu_custom_call" | custom-call | bytes 15728640 | tf_op jit(solution)/shard_map/assemble_heads/pallas_call | solution.py:459
  (80 shorter events, 46.9 us)
Async XLA Ops:
  3.2 18.6 %collective-permute-start.3 = (bf16[320,1280]{1,0:T(8,128)(2,1)}, bf16[320,1280]{1,0:T(8,128)(2,1)}, u32[]{:S(2)}, u32[]{:S(2)}) collective-permute-start(bf16[320,1280]{1,0:T(8,128)(2,1)} %refs_14_.1), channel_id=1, source_target_pairs={{0,8},{4,20},{8,0},{12,28},{16,24},{20,4},{24,16},{28,12},{1,9},{5... | collective-permute-start | bytes 2457608 | tf_op jit(solution)/shard_map/ppermute | solution.py:487
  6.2 14.8 %collective-permute-start = (bf16[3,128,640]{2,1,0:T(8,128)(2,1)}, bf16[3,128,640]{2,1,0:T(8,128)(2,1)S(1)}, u32[]{:S(2)}, u32[]{:S(2)}) collective-permute-start(bf16[3,128,640]{2,1,0:T(8,128)(2,1)} %get-tuple-element.49), channel_id=1, source_target_pairs={{0,1},{1,2},{2,3},{3,0},{4,5},{5,6},{6,7},{7,4},{8,9},{9,10},{10,1... | collective-permute-start | bytes 1474568 | tf_op jit(solution)/shard_map/ppermute | solution.py:477
  21.7 12.6 %collective-permute-start.5 = (bf16[320,1280]{1,0:T(8,128)(2,1)}, bf16[320,1280]{1,0:T(8,128)(2,1)S(1)}, u32[]{:S(2)}, u32[]{:S(2)}) collective-permute-start(bf16[320,1280]{1,0:T(8,128)(2,1)} %collective-permute-done.3.refs_1_.refs_15_), channel_id=1, source_target_pairs={{0,16},{4,12},{8,24},{12,4},{16,0},{20,28},{24,8},{28,20},{1,17},{... | collective-permute-start | bytes 2457608 | tf_op jit(solution)/shard_map/ppermute | solution.py:487
  22.2 20.9 %collective-permute-start.4 = (bf16[320,1280]{1,0:T(8,128)(2,1)}, bf16[320,1280]{1,0:T(8,128)(2,1)}, u32[]{:S(2)}, u32[]{:S(2)}) collective-permute-start(bf16[320,1280]{1,0:T(8,128)(2,1)} %refs_14_.1), channel_id=1, source_target_pairs={{0,16},{4,12},{8,24},{12,4},{16,0},{20,28},{24,8},{28,20},{1,17},{... | collective-permute-start | bytes 2457608 | tf_op jit(solution)/shard_map/ppermute | solution.py:487
  23.8 34.4 %collective-permute-start.1 = (bf16[3,128,640]{2,1,0:T(8,128)(2,1)}, bf16[3,128,640]{2,1,0:T(8,128)(2,1)}, u32[]{:S(2)}, u32[]{:S(2)}) collective-permute-start(bf16[3,128,640]{2,1,0:T(8,128)(2,1)} %get-tuple-element.50), channel_id=1, source_target_pairs={{0,2},{1,3},{2,0},{3,1},{4,6},{5,7},{6,4},{7,5},{8,10},{9,11},{10,... | collective-permute-start | bytes 1474568 | tf_op jit(solution)/shard_map/ppermute | solution.py:477
  24.5 19.7 %collective-permute-start.6 = (bf16[320,1280]{1,0:T(8,128)(2,1)}, bf16[320,1280]{1,0:T(8,128)(2,1)}, u32[]{:S(2)}, u32[]{:S(2)}) collective-permute-start(bf16[320,1280]{1,0:T(8,128)(2,1)} %refs_14_.1), channel_id=1, source_target_pairs={{0,4},{4,0},{8,12},{12,8},{16,20},{20,16},{24,28},{28,24},{1,5},{5... | collective-permute-start | bytes 2457608 | tf_op jit(solution)/shard_map/ppermute | solution.py:482
  25.9 18.7 %collective-permute-start.7 = (bf16[320,1280]{1,0:T(8,128)(2,1)}, bf16[320,1280]{1,0:T(8,128)(2,1)S(1)}, u32[]{:S(2)}, u32[]{:S(2)}) collective-permute-start(bf16[320,1280]{1,0:T(8,128)(2,1)} %collective-permute-done.3.refs_1_.refs_15_), channel_id=1, source_target_pairs={{0,4},{4,0},{8,12},{12,8},{16,20},{20,16},{24,28},{28,24},{1,5},{5... | collective-permute-start | bytes 2457608 | tf_op jit(solution)/shard_map/ppermute | solution.py:482
  34.3 23.9 %collective-permute-start.2 = (bf16[3,128,640]{2,1,0:T(8,128)(2,1)}, bf16[3,128,640]{2,1,0:T(8,128)(2,1)}, u32[]{:S(2)}, u32[]{:S(2)}) collective-permute-start(bf16[3,128,640]{2,1,0:T(8,128)(2,1)} %get-tuple-element.51), channel_id=1, source_target_pairs={{0,3},{1,0},{2,1},{3,2},{4,7},{5,4},{6,5},{7,6},{8,11},{9,8},{10,9... | collective-permute-start | bytes 1474568 | tf_op jit(solution)/shard_map/ppermute | solution.py:477
  61.4 13.7 %collective-permute-start.12 = (bf16[256,640]{1,0:T(8,128)(2,1)S(1)}, bf16[256,640]{1,0:T(8,128)(2,1)S(1)}, u32[]{:S(2)}, u32[]{:S(2)}) collective-permute-start(bf16[256,640]{1,0:T(8,128)(2,1)S(1)} %get-tuple-element.60.refs_0_.refs_1_.refs_3_), channel_id=1, source_target_pairs={{1,0},{2,1},{3,2},{4,5},{5,6},{6,7},{9,8},{10,9},{11,10},{12,13},{... | collective-permute-start | bytes 983048 | tf_op jit(solution)/shard_map/ppermute | solution.py:497
  62.7 12.4 %collective-permute-start.11 = (bf16[256,640]{1,0:T(8,128)(2,1)S(1)}, bf16[256,640]{1,0:T(8,128)(2,1)S(1)}, u32[]{:S(2)}, u32[]{:S(2)}) collective-permute-start(bf16[256,640]{1,0:T(8,128)(2,1)S(1)} %get-tuple-element.60.refs_0_.refs_1_.refs_3_), channel_id=1, source_target_pairs={{0,1},{1,2},{2,3},{5,4},{6,5},{7,6},{8,9},{9,10},{10,11},{13,12},{... | collective-permute-start | bytes 983048 | tf_op jit(solution)/shard_map/ppermute | solution.py:497
  69.3 12.5 %collective-permute-start.16 = (bf16[256,640]{1,0:T(8,128)(2,1)S(1)}, bf16[256,640]{1,0:T(8,128)(2,1)S(1)}, u32[]{:S(2)}, u32[]{:S(2)}) collective-permute-start(bf16[256,640]{1,0:T(8,128)(2,1)S(1)} %attention_heads.3.refs_2_.refs_3_.refs_4_.refs_1_), channel_id=1, source_target_pairs={{1,0},{2,1},{3,2},{4,5},{5,6},{6,7},{9,8},{10,9},{11,10},{12,13},{... | collective-permute-start | bytes 983048 | tf_op jit(solution)/shard_map/ppermute | solution.py:497
  78.1 12.4 %collective-permute-start.14 = (bf16[256,640]{1,0:T(8,128)(2,1)S(1)}, bf16[256,640]{1,0:T(8,128)(2,1)S(1)}, u32[]{:S(2)}, u32[]{:S(2)}) collective-permute-start(bf16[256,640]{1,0:T(8,128)(2,1)S(1)} %get-tuple-element.65), channel_id=1, source_target_pairs={{1,0},{2,1},{3,2},{4,5},{5,6},{6,7},{9,8},{10,9},{11,10},{12,13},{... | collective-permute-start | bytes 983048 | tf_op jit(solution)/shard_map/ppermute | solution.py:497
  82.4 12.0 %collective-permute-start.17 = (bf16[256,640]{1,0:T(8,128)(2,1)S(1)}, bf16[256,640]{1,0:T(8,128)(2,1)S(1)}, u32[]{:S(2)}, u32[]{:S(2)}) collective-permute-start(bf16[256,640]{1,0:T(8,128)(2,1)S(1)} %get-tuple-element.66), channel_id=1, source_target_pairs={{0,1},{1,2},{2,3},{5,4},{6,5},{7,6},{8,9},{9,10},{10,11},{13,12},{... | collective-permute-start | bytes 983048 | tf_op jit(solution)/shard_map/ppermute | solution.py:497
  84.7 12.8 %collective-permute-start.18 = (bf16[256,640]{1,0:T(8,128)(2,1)S(1)}, bf16[256,640]{1,0:T(8,128)(2,1)S(1)}, u32[]{:S(2)}, u32[]{:S(2)}) collective-permute-start(bf16[256,640]{1,0:T(8,128)(2,1)S(1)} %get-tuple-element.67), channel_id=1, source_target_pairs={{1,0},{2,1},{3,2},{4,5},{5,6},{6,7},{9,8},{10,9},{11,10},{12,13},{... | collective-permute-start | bytes 983048 | tf_op jit(solution)/shard_map/ppermute | solution.py:497
  93.1 12.5 %collective-permute-start.21 = (bf16[256,640]{1,0:T(8,128)(2,1)S(1)}, bf16[256,640]{1,0:T(8,128)(2,1)S(1)}, u32[]{:S(2)}, u32[]{:S(2)}) collective-permute-start(bf16[256,640]{1,0:T(8,128)(2,1)S(1)} %get-tuple-element.70), channel_id=1, source_target_pairs={{1,0},{2,1},{3,2},{4,5},{5,6},{6,7},{9,8},{10,9},{11,10},{12,13},{... | collective-permute-start | bytes 983048 | tf_op jit(solution)/shard_map/ppermute | solution.py:497
  99.7 12.5 %collective-permute-start.22 = (bf16[256,640]{1,0:T(8,128)(2,1)S(1)}, bf16[256,640]{1,0:T(8,128)(2,1)S(1)}, u32[]{:S(2)}, u32[]{:S(2)}) collective-permute-start(bf16[256,640]{1,0:T(8,128)(2,1)S(1)} %get-tuple-element.71), channel_id=1, source_target_pairs={{1,0},{2,1},{3,2},{4,5},{5,6},{6,7},{9,8},{10,9},{11,10},{12,13},{... | collective-permute-start | bytes 983048 | tf_op jit(solution)/shard_map/ppermute | solution.py:497
  106.3 15.7 %collective-permute-start.24 = (bf16[256,640]{1,0:T(8,128)(2,1)S(1)}, bf16[256,640]{1,0:T(8,128)(2,1)S(1)}, u32[]{:S(2)}, u32[]{:S(2)}) collective-permute-start(bf16[256,640]{1,0:T(8,128)(2,1)S(1)} %get-tuple-element.74), channel_id=1, source_target_pairs={{0,1},{1,2},{2,3},{5,4},{6,5},{7,6},{8,9},{9,10},{10,11},{13,12},{... | collective-permute-start | bytes 983048 | tf_op jit(solution)/shard_map/ppermute | solution.py:497
  107.9 14.2 %collective-permute-start.26 = (bf16[256,640]{1,0:T(8,128)(2,1)S(1)}, bf16[256,640]{1,0:T(8,128)(2,1)S(1)}, u32[]{:S(2)}, u32[]{:S(2)}) collective-permute-start(bf16[256,640]{1,0:T(8,128)(2,1)S(1)} %get-tuple-element.76), channel_id=1, source_target_pairs={{1,0},{2,1},{3,2},{4,5},{5,6},{6,7},{9,8},{10,9},{11,10},{12,13},{... | collective-permute-start | bytes 983048 | tf_op jit(solution)/shard_map/ppermute | solution.py:497
  130.0 21.2 %collective-permute-start.28 = (bf16[2,320,1280]{2,1,0:T(8,128)(2,1)S(1)}, bf16[2,320,1280]{2,1,0:T(8,128)(2,1)S(1)}, u32[]{:S(2)}, u32[]{:S(2)}) collective-permute-start(bf16[2,320,1280]{2,1,0:T(8,128)(2,1)S(1)} %add_convert_fusion), channel_id=1, source_target_pairs={{0,8},{4,20},{8,0},{12,28},{16,24},{20,4},{24,16},{28,12},{1,9},{5... | collective-permute-start | bytes 4915208 | tf_op jit(solution)/shard_map/ppermute | solution.py:487
  131.5 32.3 %collective-permute-start.29 = (bf16[3,128,640]{2,1,0:T(8,128)(2,1)S(1)}, bf16[3,128,640]{2,1,0:T(8,128)(2,1)S(1)}, u32[]{:S(2)}, u32[]{:S(2)}) collective-permute-start(bf16[3,128,640]{2,1,0:T(8,128)(2,1)S(1)} %get-tuple-element.79), channel_id=1, source_target_pairs={{0,3},{1,0},{2,1},{3,2},{4,7},{5,4},{6,5},{7,6},{8,11},{9,8},{10,9... | collective-permute-start | bytes 1474568 | tf_op jit(solution)/shard_map/ppermute | solution.py:477
  132.5 43.2 %collective-permute-start.30 = (bf16[3,128,640]{2,1,0:T(8,128)(2,1)S(1)}, bf16[3,128,640]{2,1,0:T(8,128)(2,1)S(1)}, u32[]{:S(2)}, u32[]{:S(2)}) collective-permute-start(bf16[3,128,640]{2,1,0:T(8,128)(2,1)S(1)} %get-tuple-element.80), channel_id=1, source_target_pairs={{0,2},{1,3},{2,0},{3,1},{4,6},{5,7},{6,4},{7,5},{8,10},{9,11},{10,... | collective-permute-start | bytes 1474568 | tf_op jit(solution)/shard_map/ppermute | solution.py:477
  134.2 41.5 %collective-permute-start.31 = (bf16[3,128,640]{2,1,0:T(8,128)(2,1)S(1)}, bf16[3,128,640]{2,1,0:T(8,128)(2,1)S(1)}, u32[]{:S(2)}, u32[]{:S(2)}) collective-permute-start(bf16[3,128,640]{2,1,0:T(8,128)(2,1)S(1)} %get-tuple-element.81), channel_id=1, source_target_pairs={{0,1},{1,2},{2,3},{3,0},{4,5},{5,6},{6,7},{7,4},{8,9},{9,10},{10,1... | collective-permute-start | bytes 1474568 | tf_op jit(solution)/shard_map/ppermute | solution.py:477
  151.9 25.7 %collective-permute-start.32 = (bf16[160,1280]{1,0:T(8,128)(2,1)S(1)}, bf16[160,1280]{1,0:T(8,128)(2,1)S(1)}, u32[]{:S(2)}, u32[]{:S(2)}) collective-permute-start(bf16[160,1280]{1,0:T(8,128)(2,1)S(1)} %get-tuple-element.95), channel_id=1, source_target_pairs={{0,16},{4,12},{8,24},{12,4},{16,0},{20,28},{24,8},{28,20},{1,17},{... | collective-permute-start | bytes 1228808 | tf_op jit(solution)/shard_map/ppermute | solution.py:487
  152.5 25.1 %collective-permute-start.33 = (bf16[160,1280]{1,0:T(8,128)(2,1)S(1)}, bf16[160,1280]{1,0:T(8,128)(2,1)S(1)}, u32[]{:S(2)}, u32[]{:S(2)}) collective-permute-start(bf16[160,1280]{1,0:T(8,128)(2,1)S(1)} %get-tuple-element.96), channel_id=1, source_target_pairs={{0,16},{4,12},{8,24},{12,4},{16,0},{20,28},{24,8},{28,20},{1,17},{... | collective-permute-start | bytes 1228808 | tf_op jit(solution)/shard_map/ppermute | solution.py:487
  (17 other events, 168.1 us)

commit v7 on v6

--- a/solution.py
+++ b/solution.py
@@ -97,8 +97,8 @@
     slabs = n // PARTS
 
     def body(place_ref, *refs):
-        in_refs, out_ref = refs[: len(inputs)], refs[len(inputs)]
-        kept_refs = refs[len(inputs) + 1 :] if first else in_refs
+        in_refs, (out_ref, exp_ref, inverse_ref) = refs[: len(inputs)], refs[len(inputs) :][:3]
+        kept_refs = refs[len(inputs) + 3 :] if first else in_refs
         if first:
             for t in range(3):
                 for s in range(n):
@@ -118,7 +118,9 @@
             if h + 1 < len(every):
                 ready = scores_of(every[h + 1])
             shifted, inverse = exponentials(scores)
-            out = dot(kept_refs[2][:, lanes], shifted.astype(BF16), ((0,), (0,))) * inverse
+            shifted = shifted.astype(BF16)
+            exp_ref[h], inverse_ref[h] = shifted, inverse
+            out = dot(kept_refs[2][:, lanes], shifted, ((0,), (0,))) * inverse
             out_ref[:, lanes] = out.T.astype(BF16)
 
     def spec(*shape):
@@ -128,15 +130,22 @@
         return jax.ShapeDtypeStruct(shape, BF16)
 
     kept = [(length, width)] * (3 * first)
+    heads, cols = width // HEAD_DIM, length // PARTS
     outs = pl.pallas_call(
         body,
         grid_spec=pltpu.PrefetchScalarGridSpec(
             num_scalar_prefetch=1,
             grid=(1,),
             in_specs=[spec(*x.shape) for x in inputs],
-            out_specs=[spec(length // PARTS, width)] + [spec(*k) for k in kept],
-        ),
-        out_shape=[out_of(length // PARTS, width)] + [out_of(*k) for k in kept],
+            out_specs=[spec(cols, width), spec(heads, length, cols), spec(heads, 1, cols)]
+            + [spec(*k) for k in kept],
+        ),
+        out_shape=[
+            out_of(cols, width),
+            out_of(heads, length, cols),
+            jax.ShapeDtypeStruct((heads, 1, cols), F32),
+        ]
+        + [out_of(*k) for k in kept],
         compiler_params=params(),
         cost_estimate=cost(
             4 * length * length * width // PARTS,
@@ -145,54 +154,53 @@
         ),
         name="attention_heads",
     )(place, *inputs)
-    return outs[0], list(outs[1:])
-
-
-def attention_grad_call(place, kept, attention, parts, d_terms, n):
+    return outs[0], outs[1:3], list(outs[3:])
+
+
+def attention_grad_call(place, kept, weights, attention, parts, d_terms, n):
     length, width = kept[0].shape
-    rows, block = length // n, length // PARTS
+    rows, block, heads = length // n, length // PARTS, width // HEAD_DIM
     n_terms = len(d_terms)
     scale = HEAD_DIM ** (-0.5)
 
     def body(place_ref, *refs):
-        kept_refs, attn_refs = refs[:3], refs[3 : 3 + PARTS]
-        part_ref, term_refs = refs[3 + PARTS], refs[4 + PARTS : 4 + PARTS * (1 + n_terms)]
-        out_refs, (attn_held, d_held) = refs[4 + PARTS * (1 + n_terms) : -2], refs[-2:]
-        places = slab_rows(place_ref[0], n, rows)
+        kept_refs, refs = refs[:3], refs[3:]
+        weight_refs, refs = refs[: 2 * PARTS], refs[2 * PARTS :]
+        attn_refs, part_ref, refs = refs[:PARTS], refs[PARTS], refs[PARTS + 1 :]
+        term_refs, refs = refs[: PARTS * n_terms], refs[PARTS * n_terms :]
+        out_refs, (attn_held, d_held, query_grad) = refs[:n], refs[n:]
+        me = place_ref[0]
+        wanted = slab_rows(me, n, rows)
         for i in range(PARTS):
             here = slice(i * block, (i + 1) * block)
             attn_held[here] = attn_refs[i][...]
             terms = [term_refs[t * PARTS + i][...].astype(F32) for t in range(n_terms)]
             d_held[here] = sum(terms, part_ref[i, 0].astype(F32)).astype(BF16)
-        def scores_of(lanes):
-            k = kept_refs[1][:, lanes]
-            return dot(k, kept_refs[0][:, lanes], ((1,), (1,)))
 
         def d_of(lanes):
-            d_attn = jnp.concatenate([d_held[p, lanes] for p in places], axis=0)
-            return d_attn, dot(kept_refs[2][:, lanes], d_attn, ((1,), (1,)))
+            return dot(kept_refs[2][:, lanes], d_held[:, lanes], ((1,), (1,)))
 
         every = head_lanes(width)
-        ready = (scores_of(every[0]), d_of(every[0]))
+        ready = d_of(every[0])
         for h, lanes in enumerate(every):
-            scores, (d_attn, d_prob) = ready
+            d_prob = ready
             if h + 1 < len(every):
-                ready = (scores_of(every[h + 1]), d_of(every[h + 1]))
-            q, k, v = (r[:, lanes] for r in kept_refs)
-            attn = jnp.concatenate([attn_held[p, lanes] for p in places], axis=0).astype(F32)
-            shifted, inverse = exponentials(scores)
-            prob = shifted * inverse
+                ready = d_of(every[h + 1])
+            q = jnp.concatenate([kept_refs[0][w, lanes] for w in wanted], axis=0)
+            shifted = jnp.concatenate([r[h] for r in weight_refs[::2]], axis=1).astype(F32)
+            inverse = jnp.concatenate([r[h] for r in weight_refs[1::2]], axis=1)
+            prob, d_attn = shifted * inverse, d_held[:, lanes]
+            attn = attn_held[:, lanes].astype(F32)
             delta = jnp.sum(d_attn.astype(F32) * attn, axis=1, keepdims=True).T
             d_half = (prob * (d_prob - delta) * scale).astype(BF16)
-            grads = (
-                dot(k, d_half, ((0,), (0,))).T,
-                dot(d_half, q, ((1,), (0,))),
-                dot(prob.astype(BF16), d_attn, ((1,), (0,))),
-            )
-            for t in range(3):
+            query_grad[:, lanes] = dot(kept_refs[1][:, lanes], d_half, ((0,), (0,))).T.astype(BF16)
+            grads = dot(d_half, q, ((1,), (0,))), dot(prob.astype(BF16), d_attn, ((1,), (0,)))
+            for t in range(2):
                 g = grads[t].astype(BF16)
                 for s in range(n):
-                    out_refs[s][t, :, lanes] = g[s * rows : (s + 1) * rows]
+                    out_refs[s][1 + t, :, lanes] = g[s * rows : (s + 1) * rows]
+        for s in range(n):
+            out_refs[s][0] = query_grad[wanted[s], :]
 
     def spec(*shape):
         return pl.BlockSpec(shape, lambda i, p: (0,) * len(shape))
@@ -203,11 +211,12 @@
             num_scalar_prefetch=1,
             grid=(1,),
             in_specs=[spec(length, width)] * 3
+            + [spec(heads, length, block), spec(heads, 1, block)] * PARTS
             + [spec(block, width)] * PARTS
             + [spec(PARTS, 1, block, width)]
             + [spec(block, width)] * (PARTS * n_terms),
             out_specs=[spec(3, rows, width)] * n,
-            scratch_shapes=[pltpu.VMEM((length, width), BF16)] * 2,
+            scratch_shapes=[pltpu.VMEM((length, width), BF16)] * 3,
         ),
         out_shape=[jax.ShapeDtypeStruct((3, rows, width), BF16)] * n,
         compiler_params=params(),
@@ -215,7 +224,7 @@
             200 * length * length * width, 24 * length * width, length * length * width // HEAD_DIM
         ),
         name="attention_heads_grad",
-    )(place, *kept, *attention, parts, *sum(d_terms, []))
+    )(place, *kept, *sum(weights, []), *attention, parts, *sum(d_terms, []))
 
 
 def ahead(place_ref, s, n):
@@ -558,8 +567,12 @@
     shards = [out_weight, one, two, far, own, swap(one, "dp", 1), swap(two, "dp", 1)]
     shards += [swap(x, "dp", 1) for x in jnp.split(after(far, d_proj), FAR_PARTS)]
     parts = d_attn_parts_call(place, d_proj, shards, n)
-    attended, kept = attention_call(place, after(pieces, parts), 0, n)
-    attention = [attended] + [attention_call(place, kept, g, n)[0] for g in range(1, PARTS)]
+    attended, exps, kept = attention_call(place, after(pieces, parts), 0, n)
+    attention, weights = [attended], [list(exps)]
+    for g in range(1, PARTS):
+        attended, exps, _ = attention_call(place, kept, g, n)
+        attention.append(attended)
+        weights.append(list(exps))
 
     def both_ways(forward, back):
         return line_move(forward, "dp", "ctx", True), line_move(back, "dp", "ctx", False)
@@ -581,7 +594,7 @@
     front = [[got[g][i][1] for i in range(n - 1)] for g in range(PARTS)]
     d_terms = [[got[g][-1][i] for g in range(PARTS)] for i in range(2)]
 
-    grads = attention_grad_call(place, kept, attention, parts, d_terms, n)
+    grads = attention_grad_call(place, kept, weights, attention, parts, d_terms, n)
     received = after(received, grads)
     far = add_rounded(keep[2:], received[2:])
     grads = [grads[0]] + [shift(grads[s], "ctx", -s) for s in range(1, n)]

time: 180 us -> 180 us (level)
  no operation moved by 1% of the time
where the time goes in v7:
time: 180 us; the launch traced here: 179 us
  waiting for transfers between devices  75.9 us (42%)
  starting transfers between devices  49.5 us (28%)
  Pallas kernels  43.1 us (24%)
  local copies, waits for them, and re-layouts  4.66 us (3%)
  other arithmetic  4.05 us (2%)
    ppermute x16, starting transfers between devices, line_move(): return lax.ppermute(x, (dp_axis, axis), pairs)  30.7 us
    ppermute x6, waiting for transfers between devices, chip_swap(): lax.ppermute(x, axis, [(i, i ^ (2 if (i + step) % 2 == 0 else 4)) for i i...  28.1 us
    ppermute x6, waiting for transfers between devices, shift(): return lax.ppermute(x, axis, [(i, (i + by) % n) for i in range(n)])  26.4 us
    ppermute x16, waiting for transfers between devices, line_move(): return lax.ppermute(x, (dp_axis, axis), pairs)  19.5 us
    pallas_call x1, Pallas kernels, projection_call(): pl.pallas_call(body, grid_spec=pltpu.PrefetchScalarGridSpec(num_scalar_pr...  9.75 us
    pallas_call x1, Pallas kernels, d_attn_parts_call(): pl.pallas_call(body, grid_spec=pltpu.PrefetchScalarGridSpec(num_scalar_pr...  9.33 us
    ppermute x6, starting transfers between devices, shift(): return lax.ppermute(x, axis, [(i, (i + by) % n) for i in range(n)])  8.96 us
    ppermute x6, starting transfers between devices, chip_swap(): lax.ppermute(x, axis, [(i, i ^ (2 if (i + step) % 2 == 0 else 4)) for i i...  8.7 us
  transfers between devices with their start and end apart: 34, of which 15 were waited for; matrix products, arithmetic and copies ran while one was open for 2% of the time, Pallas kernels for 21%

profile of v7, /device:TPU:0, one launch (start us, length us, event | category | flops | bytes accessed | tf_op | source)
XLA Modules:
  0.0 179.0 jit_solution(2910474002533639545)
XLA Ops:
  0.6 2.6 %pack_heads.1 = (bf16[3,128,640]{2,1,0:T(8,128)(2,1)}, bf16[3,128,640]{2,1,0:T(8,128)(2,1)}, bf16[3,128,640]{2,1,0:T(8,128)(2,1)}, bf16[3,128,640]{2,1,0:T(8,128)(2,1)}) custom-call(bf16[1,128,2560]{2,1,0:T(8,128)(2,1)} %refs_0_.2, bf16[1,128,2560]{2,1,0:T(8,128)(2,1)} %refs_1_.1, bf16[1,128,2560]{2,1,0:T(8,128)(2,1)} %refs_2_.1), custom_call_target="tpu_custom_call" | custom-call | bytes 3932160 | tf_op jit(solution)/shard_map/pack_heads/pallas_call | solution.py:77
  3.2 3.0 %collective-permute-start.3 = (bf16[320,1280]{1,0:T(8,128)(2,1)S(1)}, bf16[320,1280]{1,0:T(8,128)(2,1)}, u32[]{:S(2)}, u32[]{:S(2)}) collective-permute-start(bf16[320,1280]{1,0:T(8,128)(2,1)S(1)} %copy-done), channel_id=1, source_target_pairs={{0,8},{4,20},{8,0},{12,28},{16,24},{20,4},{24,16},{28,12},{1,9},{5... | collective-permute-start | bytes 2457608 | tf_op jit(solution)/shard_map/ppermute | solution.py:496
  7.8 13.2 %collective-permute-done.refs_1_ = bf16[3,128,640]{2,1,0:T(8,128)(2,1)S(1)} collective-permute-done((bf16[3,128,640]{2,1,0:T(8,128)(2,1)}, bf16[3,128,640]{2,1,0:T(8,128)(2,1)S(1)}, u32[]{:S(2)}, u32[]{:S(2)}) %collective-permute-start) | collective-permute-done | bytes 491552 | tf_op jit(solution)/shard_map/ppermute | solution.py:486
  28.1 6.2 %collective-permute-done.5.refs_3_.refs_17_ = bf16[320,1280]{1,0:T(8,128)(2,1)S(1)} collective-permute-done((bf16[320,1280]{1,0:T(8,128)(2,1)}, bf16[320,1280]{1,0:T(8,128)(2,1)S(1)}, u32[]{:S(2)}, u32[]{:S(2)}) %collective-permute-start.5) | collective-permute-done | bytes 819232 | tf_op jit(solution)/shard_map/ppermute | solution.py:496
  36.1 7.1 %collective-permute-done.4.refs_2_.refs_16_ = bf16[320,1280]{1,0:T(8,128)(2,1)} collective-permute-done((bf16[320,1280]{1,0:T(8,128)(2,1)S(1)}, bf16[320,1280]{1,0:T(8,128)(2,1)}, u32[]{:S(2)}, u32[]{:S(2)}) %collective-permute-start.4) | collective-permute-done | bytes 819232 | tf_op jit(solution)/shard_map/ppermute | solution.py:496
  48.8 9.3 %d_attn_parts.1.part_f.part_b.refs_9_ = bf16[2,4,256,640]{3,2,1,0:T(8,128)(2,1)S(1)} custom-call(s32[3]{0:T(128)S(1)} %pad_add_fusion.place_ref, bf16[512,1280]{1,0:T(8,128)(2,1)S(1)} %fusion.d_ref, bf16[320,1280]{1,0:T(8,128)(2,1)S(1)} %copy-done, bf16[320,1280]{1,0:T(8,128)(2,1)} %collective-permute-done.3.refs_1_.refs_15_, ...), custom_call_target="tpu_custom_call" | custom-call | tf_op jit(solution)/shard_map/d_attn_parts/pallas_call | solution.py:325
  58.2 3.3 %attention_heads.2 = (bf16[256,640]{1,0:T(8,128)(2,1)S(1)}, bf16[5,512,256]{2,1,0:T(8,128)(2,1)S(1)}, f32[5,1,256]{2,1,0:T(1,128)S(1)}, bf16[512,640]{1,0:T(8,12...) custom-call(s32[3]{0:T(128)S(1)} %pad_add_fusion.place_ref, bf16[3,128,640]{2,1,0:T(8,128)(2,1)S(1)} %copy-done.4, ...), custom_call_target="tpu_custom_call" | custom-call | flops 335544320 | bytes 3276800 | tf_op jit(solution)/shard_map/attention_heads/pallas_call | solution.py:134
  62.8 4.6 %collective-permute-start.11 = (bf16[256,640]{1,0:T(8,128)(2,1)S(1)}, bf16[256,640]{1,0:T(8,128)(2,1)S(1)}, u32[]{:S(2)}, u32[]{:S(2)}) collective-permute-start(bf16[256,640]{1,0:T(8,128)(2,1)S(1)} %get-tuple-element.65.refs_0_.refs_1_.refs_7_), channel_id=1, source_target_pairs={{0,1},{1,2},{2,3},{5,4},{6,5},{7,6},{8,9},{9,10},{10,11},{13,12},{... | collective-permute-start | bytes 983048 | tf_op jit(solution)/shard_map/ppermute | solution.py:506
  67.4 2.0 %attention_heads.3 = (bf16[256,640]{1,0:T(8,128)(2,1)S(1)}, bf16[5,512,256]{2,1,0:T(8,128)(2,1)S(1)}, f32[5,1,256]{2,1,0:T(1,128)S(1)}) custom-call(s32[3]{0:T(128)S(1)} %pad_add_fusion.place_ref, bf16[512,640]{1,0:T(8,128)(2,1)S(1)} %get-tuple-element.66.refs_0_, bf16[512,640]{1,0:T(8,128)(2,1)S(1)} %get-tuple-element.67.refs_1_, ...), custom_call_target="tpu_custom_call" | custom-call | flops 335544320 | bytes 3276800 | tf_op jit(solution)/shard_map/attention_heads/pallas_call | solution.py:134
  70.7 4.6 %collective-permute-start.15 = (bf16[256,640]{1,0:T(8,128)(2,1)S(1)}, bf16[256,640]{1,0:T(8,128)(2,1)S(1)}, u32[]{:S(2)}, u32[]{:S(2)}) collective-permute-start(bf16[256,640]{1,0:T(8,128)(2,1)S(1)} %get-tuple-element.69.refs_2_.refs_3_.refs_8_.refs_1_), channel_id=1, source_target_pairs={{0,1},{1,2},{2,3},{5,4},{6,5},{7,6},{8,9},{9,10},{10,11},{13,12},{... | collective-permute-start | bytes 983048 | tf_op jit(solution)/shard_map/ppermute | solution.py:506
  76.0 2.2 %collective-permute-start.13 = (bf16[256,640]{1,0:T(8,128)(2,1)S(1)}, bf16[256,640]{1,0:T(8,128)(2,1)S(1)}, u32[]{:S(2)}, u32[]{:S(2)}) collective-permute-start(bf16[256,640]{1,0:T(8,128)(2,1)S(1)} %get-tuple-element.70), channel_id=1, source_target_pairs={{0,1},{1,2},{2,3},{5,4},{6,5},{7,6},{8,9},{9,10},{10,11},{13,12},{... | collective-permute-start | bytes 983048 | tf_op jit(solution)/shard_map/ppermute | solution.py:506
  79.5 2.4 %collective-permute-done.16.back.refs_11_ = bf16[256,640]{1,0:T(8,128)(2,1)S(1)} collective-permute-done((bf16[256,640]{1,0:T(8,128)(2,1)S(1)}, bf16[256,640]{1,0:T(8,128)(2,1)S(1)}, u32[]{:S(2)}, u32[]{:S(2)}) %collective-permute-start.16) | collective-permute-done | bytes 327712 | tf_op jit(solution)/shard_map/ppermute | solution.py:506
  82.6 2.3 %collective-permute-start.17 = (bf16[256,640]{1,0:T(8,128)(2,1)S(1)}, bf16[256,640]{1,0:T(8,128)(2,1)S(1)}, u32[]{:S(2)}, u32[]{:S(2)}) collective-permute-start(bf16[256,640]{1,0:T(8,128)(2,1)S(1)} %get-tuple-element.72), channel_id=1, source_target_pairs={{0,1},{1,2},{2,3},{5,4},{6,5},{7,6},{8,9},{9,10},{10,11},{13,12},{... | collective-permute-start | bytes 983048 | tf_op jit(solution)/shard_map/ppermute | solution.py:506
  86.5 4.1 %collective-permute-done.14.back.refs_5_.refs_9_ = bf16[256,640]{1,0:T(8,128)(2,1)S(1)} collective-permute-done((bf16[256,640]{1,0:T(8,128)(2,1)S(1)}, bf16[256,640]{1,0:T(8,128)(2,1)S(1)}, u32[]{:S(2)}, u32[]{:S(2)}) %collective-permute-start.14) | collective-permute-done | bytes 327712 | tf_op jit(solution)/shard_map/ppermute | solution.py:506
  91.3 2.0 %collective-permute-start.19 = (bf16[256,640]{1,0:T(8,128)(2,1)S(1)}, bf16[256,640]{1,0:T(8,128)(2,1)S(1)}, u32[]{:S(2)}, u32[]{:S(2)}) collective-permute-start(bf16[256,640]{1,0:T(8,128)(2,1)S(1)} %get-tuple-element.74), channel_id=1, source_target_pairs={{0,1},{1,2},{2,3},{5,4},{6,5},{7,6},{8,9},{9,10},{10,11},{13,12},{... | collective-permute-start | bytes 983048 | tf_op jit(solution)/shard_map/ppermute | solution.py:506
  94.6 3.1 %collective-permute-done.18.back.refs_7_.refs_12_ = bf16[256,640]{1,0:T(8,128)(2,1)S(1)} collective-permute-done((bf16[256,640]{1,0:T(8,128)(2,1)S(1)}, bf16[256,640]{1,0:T(8,128)(2,1)S(1)}, u32[]{:S(2)}, u32[]{:S(2)}) %collective-permute-start.18) | collective-permute-done | bytes 327712 | tf_op jit(solution)/shard_map/ppermute | solution.py:506
  101.2 4.6 %collective-permute-done.21.refs_13_.back.refs_10_ = bf16[256,640]{1,0:T(8,128)(2,1)S(1)} collective-permute-done((bf16[256,640]{1,0:T(8,128)(2,1)S(1)}, bf16[256,640]{1,0:T(8,128)(2,1)S(1)}, u32[]{:S(2)}, u32[]{:S(2)}) %collective-permute-start.21) | collective-permute-done | bytes 327712 | tf_op jit(solution)/shard_map/ppermute | solution.py:506
  109.3 3.0 %collective-permute-done.22.refs_15_.back.refs_13_ = bf16[256,640]{1,0:T(8,128)(2,1)S(1)} collective-permute-done((bf16[256,640]{1,0:T(8,128)(2,1)S(1)}, bf16[256,640]{1,0:T(8,128)(2,1)S(1)}, u32[]{:S(2)}, u32[]{:S(2)}) %collective-permute-start.22) | collective-permute-done | bytes 327712 | tf_op jit(solution)/shard_map/ppermute | solution.py:506
  116.1 6.0 %weight_grad.1 = (bf16[4,320,1280]{2,1,0:T(8,128)(2,1)S(1)}, bf16[4,320,1280]{2,1,0:T(8,128)(2,1)S(1)}) custom-call(s32[3]{0:T(128)S(1)} %pad_add_fusion.place_ref, bf16[512,1280]{1,0:T(8,128)(2,1)S(1)} %fusion.d_ref, bf16[256,640]{1,0:T(8,128)(2,1)S(1)} %get-tuple-element.65.refs_0_.refs_1_.refs_7_, ...), custom_call_target="tpu_custom_call" | custom-call | flops 3355443200 | bytes 13107200 | tf_op jit(solution)/shard_map/weight_grad/pallas_call | solution.py:427
  124.0 4.2 %attention_heads_grad.1 = (bf16[3,128,640]{2,1,0:T(8,128)(2,1)S(1)}, bf16[3,128,640]{2,1,0:T(8,128)(2,1)S(1)}, bf16[3,128,640]{2,1,0:T(8,128)(2,1)S(1)}, bf16[3,128,640]{2,1,0:T(8,128)(2,1)S(1)}) custom-call(s32[3]{0:T(128)S(1)} %pad_add_fusion.place_ref, bf16[512,640]{1,0:T(8,128)(2,1)S(1)} %get-tuple-element.66.refs_0_, ...), custom_call_target="tpu_custom_call" | custom-call | flops 33554432000 | bytes 7864320 | tf_op jit(solution)/shard_map/attention_heads_grad/pallas_call | solution.py:208
  130.3 2.4 %collective-permute-start.29 = (bf16[3,128,640]{2,1,0:T(8,128)(2,1)S(1)}, bf16[3,128,640]{2,1,0:T(8,128)(2,1)S(1)}, u32[]{:S(2)}, u32[]{:S(2)}) collective-permute-start(bf16[3,128,640]{2,1,0:T(8,128)(2,1)S(1)} %get-tuple-element.89), channel_id=1, source_target_pairs={{0,3},{1,0},{2,1},{3,2},{4,7},{5,4},{6,5},{7,6},{8,11},{9,8},{10,9... | collective-permute-start | bytes 1474568 | tf_op jit(solution)/shard_map/ppermute | solution.py:486
  135.2 14.7 %collective-permute-done.28 = bf16[2,320,1280]{2,1,0:T(8,128)(2,1)S(1)} collective-permute-done((bf16[2,320,1280]{2,1,0:T(8,128)(2,1)S(1)}, bf16[2,320,1280]{2,1,0:T(8,128)(2,1)S(1)}, u32[]{:S(2)}, u32[]{:S(2)}) %collective-permute-start.28) | collective-permute-done | bytes 1638432 | tf_op jit(solution)/shard_map/ppermute | solution.py:496
  152.8 9.7 %projection.1 = bf16[512,1280]{1,0:T(8,128)(2,1)} custom-call(s32[3]{0:T(128)S(1)} %pad_add_fusion.place_ref, f32[1,1280]{1,0:T(1,128)S(1)} %get-tuple-element.93.gate_ref, bf16[256,640]{1,0:T(8,128)(2,1)S(1)} %get-tuple-element.65.refs_0_.refs_1_.refs_7_, bf16[256,640]{1,0:T(8,128)(2,1)S(1)} %get-tuple-element.69.refs_2_.refs_3_.refs_8_.refs_1_, ...), custom_call_target="tpu_custom_call" | custom-call | tf_op jit(solution)/shard_map/projection/pallas_call | solution.py:364
  162.5 13.2 %collective-permute-done.30.refs_2_ = bf16[3,128,640]{2,1,0:T(8,128)(2,1)S(1)} collective-permute-done((bf16[3,128,640]{2,1,0:T(8,128)(2,1)S(1)}, bf16[3,128,640]{2,1,0:T(8,128)(2,1)S(1)}, u32[]{:S(2)}, u32[]{:S(2)}) %collective-permute-start.30) | collective-permute-done | bytes 491552 | tf_op jit(solution)/shard_map/ppermute | solution.py:486
  (80 shorter events, 47.4 us)
Async XLA Ops:
  3.2 18.6 %collective-permute-start.3 = (bf16[320,1280]{1,0:T(8,128)(2,1)S(1)}, bf16[320,1280]{1,0:T(8,128)(2,1)}, u32[]{:S(2)}, u32[]{:S(2)}) collective-permute-start(bf16[320,1280]{1,0:T(8,128)(2,1)S(1)} %copy-done), channel_id=1, source_target_pairs={{0,8},{4,20},{8,0},{12,28},{16,24},{20,4},{24,16},{28,12},{1,9},{5... | collective-permute-start | bytes 2457608 | tf_op jit(solution)/shard_map/ppermute | solution.py:496
  6.2 14.8 %collective-permute-start = (bf16[3,128,640]{2,1,0:T(8,128)(2,1)}, bf16[3,128,640]{2,1,0:T(8,128)(2,1)S(1)}, u32[]{:S(2)}, u32[]{:S(2)}) collective-permute-start(bf16[3,128,640]{2,1,0:T(8,128)(2,1)} %get-tuple-element.54), channel_id=1, source_target_pairs={{0,1},{1,2},{2,3},{3,0},{4,5},{5,6},{6,7},{7,4},{8,9},{9,10},{10,1... | collective-permute-start | bytes 1474568 | tf_op jit(solution)/shard_map/ppermute | solution.py:486
  21.8 12.6 %collective-permute-start.5 = (bf16[320,1280]{1,0:T(8,128)(2,1)}, bf16[320,1280]{1,0:T(8,128)(2,1)S(1)}, u32[]{:S(2)}, u32[]{:S(2)}) collective-permute-start(bf16[320,1280]{1,0:T(8,128)(2,1)} %collective-permute-done.3.refs_1_.refs_15_), channel_id=1, source_target_pairs={{0,16},{4,12},{8,24},{12,4},{16,0},{20,28},{24,8},{28,20},{1,17},{... | collective-permute-start | bytes 2457608 | tf_op jit(solution)/shard_map/ppermute | solution.py:496
  22.3 20.9 %collective-permute-start.4 = (bf16[320,1280]{1,0:T(8,128)(2,1)S(1)}, bf16[320,1280]{1,0:T(8,128)(2,1)}, u32[]{:S(2)}, u32[]{:S(2)}) collective-permute-start(bf16[320,1280]{1,0:T(8,128)(2,1)S(1)} %copy-done), channel_id=1, source_target_pairs={{0,16},{4,12},{8,24},{12,4},{16,0},{20,28},{24,8},{28,20},{1,17},{... | collective-permute-start | bytes 2457608 | tf_op jit(solution)/shard_map/ppermute | solution.py:496
  23.8 34.4 %collective-permute-start.1 = (bf16[3,128,640]{2,1,0:T(8,128)(2,1)}, bf16[3,128,640]{2,1,0:T(8,128)(2,1)}, u32[]{:S(2)}, u32[]{:S(2)}) collective-permute-start(bf16[3,128,640]{2,1,0:T(8,128)(2,1)} %get-tuple-element.55), channel_id=1, source_target_pairs={{0,2},{1,3},{2,0},{3,1},{4,6},{5,7},{6,4},{7,5},{8,10},{9,11},{10,... | collective-permute-start | bytes 1474568 | tf_op jit(solution)/shard_map/ppermute | solution.py:486
  24.6 19.6 %collective-permute-start.6 = (bf16[320,1280]{1,0:T(8,128)(2,1)S(1)}, bf16[320,1280]{1,0:T(8,128)(2,1)}, u32[]{:S(2)}, u32[]{:S(2)}) collective-permute-start(bf16[320,1280]{1,0:T(8,128)(2,1)S(1)} %copy-done), channel_id=1, source_target_pairs={{0,4},{4,0},{8,12},{12,8},{16,20},{20,16},{24,28},{28,24},{1,5},{5... | collective-permute-start | bytes 2457608 | tf_op jit(solution)/shard_map/ppermute | solution.py:491
  26.0 18.7 %collective-permute-start.7 = (bf16[320,1280]{1,0:T(8,128)(2,1)}, bf16[320,1280]{1,0:T(8,128)(2,1)S(1)}, u32[]{:S(2)}, u32[]{:S(2)}) collective-permute-start(bf16[320,1280]{1,0:T(8,128)(2,1)} %collective-permute-done.3.refs_1_.refs_15_), channel_id=1, source_target_pairs={{0,4},{4,0},{8,12},{12,8},{16,20},{20,16},{24,28},{28,24},{1,5},{5... | collective-permute-start | bytes 2457608 | tf_op jit(solution)/shard_map/ppermute | solution.py:491
  34.3 23.9 %collective-permute-start.2 = (bf16[3,128,640]{2,1,0:T(8,128)(2,1)}, bf16[3,128,640]{2,1,0:T(8,128)(2,1)}, u32[]{:S(2)}, u32[]{:S(2)}) collective-permute-start(bf16[3,128,640]{2,1,0:T(8,128)(2,1)} %get-tuple-element.56), channel_id=1, source_target_pairs={{0,3},{1,0},{2,1},{3,2},{4,7},{5,4},{6,5},{7,6},{8,11},{9,8},{10,9... | collective-permute-start | bytes 1474568 | tf_op jit(solution)/shard_map/ppermute | solution.py:486
  61.5 13.8 %collective-permute-start.12 = (bf16[256,640]{1,0:T(8,128)(2,1)S(1)}, bf16[256,640]{1,0:T(8,128)(2,1)S(1)}, u32[]{:S(2)}, u32[]{:S(2)}) collective-permute-start(bf16[256,640]{1,0:T(8,128)(2,1)S(1)} %get-tuple-element.65.refs_0_.refs_1_.refs_7_), channel_id=1, source_target_pairs={{1,0},{2,1},{3,2},{4,5},{5,6},{6,7},{9,8},{10,9},{11,10},{12,13},{... | collective-permute-start | bytes 983048 | tf_op jit(solution)/shard_map/ppermute | solution.py:506
  62.8 12.5 %collective-permute-start.11 = (bf16[256,640]{1,0:T(8,128)(2,1)S(1)}, bf16[256,640]{1,0:T(8,128)(2,1)S(1)}, u32[]{:S(2)}, u32[]{:S(2)}) collective-permute-start(bf16[256,640]{1,0:T(8,128)(2,1)S(1)} %get-tuple-element.65.refs_0_.refs_1_.refs_7_), channel_id=1, source_target_pairs={{0,1},{1,2},{2,3},{5,4},{6,5},{7,6},{8,9},{9,10},{10,11},{13,12},{... | collective-permute-start | bytes 983048 | tf_op jit(solution)/shard_map/ppermute | solution.py:506
  69.4 12.5 %collective-permute-start.16 = (bf16[256,640]{1,0:T(8,128)(2,1)S(1)}, bf16[256,640]{1,0:T(8,128)(2,1)S(1)}, u32[]{:S(2)}, u32[]{:S(2)}) collective-permute-start(bf16[256,640]{1,0:T(8,128)(2,1)S(1)} %get-tuple-element.69.refs_2_.refs_3_.refs_8_.refs_1_), channel_id=1, source_target_pairs={{1,0},{2,1},{3,2},{4,5},{5,6},{6,7},{9,8},{10,9},{11,10},{12,13},{... | collective-permute-start | bytes 983048 | tf_op jit(solution)/shard_map/ppermute | solution.py:506
  78.2 12.5 %collective-permute-start.14 = (bf16[256,640]{1,0:T(8,128)(2,1)S(1)}, bf16[256,640]{1,0:T(8,128)(2,1)S(1)}, u32[]{:S(2)}, u32[]{:S(2)}) collective-permute-start(bf16[256,640]{1,0:T(8,128)(2,1)S(1)} %get-tuple-element.71), channel_id=1, source_target_pairs={{1,0},{2,1},{3,2},{4,5},{5,6},{6,7},{9,8},{10,9},{11,10},{12,13},{... | collective-permute-start | bytes 983048 | tf_op jit(solution)/shard_map/ppermute | solution.py:506
  82.6 12.0 %collective-permute-start.17 = (bf16[256,640]{1,0:T(8,128)(2,1)S(1)}, bf16[256,640]{1,0:T(8,128)(2,1)S(1)}, u32[]{:S(2)}, u32[]{:S(2)}) collective-permute-start(bf16[256,640]{1,0:T(8,128)(2,1)S(1)} %get-tuple-element.72), channel_id=1, source_target_pairs={{0,1},{1,2},{2,3},{5,4},{6,5},{7,6},{8,9},{9,10},{10,11},{13,12},{... | collective-permute-start | bytes 983048 | tf_op jit(solution)/shard_map/ppermute | solution.py:506
  84.9 12.8 %collective-permute-start.18 = (bf16[256,640]{1,0:T(8,128)(2,1)S(1)}, bf16[256,640]{1,0:T(8,128)(2,1)S(1)}, u32[]{:S(2)}, u32[]{:S(2)}) collective-permute-start(bf16[256,640]{1,0:T(8,128)(2,1)S(1)} %get-tuple-element.73), channel_id=1, source_target_pairs={{1,0},{2,1},{3,2},{4,5},{5,6},{6,7},{9,8},{10,9},{11,10},{12,13},{... | collective-permute-start | bytes 983048 | tf_op jit(solution)/shard_map/ppermute | solution.py:506
  93.3 12.5 %collective-permute-start.21 = (bf16[256,640]{1,0:T(8,128)(2,1)S(1)}, bf16[256,640]{1,0:T(8,128)(2,1)S(1)}, u32[]{:S(2)}, u32[]{:S(2)}) collective-permute-start(bf16[256,640]{1,0:T(8,128)(2,1)S(1)} %get-tuple-element.76), channel_id=1, source_target_pairs={{1,0},{2,1},{3,2},{4,5},{5,6},{6,7},{9,8},{10,9},{11,10},{12,13},{... | collective-permute-start | bytes 983048 | tf_op jit(solution)/shard_map/ppermute | solution.py:506
  99.8 12.5 %collective-permute-start.22 = (bf16[256,640]{1,0:T(8,128)(2,1)S(1)}, bf16[256,640]{1,0:T(8,128)(2,1)S(1)}, u32[]{:S(2)}, u32[]{:S(2)}) collective-permute-start(bf16[256,640]{1,0:T(8,128)(2,1)S(1)} %get-tuple-element.77), channel_id=1, source_target_pairs={{1,0},{2,1},{3,2},{4,5},{5,6},{6,7},{9,8},{10,9},{11,10},{12,13},{... | collective-permute-start | bytes 983048 | tf_op jit(solution)/shard_map/ppermute | solution.py:506
  106.5 15.7 %collective-permute-start.24 = (bf16[256,640]{1,0:T(8,128)(2,1)S(1)}, bf16[256,640]{1,0:T(8,128)(2,1)S(1)}, u32[]{:S(2)}, u32[]{:S(2)}) collective-permute-start(bf16[256,640]{1,0:T(8,128)(2,1)S(1)} %get-tuple-element.84), channel_id=1, source_target_pairs={{0,1},{1,2},{2,3},{5,4},{6,5},{7,6},{8,9},{9,10},{10,11},{13,12},{... | collective-permute-start | bytes 983048 | tf_op jit(solution)/shard_map/ppermute | solution.py:506
  108.0 14.2 %collective-permute-start.26 = (bf16[256,640]{1,0:T(8,128)(2,1)S(1)}, bf16[256,640]{1,0:T(8,128)(2,1)S(1)}, u32[]{:S(2)}, u32[]{:S(2)}) collective-permute-start(bf16[256,640]{1,0:T(8,128)(2,1)S(1)} %get-tuple-element.86), channel_id=1, source_target_pairs={{1,0},{2,1},{3,2},{4,5},{5,6},{6,7},{9,8},{10,9},{11,10},{12,13},{... | collective-permute-start | bytes 983048 | tf_op jit(solution)/shard_map/ppermute | solution.py:506
  128.7 21.2 %collective-permute-start.28 = (bf16[2,320,1280]{2,1,0:T(8,128)(2,1)S(1)}, bf16[2,320,1280]{2,1,0:T(8,128)(2,1)S(1)}, u32[]{:S(2)}, u32[]{:S(2)}) collective-permute-start(bf16[2,320,1280]{2,1,0:T(8,128)(2,1)S(1)} %add_convert_fusion), channel_id=1, source_target_pairs={{0,8},{4,20},{8,0},{12,28},{16,24},{20,4},{24,16},{28,12},{1,9},{5... | collective-permute-start | bytes 4915208 | tf_op jit(solution)/shard_map/ppermute | solution.py:496
  130.3 32.2 %collective-permute-start.29 = (bf16[3,128,640]{2,1,0:T(8,128)(2,1)S(1)}, bf16[3,128,640]{2,1,0:T(8,128)(2,1)S(1)}, u32[]{:S(2)}, u32[]{:S(2)}) collective-permute-start(bf16[3,128,640]{2,1,0:T(8,128)(2,1)S(1)} %get-tuple-element.89), channel_id=1, source_target_pairs={{0,3},{1,0},{2,1},{3,2},{4,7},{5,4},{6,5},{7,6},{8,11},{9,8},{10,9... | collective-permute-start | bytes 1474568 | tf_op jit(solution)/shard_map/ppermute | solution.py:486
  132.7 43.0 %collective-permute-start.30 = (bf16[3,128,640]{2,1,0:T(8,128)(2,1)S(1)}, bf16[3,128,640]{2,1,0:T(8,128)(2,1)S(1)}, u32[]{:S(2)}, u32[]{:S(2)}) collective-permute-start(bf16[3,128,640]{2,1,0:T(8,128)(2,1)S(1)} %get-tuple-element.90), channel_id=1, source_target_pairs={{0,2},{1,3},{2,0},{3,1},{4,6},{5,7},{6,4},{7,5},{8,10},{9,11},{10,... | collective-permute-start | bytes 1474568 | tf_op jit(solution)/shard_map/ppermute | solution.py:486
  134.1 41.6 %collective-permute-start.31 = (bf16[3,128,640]{2,1,0:T(8,128)(2,1)S(1)}, bf16[3,128,640]{2,1,0:T(8,128)(2,1)S(1)}, u32[]{:S(2)}, u32[]{:S(2)}) collective-permute-start(bf16[3,128,640]{2,1,0:T(8,128)(2,1)S(1)} %get-tuple-element.91), channel_id=1, source_target_pairs={{0,1},{1,2},{2,3},{3,0},{4,5},{5,6},{6,7},{7,4},{8,9},{9,10},{10,1... | collective-permute-start | bytes 1474568 | tf_op jit(solution)/shard_map/ppermute | solution.py:486
  150.7 27.0 %collective-permute-start.32 = (bf16[160,1280]{1,0:T(8,128)(2,1)S(1)}, bf16[160,1280]{1,0:T(8,128)(2,1)S(1)}, u32[]{:S(2)}, u32[]{:S(2)}) collective-permute-start(bf16[160,1280]{1,0:T(8,128)(2,1)S(1)} %get-tuple-element.105), channel_id=1, source_target_pairs={{0,16},{4,12},{8,24},{12,4},{16,0},{20,28},{24,8},{28,20},{1,17},{... | collective-permute-start | bytes 1228808 | tf_op jit(solution)/shard_map/ppermute | solution.py:496
  151.2 26.4 %collective-permute-start.33 = (bf16[160,1280]{1,0:T(8,128)(2,1)S(1)}, bf16[160,1280]{1,0:T(8,128)(2,1)S(1)}, u32[]{:S(2)}, u32[]{:S(2)}) collective-permute-start(bf16[160,1280]{1,0:T(8,128)(2,1)S(1)} %get-tuple-element.106), channel_id=1, source_target_pairs={{0,16},{4,12},{8,24},{12,4},{16,0},{20,28},{24,8},{28,20},{1,17},{... | collective-permute-start | bytes 1228808 | tf_op jit(solution)/shard_map/ppermute | solution.py:496
  (17 other events, 102.9 us)
